TPU v7x, 256 devices: a whole 4x4x8 slice. The times are simulated.
256 devices in a mesh: table: 128 (over y, z, x), row: 2 (over core).
Axes of the slice: x: 4, y: 4, z: 8, core: 2. Of those that a mesh axis runs over, the one named last changes fastest.
Arguments:
- dense_input: bfloat16 [4096, 13], P(('table', 'row')), may hold values from -6 to 6
- bottom_first: bfloat16 [13, 512], replicated, may hold values from -1.75 to 1.75
- bottom_second: bfloat16 [512, 256], replicated, may hold values from -0.375 to 0.375
- bottom_third: bfloat16 [256, 128], replicated, may hold values from -0.5 to 0.5
- wide_tables: bfloat16 [1048576, 256], P(('table', 'row')), may hold values from -6 to 6
- narrow_tables: bfloat16 [1048576, 64], P(('table', 'row')), may hold values from -6 to 6
- wide_indices: int32 [4096, 32, 8], P(('table', 'row')), may hold values from 0 to 32767
- wide_lengths: int32 [4096, 32], P(('table', 'row')), may hold values from 4 to 8
- narrow_indices: int32 [4096, 32, 8], P(('table', 'row')), may hold values from 0 to 32767
- narrow_lengths: int32 [4096, 32], P(('table', 'row')), may hold values from 4 to 8
- wide_projection: bfloat16 [32, 256, 128], replicated, may hold values from -0.125 to 0.125
- narrow_projection: bfloat16 [32, 64, 128], replicated, may hold values from -0.25 to 0.25
- top_first: bfloat16 [2208, 1024], replicated, may hold values from -0.0234375 to 0.0234375
- top_last: bfloat16 [1024], replicated, may hold values from -0.1875 to 0.1875
Outputs:
- hidden: bfloat16 [4096, 1024], P(('table', 'row'))
- logits: float32 [4096], P(('table', 'row'))
All inputs are finite; a program needn't handle non-finite values.
Results may differ from a plain program's by a relative error of at most 0.02.
Values may be sent and summed in bfloat16 or wider, within the bound.
No kernel may reach another device: no remote copies, remote signals or barrier semaphores. Data moves between devices by JAX's collectives and lax.ppermute only.
A program may use at most 64 MiB of HBM per device.

v0:
```python
import math

import jax
import jax.numpy as jnp
from jax import lax
from jax.sharding import PartitionSpec as P

SPAN = 4


def in_blocks(shard, dim, length):
    shape = shard.shape
    tiles = shard.reshape(*shape[:dim], length, shape[dim] // length, *shape[dim + 1 :])
    return jnp.moveaxis(tiles, dim, 0)


def sent_and_summed(shard, axis, dim):
    length = lax.axis_size(axis)
    tiles = lax.all_to_all(in_blocks(shard, dim, length), axis, 0, 0, tiled=True)
    return jnp.sum(tiles.astype(jnp.float32), axis=0)


def swapped(block, axis, apart):
    count = lax.axis_size(axis)
    route = []
    for low in range(count):
        high = low | 1 << apart
        if high != low and high < count:
            route += [(low, high), (high, low)]
    return lax.ppermute(block, axis, route)


def in_one_piece(arrays, axis, split_dim, concat_dim, along):
    columns = [a.reshape(*a.shape[:along], -1) for a in arrays]
    both = jnp.concatenate(columns, axis=along)
    filled, at, done = (
        lax.all_to_all(both, axis, split_axis=split_dim, concat_axis=concat_dim, tiled=True),
        0,
        [],
    )
    for a, column in zip(arrays, columns):
        slab = filled[..., at : at + column.shape[along]]
        done.append(slab.reshape(*slab.shape[:along], *a.shape[along:]))
        at += column.shape[along]
    return tuple(done)


def sent_together(arrays, axis, dim, along):
    widths = [math.prod(a.shape[along:]) for a in arrays]
    both = jnp.concatenate(
        [a.reshape(*a.shape[:along], w) for a, w in zip(arrays, widths)], axis=along
    )
    filled = lax.all_gather(both, axis, axis=dim, tiled=True)
    tiles = jnp.split(filled, [sum(widths[:k]) for k in range(1, len(widths))], axis=along)
    return tuple(
        (b.reshape(*filled.shape[:along], *a.shape[along:]) for a, b in zip(arrays, tiles))
    )


def side_by_side(arrays, axis, split_dim, concat_dim, along):
    widths = [a.shape[along] for a in arrays]
    both = jnp.concatenate(arrays, axis=along)
    filled = lax.all_to_all(both, axis, split_axis=split_dim, concat_axis=concat_dim, tiled=True)
    return tuple(jnp.split(filled, [sum(widths[:k]) for k in range(1, len(widths))], axis=along))


def dense_layer(values, weight):
    return jnp.maximum(jnp.dot(values, weight, preferred_element_type=jnp.float32), 0.0).astype(
        jnp.bfloat16
    )


def pool_shard(table_rows, bag_ids, bag_sizes, first_row):
    row_total = table_rows.shape[0]
    leading = bag_ids.shape[:-1]
    slot_count = bag_ids.shape[-1]
    local_ids = (bag_ids - first_row).reshape(-1, slot_count)
    flat_sizes = bag_sizes.reshape(-1)
    bag_total = local_ids.shape[0]
    block_rows = math.gcd(bag_total, 512)
    positions = lax.broadcasted_iota(jnp.int32, (1, row_total), 1)

    def one_block(operands):
        block_ids, block_sizes = operands
        counts = jnp.zeros((block_ids.shape[0], row_total), jnp.float32)
        for slot_pos in range(slot_count):
            matched = (block_ids[:, slot_pos : slot_pos + 1] == positions) & (
                block_sizes[:, None] > slot_pos
            )
            counts = counts + matched.astype(jnp.float32)
        return jnp.dot(counts.astype(jnp.bfloat16), table_rows, preferred_element_type=jnp.float32)

    pooled = lax.map(
        one_block,
        (local_ids.reshape(-1, block_rows, slot_count), flat_sizes.reshape(-1, block_rows)),
    )
    return pooled.reshape(leading + (table_rows.shape[1],))


def reduce_group(partial_value, group_span):
    shaped = partial_value.reshape(
        partial_value.shape[0],
        partial_value.shape[1],
        group_span,
        partial_value.shape[2] // group_span,
        partial_value.shape[3],
    )
    shaped = sent_and_summed(shaped.astype(jnp.bfloat16), "row", 1)
    member = lax.axis_index("table") % group_span
    width_now = group_span
    for bit_pos in reversed(range(group_span.bit_length() - 1)):
        half_width = width_now // 2
        upper_bit = member // (1 << bit_pos) % 2
        kept_half = lax.dynamic_slice_in_dim(shaped, upper_bit * half_width, half_width, 2)
        sent_half = lax.dynamic_slice_in_dim(shaped, (1 - upper_bit) * half_width, half_width, 2)
        shaped = kept_half + swapped(sent_half, "table", bit_pos)
        width_now = half_width
    return shaped[:, 0, 0]


def body(
    dense_input,
    bottom_first,
    bottom_second,
    bottom_third,
    wide_tables,
    narrow_tables,
    wide_indices,
    wide_lengths,
    narrow_indices,
    narrow_lengths,
    wide_projection,
    narrow_projection,
    top_first,
    top_last,
):
    table_count = lax.axis_size("table")
    group_span = SPAN
    local_batch = dense_input.shape[0]
    table_pos = lax.axis_index("table")
    own_table = table_pos // group_span
    first_row = (
        table_pos % group_span * lax.axis_size("row") + lax.axis_index("row")
    ) * wide_tables.shape[0]
    wide_ids = jnp.repeat(wide_indices, group_span, axis=1)
    wide_sizes = jnp.repeat(wide_lengths, group_span, axis=1)
    narrow_ids = jnp.repeat(narrow_indices, group_span, axis=1)
    narrow_sizes = jnp.repeat(narrow_lengths, group_span, axis=1)
    wide_ids, wide_sizes, narrow_ids, narrow_sizes = in_one_piece(
        (wide_ids, wide_sizes, narrow_ids, narrow_sizes), "table", 1, 0, 2
    )
    slot_count = wide_ids.shape[2]
    wide_ids = wide_ids.reshape(table_count, 1, local_batch, slot_count)
    narrow_ids = narrow_ids.reshape(table_count, 1, local_batch, slot_count)
    wide_sizes = wide_sizes.reshape(table_count, 1, local_batch)
    narrow_sizes = narrow_sizes.reshape(table_count, 1, local_batch)
    wide_ids, wide_sizes, narrow_ids, narrow_sizes = sent_together(
        (wide_ids, wide_sizes, narrow_ids, narrow_sizes), "row", 1, 3
    )
    wide_part = pool_shard(wide_tables, wide_ids, wide_sizes, first_row)
    narrow_part = pool_shard(narrow_tables, narrow_ids, narrow_sizes, first_row)
    wide_weight = lax.dynamic_index_in_dim(wide_projection, own_table, 0, keepdims=False).astype(
        jnp.float32
    )
    wide_part = jnp.dot(wide_part, wide_weight)
    reduced = reduce_group(jnp.concatenate([wide_part, narrow_part], 3), group_span)
    wide_sum = reduced[..., : wide_part.shape[3]]
    wide_embedded = wide_sum.astype(jnp.bfloat16)
    narrow_pooled = reduced[..., wide_part.shape[3] :].astype(jnp.bfloat16)
    own_narrow = lax.dynamic_index_in_dim(narrow_projection, own_table, 0, keepdims=False)
    narrow_payload = jnp.dot(narrow_pooled, own_narrow, preferred_element_type=jnp.float32).astype(
        jnp.bfloat16
    )
    wide_home, narrow_home = side_by_side((wide_embedded, narrow_payload), "table", 0, 0, 1)
    wide_home = wide_home.reshape(-1, local_batch, wide_home.shape[2])
    narrow_home = narrow_home.reshape(-1, local_batch, narrow_home.shape[2])
    bottom = dense_layer(
        dense_layer(dense_layer(dense_input, bottom_first), bottom_second), bottom_third
    )
    features = jnp.concatenate([bottom[None], wide_home, narrow_home], 0)
    products = jnp.einsum("fbe,gbe->bfg", features, features, preferred_element_type=jnp.float32)
    feature_total = features.shape[0]
    pair_values = jnp.concatenate(
        [products[:, outer_pos, outer_pos + 1 :] for outer_pos in range(feature_total - 1)], 1
    )
    joined = jnp.concatenate([bottom.astype(jnp.float32), pair_values], 1).astype(jnp.bfloat16)
    hidden = dense_layer(joined, top_first)
    logits = jnp.dot(hidden, top_last, preferred_element_type=jnp.float32)
    return (hidden, logits)


def solution(mesh):
    in_specs = (
        P(("table", "row"), None),
        P(),
        P(),
        P(),
        P(("table", "row"), None),
        P(("table", "row"), None),
        P(("table", "row"), None, None),
        P(("table", "row"), None),
        P(("table", "row"), None, None),
        P(("table", "row"), None),
        P(),
        P(),
        P(),
        P(),
    )
    out_specs = (P(("table", "row"), None), P(("table", "row")))
    return jax.shard_map(body, mesh=mesh, in_specs=in_specs, out_specs=out_specs, check_vma=False)
```

profile of v0, /device:TPU:32, one launch (start us, length us, event | category | flops | bytes accessed | tf_op | source)
XLA Modules:
  0.0 382.4 jit_solution(8611014978474049584)
XLA Ops:
  0.6 1.1 copy.162
  1.7 0.9 copy.164
  4.4 1.4 pad_add_fusion
  5.8 2.2 copy.168
  8.0 1.5 reshape.259
  9.5 15.0 %all-to-all-start = ((s32[128,1,288]{2,1,0:T(1,128)}), s32[128,1,288]{2,1,0:T(1,128)S(1)}, u32[]{:S(2)}, u32[]{:S(2)}) async-start(s32[128,1,288]{2,1,0:T(1,128)} %reshape.259), calls=%async_computation | async-start | bytes 393216 | tf_op jit(solution)/shard_map/all_to_all | solution.py:37
  24.6 12.8 %all-to-all-done = s32[128,1,288]{2,1,0:T(1,128)S(1)} async-done(((s32[128,1,288]{2,1,0:T(1,128)}), s32[128,1,288]{2,1,0:T(1,128)S(1)}, u32[]{:S(2)}, u32[]{:S(2)}) %all-to-all-start) | async-done | bytes 147488 | tf_op jit(solution)/shard_map/all_to_all | solution.py:37
  37.9 1.1 reduce.41
  39.7 1.7 fusion.75
  41.4 1.2 slice_reduce_fusion.1
  42.6 1.6 copy.170
  44.2 1.6 copy.172
  46.1 2.0 all_gather.3
  48.7 1.5 reshape_reshape.14
  50.6 125.5 %while.24 = (s32[]{:T(128)}, bf16[8,512,256]{2,1,0:T(8,128)(2,1)}, s32[8,512,8]{1,0,2:T(8,128)S(1)}, s32[8,512]{1,0:T(8,128)S(1)}, bf16[4096,256]{1,0:T(8,128)(2,1)}, /*index=5*/s32[]{:T(128)}) while((s32[]{:T(128)}, bf16[8,512,256]{2,1,0:T(8,128)(2,1)}, s32[8,512,8]{1,0,2:T(8,128)S(1)}, s32[8,512]{1,0:T(8,128)S(1)}, ...), condition=%wide.region_1.2_spmd.clone.clone, body=%wide.region_0.1_spmd.clone.clone.sunk | while | flops 1140854784 | bytes 2746957 | solution.py:93
  51.2 15.5 %fusion.97 = bf16[8,512,256]{2,1,0:T(8,128)(2,1)} fusion(bf16[8,512,256]{2,1,0:T(8,128)(2,1)} %get-tuple-element.431, s32[]{:T(128)} %get-tuple-element.430, bf16[4096,256]{1,0:T(8,128)(2,1)} %get-tuple-element.440, s32[512]{0:T(512)S(1)} %bitcast.287, s32[512]{0:T(512)S(1)} %bitcast.288, s32[512]{0:T(512)S(1)} %bitcast.289, s32[512]{0:T(512)S(1)} %bitcast.290, ...), kind=kOutput, calls=%fused_computation.29.clone.1 | convolution fusion | flops 1140850688 | bytes 2642432 | tf_op jit(solution)/shard_map/while/body/eval_jaxpr/dot_general | solution.py:91
  66.8 15.5 %fusion.97 = bf16[8,512,256]{2,1,0:T(8,128)(2,1)} fusion(bf16[8,512,256]{2,1,0:T(8,128)(2,1)} %get-tuple-element.431, s32[]{:T(128)} %get-tuple-element.430, bf16[4096,256]{1,0:T(8,128)(2,1)} %get-tuple-element.440, s32[512]{0:T(512)S(1)} %bitcast.287, s32[512]{0:T(512)S(1)} %bitcast.288, s32[512]{0:T(512)S(1)} %bitcast.289, s32[512]{0:T(512)S(1)} %bitcast.290, ...), kind=kOutput, calls=%fused_computation.29.clone.1 | convolution fusion | flops 1140850688 | bytes 2642432 | tf_op jit(solution)/shard_map/while/body/eval_jaxpr/dot_general | solution.py:91
  82.4 15.5 %fusion.97 = bf16[8,512,256]{2,1,0:T(8,128)(2,1)} fusion(bf16[8,512,256]{2,1,0:T(8,128)(2,1)} %get-tuple-element.431, s32[]{:T(128)} %get-tuple-element.430, bf16[4096,256]{1,0:T(8,128)(2,1)} %get-tuple-element.440, s32[512]{0:T(512)S(1)} %bitcast.287, s32[512]{0:T(512)S(1)} %bitcast.288, s32[512]{0:T(512)S(1)} %bitcast.289, s32[512]{0:T(512)S(1)} %bitcast.290, ...), kind=kOutput, calls=%fused_computation.29.clone.1 | convolution fusion | flops 1140850688 | bytes 2642432 | tf_op jit(solution)/shard_map/while/body/eval_jaxpr/dot_general | solution.py:91
  98.1 15.5 %fusion.97 = bf16[8,512,256]{2,1,0:T(8,128)(2,1)} fusion(bf16[8,512,256]{2,1,0:T(8,128)(2,1)} %get-tuple-element.431, s32[]{:T(128)} %get-tuple-element.430, bf16[4096,256]{1,0:T(8,128)(2,1)} %get-tuple-element.440, s32[512]{0:T(512)S(1)} %bitcast.287, s32[512]{0:T(512)S(1)} %bitcast.288, s32[512]{0:T(512)S(1)} %bitcast.289, s32[512]{0:T(512)S(1)} %bitcast.290, ...), kind=kOutput, calls=%fused_computation.29.clone.1 | convolution fusion | flops 1140850688 | bytes 2642432 | tf_op jit(solution)/shard_map/while/body/eval_jaxpr/dot_general | solution.py:91
  113.7 15.5 %fusion.97 = bf16[8,512,256]{2,1,0:T(8,128)(2,1)} fusion(bf16[8,512,256]{2,1,0:T(8,128)(2,1)} %get-tuple-element.431, s32[]{:T(128)} %get-tuple-element.430, bf16[4096,256]{1,0:T(8,128)(2,1)} %get-tuple-element.440, s32[512]{0:T(512)S(1)} %bitcast.287, s32[512]{0:T(512)S(1)} %bitcast.288, s32[512]{0:T(512)S(1)} %bitcast.289, s32[512]{0:T(512)S(1)} %bitcast.290, ...), kind=kOutput, calls=%fused_computation.29.clone.1 | convolution fusion | flops 1140850688 | bytes 2642432 | tf_op jit(solution)/shard_map/while/body/eval_jaxpr/dot_general | solution.py:91
  129.3 15.5 %fusion.97 = bf16[8,512,256]{2,1,0:T(8,128)(2,1)} fusion(bf16[8,512,256]{2,1,0:T(8,128)(2,1)} %get-tuple-element.431, s32[]{:T(128)} %get-tuple-element.430, bf16[4096,256]{1,0:T(8,128)(2,1)} %get-tuple-element.440, s32[512]{0:T(512)S(1)} %bitcast.287, s32[512]{0:T(512)S(1)} %bitcast.288, s32[512]{0:T(512)S(1)} %bitcast.289, s32[512]{0:T(512)S(1)} %bitcast.290, ...), kind=kOutput, calls=%fused_computation.29.clone.1 | convolution fusion | flops 1140850688 | bytes 2642432 | tf_op jit(solution)/shard_map/while/body/eval_jaxpr/dot_general | solution.py:91
  145.0 15.5 %fusion.97 = bf16[8,512,256]{2,1,0:T(8,128)(2,1)} fusion(bf16[8,512,256]{2,1,0:T(8,128)(2,1)} %get-tuple-element.431, s32[]{:T(128)} %get-tuple-element.430, bf16[4096,256]{1,0:T(8,128)(2,1)} %get-tuple-element.440, s32[512]{0:T(512)S(1)} %bitcast.287, s32[512]{0:T(512)S(1)} %bitcast.288, s32[512]{0:T(512)S(1)} %bitcast.289, s32[512]{0:T(512)S(1)} %bitcast.290, ...), kind=kOutput, calls=%fused_computation.29.clone.1 | convolution fusion | flops 1140850688 | bytes 2642432 | tf_op jit(solution)/shard_map/while/body/eval_jaxpr/dot_general | solution.py:91
  160.6 15.5 %fusion.97 = bf16[8,512,256]{2,1,0:T(8,128)(2,1)} fusion(bf16[8,512,256]{2,1,0:T(8,128)(2,1)} %get-tuple-element.431, s32[]{:T(128)} %get-tuple-element.430, bf16[4096,256]{1,0:T(8,128)(2,1)} %get-tuple-element.440, s32[512]{0:T(512)S(1)} %bitcast.287, s32[512]{0:T(512)S(1)} %bitcast.288, s32[512]{0:T(512)S(1)} %bitcast.289, s32[512]{0:T(512)S(1)} %bitcast.290, ...), kind=kOutput, calls=%fused_computation.29.clone.1 | convolution fusion | flops 1140850688 | bytes 2642432 | tf_op jit(solution)/shard_map/while/body/eval_jaxpr/dot_general | solution.py:91
  176.1 4.0 %reshape.222 = bf16[128,2,4,4,256]{4,3,2,1,0:T(4,128)(2,1)} reshape(bf16[8,512,256]{2,1,0:T(8,128)(2,1)} %get-tuple-element.108) | data formatting | bytes 4194304 | tf_op jit(solution)/shard_map/reshape.143
  180.6 1.5 reshape_reshape.15
  182.5 121.0 %while.25 = (s32[]{:T(128)}, bf16[8,512,64]{1,2,0:T(8,128)(2,1)}, s32[8,512,8]{1,0,2:T(8,128)S(1)}, s32[8,512]{1,0:T(8,128)S(1)}, bf16[4096,64]{0,1:T(8,128)(2,1)}, /*index=5*/s32[]{:T(128)}) while((s32[]{:T(128)}, bf16[8,512,64]{1,2,0:T(8,128)(2,1)}, s32[8,512,8]{1,0,2:T(8,128)S(1)}, s32[8,512]{1,0:T(8,128)S(1)}, ...), condition=%wide.region_3.4_spmd.clone.clone, body=%wide.region_2.3_spmd.clone.clone.sunk | while | flops 335548416 | bytes 780877 | solution.py:93
  182.8 15.0 %fusion.100 = bf16[8,512,64]{1,2,0:T(8,128)(2,1)} fusion(bf16[8,512,64]{1,2,0:T(8,128)(2,1)} %get-tuple-element.413, s32[]{:T(128)} %get-tuple-element.412, bf16[4096,64]{0,1:T(8,128)(2,1)} %get-tuple-element.422, s32[512]{0:T(512)S(1)} %bitcast.295, s32[512]{0:T(512)S(1)} %bitcast.296, s32[512]{0:T(512)S(1)} %bitcast.297, s32[512]{0:T(512)S(1)} %bitcast.298, ...), kind=kOutput, calls=%fused_computation.68.clone.1 | convolution fusion | flops 335544320 | bytes 676352 | tf_op jit(solution)/shard_map/while/body/eval_jaxpr/dot_general | solution.py:91
  197.8 14.9 %fusion.100 = bf16[8,512,64]{1,2,0:T(8,128)(2,1)} fusion(bf16[8,512,64]{1,2,0:T(8,128)(2,1)} %get-tuple-element.413, s32[]{:T(128)} %get-tuple-element.412, bf16[4096,64]{0,1:T(8,128)(2,1)} %get-tuple-element.422, s32[512]{0:T(512)S(1)} %bitcast.295, s32[512]{0:T(512)S(1)} %bitcast.296, s32[512]{0:T(512)S(1)} %bitcast.297, s32[512]{0:T(512)S(1)} %bitcast.298, ...), kind=kOutput, calls=%fused_computation.68.clone.1 | convolution fusion | flops 335544320 | bytes 676352 | tf_op jit(solution)/shard_map/while/body/eval_jaxpr/dot_general | solution.py:91
  212.9 15.0 %fusion.100 = bf16[8,512,64]{1,2,0:T(8,128)(2,1)} fusion(bf16[8,512,64]{1,2,0:T(8,128)(2,1)} %get-tuple-element.413, s32[]{:T(128)} %get-tuple-element.412, bf16[4096,64]{0,1:T(8,128)(2,1)} %get-tuple-element.422, s32[512]{0:T(512)S(1)} %bitcast.295, s32[512]{0:T(512)S(1)} %bitcast.296, s32[512]{0:T(512)S(1)} %bitcast.297, s32[512]{0:T(512)S(1)} %bitcast.298, ...), kind=kOutput, calls=%fused_computation.68.clone.1 | convolution fusion | flops 335544320 | bytes 676352 | tf_op jit(solution)/shard_map/while/body/eval_jaxpr/dot_general | solution.py:91
  228.0 15.0 %fusion.100 = bf16[8,512,64]{1,2,0:T(8,128)(2,1)} fusion(bf16[8,512,64]{1,2,0:T(8,128)(2,1)} %get-tuple-element.413, s32[]{:T(128)} %get-tuple-element.412, bf16[4096,64]{0,1:T(8,128)(2,1)} %get-tuple-element.422, s32[512]{0:T(512)S(1)} %bitcast.295, s32[512]{0:T(512)S(1)} %bitcast.296, s32[512]{0:T(512)S(1)} %bitcast.297, s32[512]{0:T(512)S(1)} %bitcast.298, ...), kind=kOutput, calls=%fused_computation.68.clone.1 | convolution fusion | flops 335544320 | bytes 676352 | tf_op jit(solution)/shard_map/while/body/eval_jaxpr/dot_general | solution.py:91
  243.1 15.0 %fusion.100 = bf16[8,512,64]{1,2,0:T(8,128)(2,1)} fusion(bf16[8,512,64]{1,2,0:T(8,128)(2,1)} %get-tuple-element.413, s32[]{:T(128)} %get-tuple-element.412, bf16[4096,64]{0,1:T(8,128)(2,1)} %get-tuple-element.422, s32[512]{0:T(512)S(1)} %bitcast.295, s32[512]{0:T(512)S(1)} %bitcast.296, s32[512]{0:T(512)S(1)} %bitcast.297, s32[512]{0:T(512)S(1)} %bitcast.298, ...), kind=kOutput, calls=%fused_computation.68.clone.1 | convolution fusion | flops 335544320 | bytes 676352 | tf_op jit(solution)/shard_map/while/body/eval_jaxpr/dot_general | solution.py:91
  258.1 15.0 %fusion.100 = bf16[8,512,64]{1,2,0:T(8,128)(2,1)} fusion(bf16[8,512,64]{1,2,0:T(8,128)(2,1)} %get-tuple-element.413, s32[]{:T(128)} %get-tuple-element.412, bf16[4096,64]{0,1:T(8,128)(2,1)} %get-tuple-element.422, s32[512]{0:T(512)S(1)} %bitcast.295, s32[512]{0:T(512)S(1)} %bitcast.296, s32[512]{0:T(512)S(1)} %bitcast.297, s32[512]{0:T(512)S(1)} %bitcast.298, ...), kind=kOutput, calls=%fused_computation.68.clone.1 | convolution fusion | flops 335544320 | bytes 676352 | tf_op jit(solution)/shard_map/while/body/eval_jaxpr/dot_general | solution.py:91
  273.2 15.0 %fusion.100 = bf16[8,512,64]{1,2,0:T(8,128)(2,1)} fusion(bf16[8,512,64]{1,2,0:T(8,128)(2,1)} %get-tuple-element.413, s32[]{:T(128)} %get-tuple-element.412, bf16[4096,64]{0,1:T(8,128)(2,1)} %get-tuple-element.422, s32[512]{0:T(512)S(1)} %bitcast.295, s32[512]{0:T(512)S(1)} %bitcast.296, s32[512]{0:T(512)S(1)} %bitcast.297, s32[512]{0:T(512)S(1)} %bitcast.298, ...), kind=kOutput, calls=%fused_computation.68.clone.1 | convolution fusion | flops 335544320 | bytes 676352 | tf_op jit(solution)/shard_map/while/body/eval_jaxpr/dot_general | solution.py:91
  288.3 15.0 %fusion.100 = bf16[8,512,64]{1,2,0:T(8,128)(2,1)} fusion(bf16[8,512,64]{1,2,0:T(8,128)(2,1)} %get-tuple-element.413, s32[]{:T(128)} %get-tuple-element.412, bf16[4096,64]{0,1:T(8,128)(2,1)} %get-tuple-element.422, s32[512]{0:T(512)S(1)} %bitcast.295, s32[512]{0:T(512)S(1)} %bitcast.296, s32[512]{0:T(512)S(1)} %bitcast.297, s32[512]{0:T(512)S(1)} %bitcast.298, ...), kind=kOutput, calls=%fused_computation.68.clone.1 | convolution fusion | flops 335544320 | bytes 676352 | tf_op jit(solution)/shard_map/while/body/eval_jaxpr/dot_general | solution.py:91
  303.4 1.5 copy.182
  305.0 1.6 copy.183
  306.6 4.2 %fusion.47 = bf16[128,2,1,4,4,128]{0,5,4,3,1,2:T(8,128)(2,1)S(1)} fusion(bf16[128,2,4,4,256]{4,3,2,1,0:T(4,128)(2,1)} %reshape.222, bf16[32,256,128]{2,1,0:T(8,128)(2,1)S(1)} %copy-done, s32[]{:T(128)S(6)} %select_n.45), kind=kOutput, calls=%fused_computation.86 | convolution fusion | flops 268435456 | bytes 3211268 | tf_op jit(solution)/shard_map/dot_general | solution.py:165
  311.0 5.0 %all_to_all.28 = bf16[2,128,1,4,4,192]{1,5,4,3,2,0:T(8,128)(2,1)S(1)} all-to-all(bf16[2,128,1,4,4,192]{1,5,4,3,2,0:T(8,128)(2,1)S(1)} %maximum_bitcast_fusion), channel_id=1, replica_groups=mesh['table'=128,'row'=2] {'row'}, dimensions={0} | all-to-all | bytes 3145728 | tf_op jit(solution)/shard_map/all_to_all | solution.py:19
  316.3 1.1 copy-done.1
  317.5 1.5 collective-permute-start
  319.0 19.8 %collective-permute-done = f32[128,1,2,4,192]{0,4,3,2,1:T(8,128)} collective-permute-done((f32[128,1,2,4,192]{0,4,3,2,1:T(8,128)S(1)}, f32[128,1,2,4,192]{0,4,3,2,1:T(8,128)}, u32[]{:S(2)}, u32[]{:S(2)}) %collective-permute-start) | collective-permute-done | bytes 786464 | tf_op jit(solution)/shard_map/ppermute | solution.py:30
  338.8 1.5 bitcast_add_fusion
  341.7 9.9 %collective-permute-done.1 = f32[128,1,1,4,192]{0,4,3,2,1:T(8,128)S(1)} collective-permute-done((f32[128,1,1,4,192]{0,4,3,2,1:T(8,128)}, f32[128,1,1,4,192]{0,4,3,2,1:T(8,128)S(1)}, u32[]{:S(2)}, u32[]{:S(2)}) %collective-permute-start.1) | collective-permute-done | bytes 393248 | tf_op jit(solution)/shard_map/ppermute | solution.py:30
  351.7 0.9 convolution_convert_fusion
  353.5 6.5 %all-to-all-start.2 = ((bf16[128,8,128]{2,1,0:T(8,128)(2,1)}), bf16[128,8,128]{2,1,0:T(8,128)(2,1)S(1)}, u32[]{:S(2)}, u32[]{:S(2)}) async-start(bf16[128,8,128]{2,1,0:T(8,128)(2,1)} %copy.186), calls=%async_computation.2 | async-start | bytes 524288 | tf_op jit(solution)/shard_map/all_to_all | solution.py:63
  360.0 0.9 fusion.54
  361.1 11.9 %all-to-all-done.2 = bf16[128,8,128]{2,1,0:T(8,128)(2,1)S(1)} async-done(((bf16[128,8,128]{2,1,0:T(8,128)(2,1)}), bf16[128,8,128]{2,1,0:T(8,128)(2,1)S(1)}, u32[]{:S(2)}, u32[]{:S(2)}) %all-to-all-start.2) | async-done | bytes 262176 | tf_op jit(solution)/shard_map/all_to_all | solution.py:63
  378.6 3.0 fusion.50
  (185 shorter events, 15.6 us)
Async XLA Ops:
  0.6 306.0 %copy-start = (bf16[32,256,128]{2,1,0:T(8,128)(2,1)S(1)}, bf16[32,256,128]{2,1,0:T(8,128)(2,1)}, u32[]{:S(2)}) copy-start(bf16[32,256,128]{2,1,0:T(8,128)(2,1)} %param.28) | copy-start | bytes 6291460
  9.5 28.0 %all-to-all-start = ((s32[128,1,288]{2,1,0:T(1,128)}), s32[128,1,288]{2,1,0:T(1,128)S(1)}, u32[]{:S(2)}, u32[]{:S(2)}) async-start(s32[128,1,288]{2,1,0:T(1,128)} %reshape.259), calls=%async_computation | async-start | bytes 393216 | tf_op jit(solution)/shard_map/all_to_all | solution.py:37
  306.6 4.2 %copy-start.2 = (bf16[128,2,1,4,4,64]{0,5,4,3,1,2:T(8,128)(2,1)S(1)}, bf16[128,2,1,4,4,64]{0,5,4,3,1,2:T(8,128)(2,1)}, u32[]{:S(2)}) copy-start(bf16[128,2,1,4,4,64]{0,5,4,3,1,2:T(8,128)(2,1)} %copy.183) | copy-start | bytes 1572868
  316.3 1.2 copy-start.1
  317.5 21.3 %collective-permute-start = (f32[128,1,2,4,192]{0,4,3,2,1:T(8,128)S(1)}, f32[128,1,2,4,192]{0,4,3,2,1:T(8,128)}, u32[]{:S(2)}, u32[]{:S(2)}) collective-permute-start(f32[128,1,2,4,192]{0,4,3,2,1:T(8,128)S(1)} %dynamic-slice_bitcast_fusion), channel_id=1, source_target_pairs={{0,4},{4,0},{2,6},{6,2},{8,12},{12,8},{10,14},{14,10},{16,20},{20,... | collective-permute-start | bytes 2359304 | tf_op jit(solution)/shard_map/ppermute | solution.py:30
  340.3 19.8 %copy-start.3 = (bf16[512,256]{1,0:T(8,128)(2,1)S(1)}, bf16[512,256]{1,0:T(8,128)(2,1)}, u32[]{:S(2)}) copy-start(bf16[512,256]{1,0:T(8,128)(2,1)} %param.20) | copy-start | bytes 786436
  340.3 19.8 %copy-start.6 = (bf16[13,512]{1,0:T(8,128)(2,1)S(1)}, bf16[13,512]{1,0:T(8,128)(2,1)}, u32[]{:S(2)}) copy-start(bf16[13,512]{1,0:T(8,128)(2,1)} %param.19) | copy-start | bytes 39940
  341.1 10.5 %collective-permute-start.1 = (f32[128,1,1,4,192]{0,4,3,2,1:T(8,128)}, f32[128,1,1,4,192]{0,4,3,2,1:T(8,128)S(1)}, u32[]{:S(2)}, u32[]{:S(2)}) collective-permute-start(f32[128,1,1,4,192]{0,4,3,2,1:T(8,128)} %constant_dynamic-slice_fusion.4), channel_id=1, source_target_pairs={{0,2},{2,0},{4,6},{6,4},{8,10},{10,8},{12,14},{14,12},{16,18},{18,... | collective-permute-start | bytes 1179656 | tf_op jit(solution)/shard_map/ppermute | solution.py:30
  351.6 9.3 %copy-start.4 = (bf16[256,128]{1,0:T(8,128)(2,1)S(1)}, bf16[256,128]{1,0:T(8,128)(2,1)}, u32[]{:S(2)}) copy-start(bf16[256,128]{1,0:T(8,128)(2,1)} %param.21) | copy-start | bytes 196612
  351.6 9.5 %copy-start.7 = (bf16[1024]{0:T(1024)(128)(2,1)S(1)}, bf16[1024]{0:T(1024)(128)(2,1)}, u32[]{:S(2)}) copy-start(bf16[1024]{0:T(1024)(128)(2,1)} %param.31) | copy-start | bytes 6148
  353.5 19.5 %all-to-all-start.2 = ((bf16[128,8,128]{2,1,0:T(8,128)(2,1)}), bf16[128,8,128]{2,1,0:T(8,128)(2,1)S(1)}, u32[]{:S(2)}, u32[]{:S(2)}) async-start(bf16[128,8,128]{2,1,0:T(8,128)(2,1)} %copy.186), calls=%async_computation.2 | async-start | bytes 524288 | tf_op jit(solution)/shard_map/all_to_all | solution.py:63
  381.6 0.6 copy-start.5
where the time goes:
time: 390 us; the launch traced here: 382 us
  matrix products  254 us (65%)
  waiting for transfers between devices  54.4 us (14%)
  local copies, waits for them, and re-layouts  35.4 us (9%)
  starting transfers between devices  23.6 us (6%)
  blocking collectives  7.01 us (2%)
  other arithmetic  5.59 us (1%)
    dot_general x16, matrix products, one_block(): jnp.dot(counts.astype(jnp.bfloat16), table_rows, preferred_element_type=j...  244 us
    ppermute x2, waiting for transfers between devices, swapped(): return lax.ppermute(block, axis, route)  29.7 us
    all_to_all x1, starting transfers between devices, in_one_piece(): lax.all_to_all(both, axis, split_axis=split_dim, concat_axis=concat_dim,...  15 us
    all_to_all x1, waiting for transfers between devices, in_one_piece(): lax.all_to_all(both, axis, split_axis=split_dim, concat_axis=concat_dim,...  12.8 us
    all_to_all x1, waiting for transfers between devices, side_by_side(): lax.all_to_all(both, axis, split_axis=split_dim, concat_axis=concat_dim,...  11.9 us
  transfers between devices with their start and end apart: 4, of which 4 were waited for; matrix products, arithmetic and copies ran while one was open for 0% of the time, Pallas kernels for 0%

commit v1 on v0

v1 whole, which is shorter than its diff:
```python
import jax
import jax.numpy as jnp
from jax import lax
from jax.experimental import pallas as pl
from jax.experimental.pallas import tpu as pltpu
from jax.sharding import Mesh
from jax.sharding import PartitionSpec as P

SLOTS = 8
BAGS = 16
LANES = 128


def entries(value, shard, lane):
    local = (value >> 12) == shard
    ones = local.astype(jnp.int32)
    run = ones
    for step in (16, 32, 64):
        run = run + jnp.where(lane >= step, pltpu.roll(run, step, 1), 0)
    rank = run - ones
    gap = (lane >> 4) - rank
    packed = jnp.where(local, (value & 4095) | (gap << 16) | (1 << 24), 0)
    for bit in (0, 1, 2):
        moved = jnp.where((packed & (1 << (16 + bit))) != 0, packed, 0)
        packed = packed - moved + pltpu.roll(moved, LANES - (16 << bit), 1)
    first = jnp.where(packed != 0, packed & 4095, 4096)
    more = (packed != 0) & (lane >= BAGS)
    ones = more.astype(jnp.int32)
    run = ones
    for step in (1, 2, 4, 8, 16, 32, 64):
        run = run + jnp.where(lane >= step, pltpu.roll(run, step, 1), 0)
    gap = lane - (run - ones)
    extra = jnp.where(more, (packed & 4095) | ((lane & 15) << 12) | (gap << 16) | (1 << 24), 0)
    for bit in range(7):
        moved = jnp.where((extra & (1 << (16 + bit))) != 0, extra, 0)
        extra = extra - moved + pltpu.roll(moved, LANES - (1 << bit), 1)
    return first, jnp.where(lane == LANES - 1, run, extra & 65535)


def pool_kernel(place_ref, words_ref, wide_ref, narrow_ref, keep_ref, send_ref,
                wide_rows, narrow_rows, wide_sum, narrow_sum, firsts_v, wmore_v, nmore_v,
                firsts, wmore, nmore, sems):
    copies = [
        pltpu.make_async_copy(wide_ref, wide_rows.at[pl.ds(0, 4096)], sems.at[0]),
        pltpu.make_async_copy(narrow_ref, narrow_rows.at[pl.ds(0, 4096)], sems.at[1]),
    ]
    for copy in copies:
        copy.start()
    my_x = place_ref[0]
    my_row = place_ref[1]
    shard = my_x * 2 + my_row
    wide_rows[pl.ds(4096, 8), :] = jnp.zeros((8, LANES), jnp.float32)
    narrow_rows[pl.ds(4096, 8), :] = jnp.zeros((8, LANES), jnp.float32)
    lane = lax.broadcasted_iota(jnp.int32, (32, LANES), 1)

    def prepare(j, total):
        rows = pl.ds(pl.multiple_of(j * 32, 32), 32)
        words = words_ref[rows, :]
        wfirst, wlist = entries(words & 65535, shard, lane)
        nfirst, nlist = entries((words >> 16) & 65535, shard, lane)
        wmore_v[rows, :] = wlist
        nmore_v[rows, :] = nlist
        pair = jnp.where(lane < BAGS, wfirst | (nfirst << 16), 0)
        return total + pltpu.roll(pair, j * BAGS, 1)

    firsts_v[...] = lax.fori_loop(0, 8, prepare, jnp.zeros((32, LANES), jnp.int32))
    lists = [
        pltpu.make_async_copy(firsts_v, firsts, sems.at[2]),
        pltpu.make_async_copy(wmore_v, wmore, sems.at[3]),
        pltpu.make_async_copy(nmore_v, nmore, sems.at[4]),
    ]
    for copy in lists:
        copy.start()
    for copy in lists + copies:
        copy.wait()

    def base_of(source):
        yz = source >> 3
        x = (source >> 1) & 3
        row = source & 1
        return ((row ^ my_row) << 11) + (((x - my_x) & 3) << 9) + (yz << 4)

    def one_source(source, _):
        base = pl.multiple_of(base_of(source), BAGS)
        group = source & 31
        column = (source >> 5) * BAGS
        for bag in range(BAGS):
            pair = firsts[group, column + bag]
            wide_sum[pl.ds(base + bag, 1), :] = wide_rows[pl.ds(pair & 65535, 1), :]
            narrow_sum[pl.ds(base + bag, 1), :] = narrow_rows[pl.ds(pair >> 16, 1), :]
        return 0

    lax.fori_loop(0, 256, one_source, 0)

    def more_of(source, _):
        base = base_of(source)

        def add(lists, rows, total):
            def one(i, _):
                entry = lists[source, i]
                at = pl.ds(base + (entry >> 12), 1)
                total[at, :] = total[at, :] + rows[pl.ds(entry & 4095, 1), :]
                return 0

            lax.fori_loop(0, lists[source, LANES - 1], one, 0)

        add(wmore, wide_rows, wide_sum)
        add(nmore, narrow_rows, narrow_sum)
        return 0

    lax.fori_loop(0, 256, more_of, 0)

    def finish(ref, start):
        def one(i, _):
            rows = pl.ds(pl.multiple_of(i * 128, 128), 128)
            source = pl.ds(pl.multiple_of(start + i * 128, 128), 128)
            ref[rows, 0:LANES] = wide_sum[source, :].astype(jnp.bfloat16)
            ref[rows, LANES:] = narrow_sum[source, :].astype(jnp.bfloat16)
            return 0

        lax.fori_loop(0, 16, one, 0)

    finish(keep_ref, 0)
    finish(send_ref, 2048)


def pool(place, words, wide, narrow):
    vmem = pl.BlockSpec(memory_space=pltpu.VMEM)
    half = jax.ShapeDtypeStruct((2048, 256), jnp.bfloat16)
    return pl.pallas_call(
        pool_kernel,
        out_shape=(half, half),
        in_specs=[pl.BlockSpec(memory_space=pltpu.SMEM), vmem,
                  pl.BlockSpec(memory_space=pl.ANY), pl.BlockSpec(memory_space=pl.ANY)],
        out_specs=(vmem, vmem),
        scratch_shapes=[
            pltpu.VMEM((4104, LANES), jnp.float32),
            pltpu.VMEM((4104, LANES), jnp.float32),
            pltpu.VMEM((4096, LANES), jnp.float32),
            pltpu.VMEM((4096, LANES), jnp.float32),
            pltpu.VMEM((32, LANES), jnp.int32),
            pltpu.VMEM((256, LANES), jnp.int32),
            pltpu.VMEM((256, LANES), jnp.int32),
            pltpu.SMEM((32, LANES), jnp.int32),
            pltpu.SMEM((256, LANES), jnp.int32),
            pltpu.SMEM((256, LANES), jnp.int32),
            pltpu.SemaphoreType.DMA((5,)),
        ],
        compiler_params=pltpu.CompilerParams(vmem_limit_bytes=40 * 1024 * 1024),
    )(place, words, wide, narrow)


HOME = ("y", "z", "x", "row")
TABLES = ("y", "z")


def dense_layer(values, weight):
    return jnp.maximum(jnp.dot(values, weight, preferred_element_type=jnp.float32), 0.0).astype(
        jnp.bfloat16
    )


def turned(block, axis, count, shift):
    return lax.ppermute(block, axis, [(i, (i + shift) % count) for i in range(count)])


def coded(indices, lengths):
    slots = lax.broadcasted_iota(jnp.int32, indices.shape, 2)
    return jnp.where(slots < lengths[:, :, None], indices, 32768)


def body(
    dense_input,
    bottom_first,
    bottom_second,
    bottom_third,
    wide_tables,
    narrow_tables,
    wide_indices,
    wide_lengths,
    narrow_indices,
    narrow_lengths,
    wide_projection,
    narrow_projection,
    top_first,
    top_last,
):
    own_table = lax.axis_index(TABLES)
    place = jnp.stack([lax.axis_index("x"), lax.axis_index("row")]).astype(jnp.int32)

    words = coded(wide_indices, wide_lengths) | (coded(narrow_indices, narrow_lengths) << 16)
    words = jnp.transpose(words, (1, 2, 0)).reshape(32, 1, LANES)
    words = jnp.broadcast_to(words, (32, 8, LANES)).reshape(256, LANES)
    words = lax.all_to_all(words, HOME, 0, 0, tiled=True)

    wide_weight = lax.dynamic_index_in_dim(wide_projection, own_table, 0, keepdims=False)
    narrow_weight = lax.dynamic_index_in_dim(narrow_projection, own_table, 0, keepdims=False)
    wide_rows = jnp.dot(wide_tables, wide_weight, preferred_element_type=jnp.float32)
    narrow_rows = jnp.dot(narrow_tables, narrow_weight, preferred_element_type=jnp.float32)

    keep, send = pool(place, words, wide_rows, narrow_rows)
    other = turned(send, "row", 2, 1)
    both = (keep.astype(jnp.float32) + other.astype(jnp.float32)).astype(jnp.bfloat16)
    both = both.reshape(4, 512, 256)
    total = both[0].astype(jnp.float32)
    for shift in (1, 2, 3):
        total = total + turned(both[shift], "x", 4, shift).astype(jnp.float32)
    home = lax.all_to_all(
        total.astype(jnp.bfloat16).reshape(32, BAGS, 256), TABLES, 0, 0, tiled=True
    )

    bottom = dense_layer(
        dense_layer(dense_layer(dense_input, bottom_first), bottom_second), bottom_third
    )
    features = jnp.concatenate([bottom[None], home[:, :, :LANES], home[:, :, LANES:]], 0)
    products = jnp.einsum("fbe,gbe->bfg", features, features, preferred_element_type=jnp.float32)
    pairs = jnp.concatenate([products[:, f, f + 1 :] for f in range(64)], 1)
    joined = jnp.concatenate([bottom.astype(jnp.float32), pairs], 1).astype(jnp.bfloat16)
    hidden = dense_layer(joined, top_first)
    logits = jnp.dot(hidden, top_last, preferred_element_type=jnp.float32)
    return (hidden, logits)


def solution(mesh):
    fine = Mesh(mesh.devices.reshape(4, 8, 4, 2), HOME)
    split = P(HOME)
    in_specs = (split, P(), P(), P()) + (split,) * 6 + (P(),) * 4
    return jax.shard_map(
        body, mesh=fine, in_specs=in_specs, out_specs=(split, split), check_vma=False
    )
```

time: 390 us -> 121 us (0.31); the launches traced: 382 us -> 120 us
  matrix products: 254 us -> 9.82 us
  Pallas kernels: 0 us -> 41.8 us
  local copies, waits for them, and re-layouts: 35.4 us -> 9.18 us
  waiting for transfers between devices: 54.4 us -> 31.4 us
  blocking collectives: 7.01 us -> 0 us
    dot_general x18 -> x2, matrix products: 249 us -> 5.5 us  [the longest x1 2.94 us: body(): jnp.dot(wide_tables, wide_weight, preferred_element_type=jnp.float32)]
    pallas_call x0 -> x1, Pallas kernels: none -> 41.8 us  [pool(): pl.pallas_call(pool_kernel, out_shape=(half, half), in_specs=[pl.BlockSpe...]
    ppermute x2 -> x4, waiting for transfers between devices: 29.7 us -> 13.6 us  [turned(): lax.ppermute(block, axis, [(i, (i + shift) % count) for i in range(count)])]
    another operation x10 -> x0, local copies, waits for them, and re-layouts: 9.18 us -> none
    all_to_all x2, waiting for transfers between devices: 24.7 us -> 17.8 us  [the longest x1 11.3 us: body(): lax.all_to_all(total.astype(jnp.bfloat16).reshape(32, BAGS, 256), TABLES,...]
    all_to_all x1 -> x0, blocking collectives: 5 us -> none  [sent_and_summed(): lax.all_to_all(in_blocks(shard, dim, length), axis, 0, 0, tiled=True)]
    concatenate x4 -> x1, local copies, waits for them, and re-layouts: 4.9 us -> 0.18 us  [body(): jnp.concatenate([bottom.astype(jnp.float32), pairs], 1).astype(jnp.bfloat16)]
  transfers between devices with their start and end apart: 4 -> 6, of which waited for: 4 -> 6; matrix products, arithmetic and copies ran while one was open for 0% -> 5% of each run, Pallas kernels for 0% -> 0%
where the time goes in v1:
time: 121 us; the launch traced here: 120 us
  Pallas kernels  41.8 us (35%)
  waiting for transfers between devices  31.4 us (26%)
  starting transfers between devices  24.5 us (20%)
  matrix products  9.82 us (8%)
  local copies, waits for them, and re-layouts  9.18 us (8%)
  other arithmetic  2.26 us (2%)
    pallas_call x1, Pallas kernels, pool(): pl.pallas_call(pool_kernel, out_shape=(half, half), in_specs=[pl.BlockSpe...  41.8 us
    all_to_all x1, starting transfers between devices, body(): words = lax.all_to_all(words, HOME, 0, 0, tiled=True)  14.4 us
    ppermute x4, waiting for transfers between devices, turned(): lax.ppermute(block, axis, [(i, (i + shift) % count) for i in range(count)])  13.6 us
    all_to_all x1, waiting for transfers between devices, body(): lax.all_to_all(total.astype(jnp.bfloat16).reshape(32, BAGS, 256), TABLES,...  11.3 us
    all_to_all x1, waiting for transfers between devices, body(): words = lax.all_to_all(words, HOME, 0, 0, tiled=True)  6.44 us
    ppermute x4, starting transfers between devices, turned(): lax.ppermute(block, axis, [(i, (i + shift) % count) for i in range(count)])  5.36 us
    all_to_all x1, starting transfers between devices, body(): lax.all_to_all(total.astype(jnp.bfloat16).reshape(32, BAGS, 256), TABLES,...  4.8 us
    squeeze x64, local copies, waits for them, and re-layouts, body(): pairs = jnp.concatenate([products[:, f, f + 1:] for f in range(64)], 1)  4.78 us
  transfers between devices with their start and end apart: 6, of which 6 were waited for; matrix products, arithmetic and copies ran while one was open for 5% of the time, Pallas kernels for 0%

profile of v1, /device:TPU:32, one launch (start us, length us, event | category | flops | bytes accessed | tf_op | source)
XLA Modules:
  0.0 119.8 jit_solution(4264328626061238788)
XLA Ops:
  0.6 1.0 or_bitcast_fusion
  1.8 0.7 broadcast_in_dim.20
  2.5 14.4 %all-to-all-start = ((s32[256,1,128]{2,1,0:T(1,128)}), s32[256,1,128]{2,1,0:T(1,128)S(1)}, u32[]{:S(2)}, u32[]{:S(2)}) async-start(s32[256,1,128]{2,1,0:T(1,128)} %bitcast.5), calls=%async_computation | async-start | bytes 262144 | tf_op jit(solution)/shard_map/all_to_all | solution.py:194
  16.9 0.1 pad_add_fusion.place_ref
  16.9 2.9 %convolution_bitcast_fusion.wide_ref = f32[4096,128]{1,0:T(8,128)} fusion(bf16[4096,256]{1,0:T(8,128)(2,1)S(1)} %copy-done, bf16[32,256,128]{2,1,0:T(8,128)(2,1)} %param.24, s32[]{:T(128)S(6)} %select_n.15), kind=kOutput, calls=%fused_computation | convolution fusion | flops 268435456 | bytes 4259844 | tf_op jit(solution)/shard_map/dot_general | solution.py:198
  19.9 2.6 %convolution_bitcast_fusion.1.narrow_ref = f32[4096,128]{1,0:T(8,128)} fusion(bf16[4096,64]{0,1:T(8,128)(2,1)S(1)} %copy-done.3, bf16[32,64,128]{2,1,0:T(8,128)(2,1)} %param.25, s32[]{:T(128)S(6)} %select_n.15), kind=kOutput, calls=%fused_computation.1 | convolution fusion | flops 67108864 | bytes 2637828 | tf_op jit(solution)/shard_map/dot_general | solution.py:199
  22.4 6.4 %all-to-all-done = s32[256,1,128]{2,1,0:T(1,128)S(1)} async-done(((s32[256,1,128]{2,1,0:T(1,128)}), s32[256,1,128]{2,1,0:T(1,128)S(1)}, u32[]{:S(2)}, u32[]{:S(2)}) %all-to-all-start) | async-done | bytes 131104 | tf_op jit(solution)/shard_map/all_to_all | solution.py:194
  28.9 1.6 %copy-done.1 = f32[4096,128]{1,0:T(8,128)S(1)} copy-done((f32[4096,128]{1,0:T(8,128)S(1)}, f32[4096,128]{1,0:T(8,128)}, u32[]{:S(2)}) %copy-start.1) | copy-done | bytes 2097176
  30.5 1.6 %copy-done.2 = f32[4096,128]{1,0:T(8,128)S(1)} copy-done((f32[4096,128]{1,0:T(8,128)S(1)}, f32[4096,128]{1,0:T(8,128)}, u32[]{:S(2)}) %copy-start.2) | copy-done | bytes 2097176
  32.1 41.8 %shard_map.149 = (bf16[2048,256]{1,0:T(8,128)(2,1)S(1)}, bf16[2048,256]{1,0:T(8,128)(2,1)S(1)}) custom-call(s32[2]{0:T(128)S(1)} %pad_add_fusion.place_ref, s32[256,128]{1,0:T(8,128)S(1)} %bitcast.160, f32[4096,128]{1,0:T(8,128)S(1)} %copy-done.1, f32[4096,128]{1,0:T(8,128)S(1)} %copy-done.2), custom_call_target="tpu_custom_call" | custom-call | tf_op jit(solution)/shard_map/pallas_call | solution.py:130
  73.8 0.5 collective-permute-start
  74.4 2.3 %collective-permute-done = bf16[2048,256]{1,0:T(8,128)(2,1)S(1)} collective-permute-done((bf16[2048,256]{1,0:T(8,128)(2,1)S(1)}, bf16[2048,256]{1,0:T(8,128)(2,1)S(1)}, u32[]{:S(2)}, u32[]{:S(2)}) %collective-permute-start) | collective-permute-done | bytes 1048608 | tf_op jit(solution)/shard_map/ppermute | solution.py:164
  76.7 0.3 add_convert_fusion
  77.1 0.9 collective-permute-start.1
  78.0 2.8 %collective-permute-start.2 = (bf16[512,256]{1,0:T(8,128)(2,1)S(1)}, bf16[512,256]{1,0:T(8,128)(2,1)S(1)}, u32[]{:S(2)}, u32[]{:S(2)}) collective-permute-start(bf16[512,256]{1,0:T(8,128)(2,1)S(1)} %get-tuple-element.8), channel_id=1, source_target_pairs={{0,4},{2,6},{4,0},{6,2},{1,5},{3,7},{5,1},{7,3},{8,12},{10,14},{12... | collective-permute-start | bytes 786440 | tf_op jit(solution)/shard_map/ppermute | solution.py:164
  80.8 1.1 collective-permute-start.3
  81.9 5.7 %collective-permute-done.1 = bf16[512,256]{1,0:T(8,128)(2,1)S(1)} collective-permute-done((bf16[512,256]{1,0:T(8,128)(2,1)S(1)}, bf16[512,256]{1,0:T(8,128)(2,1)S(1)}, u32[]{:S(2)}, u32[]{:S(2)}) %collective-permute-start.1) | collective-permute-done | bytes 262176 | tf_op jit(solution)/shard_map/ppermute | solution.py:164
  87.6 5.2 %collective-permute-done.2 = bf16[512,256]{1,0:T(8,128)(2,1)S(1)} collective-permute-done((bf16[512,256]{1,0:T(8,128)(2,1)S(1)}, bf16[512,256]{1,0:T(8,128)(2,1)S(1)}, u32[]{:S(2)}, u32[]{:S(2)}) %collective-permute-start.2) | collective-permute-done | bytes 262176 | tf_op jit(solution)/shard_map/ppermute | solution.py:164
  92.7 0.5 collective-permute-done.3
  93.2 0.8 add_convert_fusion.1
  94.0 4.8 %all-to-all-start.1 = ((bf16[32,16,256]{2,1,0:T(8,128)(2,1)}), bf16[32,16,256]{2,1,0:T(8,128)(2,1)S(1)}, u32[]{:S(2)}, u32[]{:S(2)}) async-start(bf16[32,16,256]{2,1,0:T(8,128)(2,1)} %bitcast.11), calls=%async_computation.1 | async-start | bytes 524288 | tf_op jit(solution)/shard_map/all_to_all | solution.py:208
  98.9 0.2 fusion.4
  99.1 0.1 fusion.5
  99.3 11.3 %all-to-all-done.1 = bf16[32,16,256]{2,1,0:T(8,128)(2,1)S(1)} async-done(((bf16[32,16,256]{2,1,0:T(8,128)(2,1)}), bf16[32,16,256]{2,1,0:T(8,128)(2,1)S(1)}, u32[]{:S(2)}, u32[]{:S(2)}) %all-to-all-start.1) | async-done | bytes 262176 | tf_op jit(solution)/shard_map/all_to_all | solution.py:208
  110.8 0.3 fusion.6
  111.1 0.1 slice_bitcast_fusion
  111.2 0.1 slice_bitcast_fusion.1
  111.3 0.1 slice_bitcast_fusion.10
  111.4 0.1 slice_bitcast_fusion.11
  111.5 0.1 slice_bitcast_fusion.13
  111.6 0.1 slice_bitcast_fusion.14
  111.7 0.1 slice_bitcast_fusion.15
  111.7 0.1 slice_bitcast_fusion.16
  111.8 0.1 slice_bitcast_fusion.17
  111.9 0.1 slice_bitcast_fusion.18
  112.0 0.1 slice_bitcast_fusion.2
  112.1 0.1 slice_bitcast_fusion.20
  112.2 0.1 slice_bitcast_fusion.21
  112.3 0.1 slice_bitcast_fusion.22
  112.3 0.1 slice_bitcast_fusion.23
  112.5 0.1 slice_bitcast_fusion.25
  112.6 0.1 slice_bitcast_fusion.26
  112.6 0.1 slice_bitcast_fusion.27
  112.7 0.1 slice_bitcast_fusion.28
  112.8 0.1 slice_bitcast_fusion.29
  116.0 0.2 concatenate.8
  116.1 3.0 %fusion = bf16[16,1024]{1,0:T(8,128)(2,1)S(1)} fusion(bf16[16,2208]{1,0:T(8,128)(2,1)S(1)} %concatenate.8, bf16[2208,1024]{1,0:T(8,128)(2,1)} %param.26), kind=kOutput, calls=%fused_computation.4 | convolution fusion | flops 72384512 | bytes 4625408 | tf_op jit(solution)/shard_map/dot_general | solution.py:158
  119.1 0.6 convolution_bitcast_fusion.2
  (71 shorter events, 3.6 us)
Async XLA Ops:
  0.6 16.3 %copy-start = (bf16[4096,256]{1,0:T(8,128)(2,1)S(1)}, bf16[4096,256]{1,0:T(8,128)(2,1)}, u32[]{:S(2)}) copy-start(bf16[4096,256]{1,0:T(8,128)(2,1)} %param.18) | copy-start | bytes 6291460
  2.5 26.4 %all-to-all-start = ((s32[256,1,128]{2,1,0:T(1,128)}), s32[256,1,128]{2,1,0:T(1,128)S(1)}, u32[]{:S(2)}, u32[]{:S(2)}) async-start(s32[256,1,128]{2,1,0:T(1,128)} %bitcast.5), calls=%async_computation | async-start | bytes 262144 | tf_op jit(solution)/shard_map/all_to_all | solution.py:194
  16.9 2.9 %copy-start.3 = (bf16[4096,64]{0,1:T(8,128)(2,1)S(1)}, bf16[4096,64]{0,1:T(8,128)(2,1)}, u32[]{:S(2)}) copy-start(bf16[4096,64]{0,1:T(8,128)(2,1)} %param.19) | copy-start | bytes 1572868
  28.9 1.6 %copy-start.1 = (f32[4096,128]{1,0:T(8,128)S(1)}, f32[4096,128]{1,0:T(8,128)}, u32[]{:S(2)}) copy-start(f32[4096,128]{1,0:T(8,128)} %convolution_bitcast_fusion.wide_ref) | copy-start | bytes 6291460
  30.5 1.6 %copy-start.2 = (f32[4096,128]{1,0:T(8,128)S(1)}, f32[4096,128]{1,0:T(8,128)}, u32[]{:S(2)}) copy-start(f32[4096,128]{1,0:T(8,128)} %convolution_bitcast_fusion.1.narrow_ref) | copy-start | bytes 6291460
  73.8 2.8 %collective-permute-start = (bf16[2048,256]{1,0:T(8,128)(2,1)S(1)}, bf16[2048,256]{1,0:T(8,128)(2,1)S(1)}, u32[]{:S(2)}, u32[]{:S(2)}) collective-permute-start(bf16[2048,256]{1,0:T(8,128)(2,1)S(1)} %get-tuple-element.5), channel_id=1, source_target_pairs={{0,1},{1,0},{2,3},{3,2},{4,5},{5,4},{6,7},{7,6},{8,9},{9,8},{10,11... | collective-permute-start | bytes 3145736 | tf_op jit(solution)/shard_map/ppermute | solution.py:164
  77.0 21.9 %copy-start.4 = (bf16[512,256]{1,0:T(8,128)(2,1)S(1)}, bf16[512,256]{1,0:T(8,128)(2,1)}, u32[]{:S(2)}) copy-start(bf16[512,256]{1,0:T(8,128)(2,1)} %param.16) | copy-start | bytes 786436
  77.0 21.9 %copy-start.7 = (bf16[13,512]{1,0:T(8,128)(2,1)S(1)}, bf16[13,512]{1,0:T(8,128)(2,1)}, u32[]{:S(2)}) copy-start(bf16[13,512]{1,0:T(8,128)(2,1)} %param.15) | copy-start | bytes 39940
  77.0 21.9 %copy-start.8 = (bf16[16,13]{1,0:T(8,128)(2,1)S(1)}, bf16[16,13]{1,0:T(8,128)(2,1)}, u32[]{:S(2)}) copy-start(bf16[16,13]{1,0:T(8,128)(2,1)} %param.14) | copy-start | bytes 1252
  77.0 22.1 %copy-start.5 = (bf16[256,128]{1,0:T(8,128)(2,1)S(1)}, bf16[256,128]{1,0:T(8,128)(2,1)}, u32[]{:S(2)}) copy-start(bf16[256,128]{1,0:T(8,128)(2,1)} %param.17) | copy-start | bytes 196612
  77.0 22.3 %copy-start.9 = (bf16[1024]{0:T(1024)(128)(2,1)S(1)}, bf16[1024]{0:T(1024)(128)(2,1)}, u32[]{:S(2)}) copy-start(bf16[1024]{0:T(1024)(128)(2,1)} %param.27) | copy-start | bytes 6148
  77.1 10.5 %collective-permute-start.1 = (bf16[512,256]{1,0:T(8,128)(2,1)S(1)}, bf16[512,256]{1,0:T(8,128)(2,1)S(1)}, u32[]{:S(2)}, u32[]{:S(2)}) collective-permute-start(bf16[512,256]{1,0:T(8,128)(2,1)S(1)} %get-tuple-element.6), channel_id=1, source_target_pairs={{0,2},{2,4},{4,6},{6,0},{1,3},{3,5},{5,7},{7,1},{8,10},{10,12},{12... | collective-permute-start | bytes 786440 | tf_op jit(solution)/shard_map/ppermute | solution.py:164
  78.0 14.7 %collective-permute-start.2 = (bf16[512,256]{1,0:T(8,128)(2,1)S(1)}, bf16[512,256]{1,0:T(8,128)(2,1)S(1)}, u32[]{:S(2)}, u32[]{:S(2)}) collective-permute-start(bf16[512,256]{1,0:T(8,128)(2,1)S(1)} %get-tuple-element.8), channel_id=1, source_target_pairs={{0,4},{2,6},{4,0},{6,2},{1,5},{3,7},{5,1},{7,3},{8,12},{10,14},{12... | collective-permute-start | bytes 786440 | tf_op jit(solution)/shard_map/ppermute | solution.py:164
  80.8 12.4 %collective-permute-start.3 = (bf16[512,256]{1,0:T(8,128)(2,1)S(1)}, bf16[512,256]{1,0:T(8,128)(2,1)S(1)}, u32[]{:S(2)}, u32[]{:S(2)}) collective-permute-start(bf16[512,256]{1,0:T(8,128)(2,1)S(1)} %get-tuple-element.7), channel_id=1, source_target_pairs={{0,6},{2,0},{4,2},{6,4},{1,7},{3,1},{5,3},{7,5},{8,14},{10,8},{12,... | collective-permute-start | bytes 786440 | tf_op jit(solution)/shard_map/ppermute | solution.py:164
  94.0 16.6 %all-to-all-start.1 = ((bf16[32,16,256]{2,1,0:T(8,128)(2,1)}), bf16[32,16,256]{2,1,0:T(8,128)(2,1)S(1)}, u32[]{:S(2)}, u32[]{:S(2)}) async-start(bf16[32,16,256]{2,1,0:T(8,128)(2,1)} %bitcast.11), calls=%async_computation.1 | async-start | bytes 524288 | tf_op jit(solution)/shard_map/all_to_all | solution.py:208
  119.1 0.6 copy-start.6

commit v2 on v1

v2 whole, which is shorter than its diff:
```python
import jax
import jax.numpy as jnp
from jax import lax
from jax.experimental import pallas as pl
from jax.experimental.pallas import tpu as pltpu
from jax.sharding import Mesh
from jax.sharding import PartitionSpec as P

SLOTS = 8
BAGS = 16
LANES = 128
ROWS = 4096
SOURCES = 256


def drawn_left(packed, field, unit, bits):
    for bit in range(bits):
        moved = jnp.where((packed & (1 << (field + bit))) != 0, packed, 0)
        packed = packed - moved + pltpu.roll(moved, LANES - (unit << bit), 1)
    return packed


def counted(flags, before):
    return jnp.dot(
        jnp.where(flags, 1.0, 0.0).astype(jnp.bfloat16), before, preferred_element_type=jnp.float32
    ).astype(jnp.int32)


def as_matrix(flags):
    return jnp.where(flags, 1.0, 0.0).astype(jnp.bfloat16)


def pool_kernel(place_ref, words_ref, wide_ref, narrow_ref, keep_ref, send_ref,
                wide_rows, narrow_rows, wide_sum, narrow_sum, firsts_v, more_v, lists_v,
                firsts, lists, sems):
    tables = [
        pltpu.make_async_copy(wide_ref, wide_rows.at[pl.ds(0, ROWS)], sems.at[0]),
        pltpu.make_async_copy(narrow_ref, narrow_rows.at[pl.ds(0, ROWS)], sems.at[1]),
    ]
    for copy in tables:
        copy.start()
    my_x = place_ref[0]
    my_row = place_ref[1]
    shard = my_x * 2 + my_row
    wide_rows[pl.ds(ROWS, 8), :] = jnp.zeros((8, LANES), jnp.float32)
    narrow_rows[pl.ds(ROWS, 8), :] = jnp.zeros((8, LANES), jnp.float32)
    at = lax.broadcasted_iota(jnp.int32, (LANES, LANES), 0)
    to = lax.broadcasted_iota(jnp.int32, (LANES, LANES), 1)
    same_bag = as_matrix(((at & 15) == (to & 15)) & (at < to))
    any_bag = as_matrix(at < to)

    def base_of(source):
        yz = source >> 3
        x = (source >> 1) & 3
        row = source & 1
        return ((row ^ my_row) << 11) + (((x - my_x) & 3) << 9) + (yz << 4)

    lane = lax.broadcasted_iota(jnp.int32, (SOURCES, LANES), 1)
    target = base_of(lax.broadcasted_iota(jnp.int32, (SOURCES, LANES), 0)) + (lane & 15)
    words = words_ref[...]
    most = jnp.int32(0)
    picks = []
    for kind, value in enumerate((words & 65535, (words >> 16) & 65535)):
        local = (value >> 12) == shard
        gap = (lane >> 4) - counted(local, same_bag)
        packed = jnp.where(local, (value & 4095) | (gap << 12) | (1 << 15), 0)
        packed = drawn_left(packed, 12, BAGS, 3)
        picks.append(jnp.where(packed != 0, packed & 4095, ROWS))
        more = (packed != 0) & (lane >= BAGS)
        before = counted(more, any_bag)
        most = jnp.maximum(most, jnp.max(before + more.astype(jnp.int32)))
        extra = (packed & 4095) | (target << 12) | ((lane - before) << 24) | jnp.int32(-(2**31))
        extra = drawn_left(jnp.where(more, extra, 0), 24, 1, 7)
        more_v[kind] = jnp.transpose(extra)
    pair = jnp.where(lane < BAGS, picks[0] | (picks[1] << 16), 0)
    line = pair[0:32]
    for j in range(1, 8):
        line = line + pltpu.roll(pair[j * 32 : (j + 1) * 32], j * BAGS, 1)
    firsts_v[...] = line
    first_copy = pltpu.make_async_copy(firsts_v, firsts, sems.at[2])
    first_copy.start()
    first_copy.wait()
    for copy in tables:
        copy.wait()

    def one_group(group, _):
        for j in range(8):
            base = pl.multiple_of(base_of(j * 32 + group), BAGS)
            for low in range(0, BAGS, 8):
                bags = range(low, low + 8)
                both = [firsts[group, j * BAGS + bag] for bag in bags]
                wide = [wide_rows[pl.ds(pair & 65535, 1), :] for pair in both]
                narrow = [narrow_rows[pl.ds(pair >> 16, 1), :] for pair in both]
                for bag, row in zip(bags, wide):
                    wide_sum[pl.ds(base + bag, 1), :] = row
                for bag, row in zip(bags, narrow):
                    narrow_sum[pl.ds(base + bag, 1), :] = row
        return 0

    lax.fori_loop(0, 32, one_group, 0)

    lane32 = lax.broadcasted_iota(jnp.int32, (32, LANES), 1)

    def one_block(block, _):
        rows = pl.ds(pl.multiple_of(block * 8, 8), 8)
        held = jnp.concatenate(
            [more_v[kind, rows, half * LANES : (half + 1) * LANES] for kind in (0, 1) for half in (0, 1)], 0
        )
        used = held < 0
        before = counted(used, any_bag)
        total = jnp.sum(used.astype(jnp.int32), axis=1, keepdims=True)
        packed = jnp.where(used, (held & 0xFFFFFF) | ((lane32 - before) << 24), 0)
        packed = drawn_left(packed, 24, 1, 7) & 0xFFFFFF
        lists_v[...] = packed | jnp.where(lane32 == 0, total << 24, 0)
        copy = pltpu.make_async_copy(lists_v, lists, sems.at[3])
        copy.start()
        copy.wait()

        def add(low, rows, sums):
            def one_list(k, _):
                def some(low, count):
                    entries = [lists[k, low + i] for i in range(count)]
                    places = [pl.ds((entry >> 12) & 4095, 1) for entry in entries]
                    values = [
                        sums[place, :] + rows[pl.ds(entry & 4095, 1), :]
                        for entry, place in zip(entries, places)
                    ]
                    for place, value in zip(places, values):
                        sums[place, :] = value

                def four(i, _):
                    some(i * 4, 4)
                    return 0

                def one(i, _):
                    some(i, 1)
                    return 0

                count = lax.shift_right_logical(lists[k, 0], 24)
                lax.fori_loop(0, count // 4, four, 0)
                lax.fori_loop(count // 4 * 4, count, one, 0)
                return 0

            lax.fori_loop(low, low + 16, one_list, 0)

        add(0, wide_rows, wide_sum)
        add(16, narrow_rows, narrow_sum)
        return 0

    lax.fori_loop(0, (most + 7) >> 3, one_block, 0)

    def finish(ref, start):
        def one(i, _):
            rows = pl.ds(pl.multiple_of(i * 128, 128), 128)
            source = pl.ds(pl.multiple_of(start + i * 128, 128), 128)
            ref[rows, 0:LANES] = wide_sum[source, :].astype(jnp.bfloat16)
            ref[rows, LANES:] = narrow_sum[source, :].astype(jnp.bfloat16)
            return 0

        lax.fori_loop(0, 16, one, 0)

    finish(keep_ref, 0)
    finish(send_ref, 2048)


def pool(place, words, wide, narrow):
    vmem = pl.BlockSpec(memory_space=pltpu.VMEM)
    half = jax.ShapeDtypeStruct((2048, 256), jnp.bfloat16)
    return pl.pallas_call(
        pool_kernel,
        out_shape=(half, half),
        in_specs=[pl.BlockSpec(memory_space=pltpu.SMEM), vmem,
                  pl.BlockSpec(memory_space=pl.ANY), pl.BlockSpec(memory_space=pl.ANY)],
        out_specs=(vmem, vmem),
        scratch_shapes=[
            pltpu.VMEM((ROWS + 8, LANES), jnp.float32),
            pltpu.VMEM((ROWS + 8, LANES), jnp.float32),
            pltpu.VMEM((ROWS, LANES), jnp.float32),
            pltpu.VMEM((ROWS, LANES), jnp.float32),
            pltpu.VMEM((32, LANES), jnp.int32),
            pltpu.VMEM((2, LANES, SOURCES), jnp.int32),
            pltpu.VMEM((32, LANES), jnp.int32),
            pltpu.SMEM((32, LANES), jnp.int32),
            pltpu.SMEM((32, LANES), jnp.int32),
            pltpu.SemaphoreType.DMA((4,)),
        ],
        compiler_params=pltpu.CompilerParams(vmem_limit_bytes=60 * 1024 * 1024),
    )(place, words, wide, narrow)


HOME = ("y", "z", "x", "row")
TABLES = ("y", "z")


def dense_layer(values, weight):
    return jnp.maximum(jnp.dot(values, weight, preferred_element_type=jnp.float32), 0.0).astype(
        jnp.bfloat16
    )


def turned(block, axis, count, shift):
    return lax.ppermute(block, axis, [(i, (i + shift) % count) for i in range(count)])


def coded(indices, lengths):
    slots = lax.broadcasted_iota(jnp.int32, indices.shape, 2)
    return jnp.where(slots < lengths[:, :, None], indices, 32768)


def body(
    dense_input,
    bottom_first,
    bottom_second,
    bottom_third,
    wide_tables,
    narrow_tables,
    wide_indices,
    wide_lengths,
    narrow_indices,
    narrow_lengths,
    wide_projection,
    narrow_projection,
    top_first,
    top_last,
):
    own_table = lax.axis_index(TABLES)
    place = jnp.stack([lax.axis_index("x"), lax.axis_index("row")]).astype(jnp.int32)

    words = coded(wide_indices, wide_lengths) | (coded(narrow_indices, narrow_lengths) << 16)
    words = jnp.transpose(words, (1, 2, 0)).reshape(32, 1, LANES)
    words = jnp.broadcast_to(words, (32, 8, LANES)).reshape(256, LANES)
    words = lax.all_to_all(words, HOME, 0, 0, tiled=True)

    wide_weight = lax.dynamic_index_in_dim(wide_projection, own_table, 0, keepdims=False)
    narrow_weight = lax.dynamic_index_in_dim(narrow_projection, own_table, 0, keepdims=False)
    wide_rows = jnp.dot(wide_tables, wide_weight, preferred_element_type=jnp.float32)
    narrow_rows = jnp.dot(narrow_tables, narrow_weight, preferred_element_type=jnp.float32)

    keep, send = pool(place, words, wide_rows, narrow_rows)
    other = turned(send, "row", 2, 1)
    both = (keep.astype(jnp.float32) + other.astype(jnp.float32)).astype(jnp.bfloat16)
    both = both.reshape(4, 512, 256)
    total = both[0].astype(jnp.float32)
    for shift in (1, 2, 3):
        total = total + turned(both[shift], "x", 4, shift).astype(jnp.float32)
    home = lax.all_to_all(
        total.astype(jnp.bfloat16).reshape(32, BAGS, 256), TABLES, 0, 0, tiled=True
    )

    bottom = dense_layer(
        dense_layer(dense_layer(dense_input, bottom_first), bottom_second), bottom_third
    )
    features = jnp.concatenate([bottom[None], home[:, :, :LANES], home[:, :, LANES:]], 0)
    products = jnp.einsum("fbe,gbe->bfg", features, features, preferred_element_type=jnp.float32)
    pairs = jnp.concatenate([products[:, f, f + 1 :] for f in range(64)], 1)
    joined = jnp.concatenate([bottom.astype(jnp.float32), pairs], 1).astype(jnp.bfloat16)
    hidden = dense_layer(joined, top_first)
    logits = jnp.dot(hidden, top_last, preferred_element_type=jnp.float32)
    return (hidden, logits)


def solution(mesh):
    fine = Mesh(mesh.devices.reshape(4, 8, 4, 2), HOME)
    split = P(HOME)
    in_specs = (split, P(), P(), P()) + (split,) * 6 + (P(),) * 4
    return jax.shard_map(
        body, mesh=fine, in_specs=in_specs, out_specs=(split, split), check_vma=False
    )
```

time: 121 us -> 95 us (0.79)
  Pallas kernels: 41.8 us -> 15.7 us
  local copies, waits for them, and re-layouts: 9.18 us -> 6.65 us
  other arithmetic: 2.26 us -> 4.02 us
    pallas_call x1, Pallas kernels: 41.8 us -> 15.7 us  [pool(): pl.pallas_call(pool_kernel, out_shape=(half, half), in_specs=[pl.BlockSpe...]
    unnamed x23 -> x21, local copies, waits for them, and re-layouts: 3.31 us -> 0.78 us
    convert_element_type x1, other arithmetic: 0.3 us -> 1.55 us  [body(): (keep.astype(jnp.float32) + other.astype(jnp.float32)).astype(jnp.bfloat16)]
  transfers between devices with their start and end apart: 6 -> 6, of which waited for: 6 -> 5; matrix products, arithmetic and copies ran while one was open for 5% -> 7% of each run, Pallas kernels for 0% -> 0%
where the time goes in v2:
time: 95 us; the launch traced here: 93.8 us
  waiting for transfers between devices  31.5 us (33%)
  starting transfers between devices  25.3 us (27%)
  Pallas kernels  15.7 us (17%)
  matrix products  9.81 us (10%)
  local copies, waits for them, and re-layouts  6.65 us (7%)
  other arithmetic  4.02 us (4%)
    pallas_call x1, Pallas kernels, pool(): pl.pallas_call(pool_kernel, out_shape=(half, half), in_specs=[pl.BlockSpe...  15.7 us
    all_to_all x1, starting transfers between devices, body(): words = lax.all_to_all(words, HOME, 0, 0, tiled=True)  14.4 us
    ppermute x4, waiting for transfers between devices, turned(): lax.ppermute(block, axis, [(i, (i + shift) % count) for i in range(count)])  14.2 us
    all_to_all x1, waiting for transfers between devices, body(): lax.all_to_all(total.astype(jnp.bfloat16).reshape(32, BAGS, 256), TABLES,...  11.3 us
    all_to_all x1, waiting for transfers between devices, body(): words = lax.all_to_all(words, HOME, 0, 0, tiled=True)  5.95 us
    all_to_all x1, starting transfers between devices, body(): lax.all_to_all(total.astype(jnp.bfloat16).reshape(32, BAGS, 256), TABLES,...  5.9 us
    ppermute x4, starting transfers between devices, turned(): lax.ppermute(block, axis, [(i, (i + shift) % count) for i in range(count)])  5 us
    squeeze x64, local copies, waits for them, and re-layouts, body(): pairs = jnp.concatenate([products[:, f, f + 1:] for f in range(64)], 1)  4.78 us
  transfers between devices with their start and end apart: 6, of which 5 were waited for; matrix products, arithmetic and copies ran while one was open for 7% of the time, Pallas kernels for 0%

profile of v2, /device:TPU:32, one launch (start us, length us, event | category | flops | bytes accessed | tf_op | source)
XLA Modules:
  0.0 93.8 jit_solution(7806398120938510954)
XLA Ops:
  0.6 1.0 %or_bitcast_fusion = s32[32,8,16]{0,1,2:T(8,128)S(1)} fusion(s32[16,32,8]{1,2,0:T(8,128)} %param.22, s32[16,32,8]{1,2,0:T(8,128)} %param.20, s32[16,32]{1,0:T(8,128)} %param.23, s32[16,32]{1,0:T(8,128)} %param.21), kind=kLoop, calls=%fused_computation.23 | loop fusion | flops 24576 | bytes 53248 | tf_op jit(solution)/shard_map/transpose | solution.py:230
  1.8 0.7 broadcast_in_dim.20
  2.5 14.4 %all-to-all-start = ((s32[256,1,128]{2,1,0:T(1,128)}), s32[256,1,128]{2,1,0:T(1,128)S(1)}, u32[]{:S(2)}, u32[]{:S(2)}) async-start(s32[256,1,128]{2,1,0:T(1,128)} %bitcast.5), calls=%async_computation | async-start | bytes 262144 | tf_op jit(solution)/shard_map/all_to_all | solution.py:232
  16.9 0.6 pad_add_fusion.place_ref
  17.5 2.9 %convolution_bitcast_fusion.wide_ref = f32[4096,128]{1,0:T(8,128)} fusion(bf16[4096,256]{1,0:T(8,128)(2,1)S(1)} %copy-done, bf16[32,256,128]{2,1,0:T(8,128)(2,1)} %param.24, s32[]{:T(128)S(6)} %select_n.15), kind=kOutput, calls=%fused_computation | convolution fusion | flops 268435456 | bytes 4259844 | tf_op jit(solution)/shard_map/dot_general | solution.py:236
  20.4 2.6 %convolution_bitcast_fusion.1.narrow_ref = f32[4096,128]{1,0:T(8,128)} fusion(bf16[4096,64]{0,1:T(8,128)(2,1)S(1)} %copy-done.2, bf16[32,64,128]{2,1,0:T(8,128)(2,1)} %param.25, s32[]{:T(128)S(6)} %select_n.15), kind=kOutput, calls=%fused_computation.1 | convolution fusion | flops 67108864 | bytes 2637828 | tf_op jit(solution)/shard_map/dot_general | solution.py:237
  23.0 5.9 %all-to-all-done = s32[256,1,128]{2,1,0:T(1,128)S(1)} async-done(((s32[256,1,128]{2,1,0:T(1,128)}), s32[256,1,128]{2,1,0:T(1,128)S(1)}, u32[]{:S(2)}, u32[]{:S(2)}) %all-to-all-start) | async-done | bytes 131104 | tf_op jit(solution)/shard_map/all_to_all | solution.py:232
  28.9 0.7 copy-done.1
  29.6 15.7 %shard_map.149 = (bf16[2048,256]{1,0:T(8,128)(2,1)}, bf16[2048,256]{1,0:T(8,128)(2,1)}) custom-call(s32[2]{0:T(128)} %pad_add_fusion.place_ref, s32[256,128]{1,0:T(8,128)} %bitcast.160, f32[4096,128]{1,0:T(8,128)} %convolution_bitcast_fusion.wide_ref, f32[4096,128]{1,0:T(8,128)} %convolution_bitcast_fusion.1.narrow_ref), custom_call_target="tpu_custom_call" | custom-call | tf_op jit(solution)/shard_map/pallas_call | solution.py:169
  45.3 0.6 collective-permute-start
  45.8 2.5 %collective-permute-done = bf16[2048,256]{1,0:T(8,128)(2,1)S(1)} collective-permute-done((bf16[2048,256]{1,0:T(8,128)(2,1)}, bf16[2048,256]{1,0:T(8,128)(2,1)S(1)}, u32[]{:S(2)}, u32[]{:S(2)}) %collective-permute-start) | collective-permute-done | bytes 1048608 | tf_op jit(solution)/shard_map/ppermute | solution.py:202
  48.3 1.5 %add_convert_fusion = bf16[2048,256]{1,0:T(8,128)(2,1)S(1)} fusion(bf16[2048,256]{1,0:T(8,128)(2,1)S(1)} %collective-permute-done, bf16[2048,256]{1,0:T(8,128)(2,1)} %get-tuple-element.4), kind=kLoop, calls=%fused_computation.2 | loop fusion | flops 2097152 | bytes 3145728 | tf_op jit(solution)/shard_map/convert_element_type | solution.py:241
  50.0 0.5 collective-permute-start.1
  50.5 2.7 %collective-permute-start.2 = (bf16[512,256]{1,0:T(8,128)(2,1)S(1)}, bf16[512,256]{1,0:T(8,128)(2,1)S(1)}, u32[]{:S(2)}, u32[]{:S(2)}) collective-permute-start(bf16[512,256]{1,0:T(8,128)(2,1)S(1)} %get-tuple-element.8), channel_id=1, source_target_pairs={{0,4},{2,6},{4,0},{6,2},{1,5},{3,7},{5,1},{7,3},{8,12},{10,14},{12... | collective-permute-start | bytes 786440 | tf_op jit(solution)/shard_map/ppermute | solution.py:202
  53.2 1.2 %collective-permute-start.3 = (bf16[512,256]{1,0:T(8,128)(2,1)S(1)}, bf16[512,256]{1,0:T(8,128)(2,1)S(1)}, u32[]{:S(2)}, u32[]{:S(2)}) collective-permute-start(bf16[512,256]{1,0:T(8,128)(2,1)S(1)} %get-tuple-element.7), channel_id=1, source_target_pairs={{0,6},{2,0},{4,2},{6,4},{1,7},{3,1},{5,3},{7,5},{8,14},{10,8},{12,... | collective-permute-start | bytes 786440 | tf_op jit(solution)/shard_map/ppermute | solution.py:202
  54.4 11.1 %collective-permute-done.1 = bf16[512,256]{1,0:T(8,128)(2,1)S(1)} collective-permute-done((bf16[512,256]{1,0:T(8,128)(2,1)S(1)}, bf16[512,256]{1,0:T(8,128)(2,1)S(1)}, u32[]{:S(2)}, u32[]{:S(2)}) %collective-permute-start.1) | collective-permute-done | bytes 262176 | tf_op jit(solution)/shard_map/ppermute | solution.py:202
  65.5 0.6 collective-permute-done.3
  66.1 0.8 add_convert_fusion.1
  66.9 5.9 %all-to-all-start.1 = ((bf16[32,16,256]{2,1,0:T(8,128)(2,1)}), bf16[32,16,256]{2,1,0:T(8,128)(2,1)S(1)}, u32[]{:S(2)}, u32[]{:S(2)}) async-start(bf16[32,16,256]{2,1,0:T(8,128)(2,1)} %bitcast.11), calls=%async_computation.1 | async-start | bytes 524288 | tf_op jit(solution)/shard_map/all_to_all | solution.py:246
  72.9 0.2 fusion.4
  73.1 0.1 fusion.5
  73.3 11.3 %all-to-all-done.1 = bf16[32,16,256]{2,1,0:T(8,128)(2,1)S(1)} async-done(((bf16[32,16,256]{2,1,0:T(8,128)(2,1)}), bf16[32,16,256]{2,1,0:T(8,128)(2,1)S(1)}, u32[]{:S(2)}, u32[]{:S(2)}) %all-to-all-start.1) | async-done | bytes 262176 | tf_op jit(solution)/shard_map/all_to_all | solution.py:246
  84.8 0.3 fusion.6
  85.1 0.1 slice_bitcast_fusion
  85.2 0.1 slice_bitcast_fusion.1
  85.3 0.1 slice_bitcast_fusion.10
  85.4 0.1 slice_bitcast_fusion.11
  85.4 0.1 slice_bitcast_fusion.12
  85.6 0.1 slice_bitcast_fusion.14
  85.7 0.1 slice_bitcast_fusion.15
  85.7 0.1 slice_bitcast_fusion.16
  85.8 0.1 slice_bitcast_fusion.17
  85.9 0.1 slice_bitcast_fusion.18
  86.0 0.1 slice_bitcast_fusion.19
  86.1 0.1 slice_bitcast_fusion.20
  86.2 0.1 slice_bitcast_fusion.21
  86.3 0.1 slice_bitcast_fusion.22
  86.3 0.1 slice_bitcast_fusion.23
  86.4 0.1 slice_bitcast_fusion.24
  86.6 0.1 slice_bitcast_fusion.26
  86.6 0.1 slice_bitcast_fusion.27
  86.7 0.1 slice_bitcast_fusion.28
  86.8 0.1 slice_bitcast_fusion.29
  86.9 0.1 slice_bitcast_fusion.3
  87.0 0.1 slice_bitcast_fusion.31
  89.9 0.2 concatenate.8
  90.1 3.0 %fusion = bf16[16,1024]{1,0:T(8,128)(2,1)S(1)} fusion(bf16[16,2208]{1,0:T(8,128)(2,1)S(1)} %concatenate.8, bf16[2208,1024]{1,0:T(8,128)(2,1)} %param.26), kind=kOutput, calls=%fused_computation.4 | convolution fusion | flops 72384512 | bytes 4625408 | tf_op jit(solution)/shard_map/dot_general | solution.py:196
  93.1 0.6 convolution_bitcast_fusion.2
  (69 shorter events, 3.5 us)
Async XLA Ops:
  0.6 16.8 %copy-start = (bf16[4096,256]{1,0:T(8,128)(2,1)S(1)}, bf16[4096,256]{1,0:T(8,128)(2,1)}, u32[]{:S(2)}) copy-start(bf16[4096,256]{1,0:T(8,128)(2,1)} %param.18) | copy-start | bytes 6291460
  2.5 26.4 %all-to-all-start = ((s32[256,1,128]{2,1,0:T(1,128)}), s32[256,1,128]{2,1,0:T(1,128)S(1)}, u32[]{:S(2)}, u32[]{:S(2)}) async-start(s32[256,1,128]{2,1,0:T(1,128)} %bitcast.5), calls=%async_computation | async-start | bytes 262144 | tf_op jit(solution)/shard_map/all_to_all | solution.py:232
  17.5 2.9 %copy-start.2 = (bf16[4096,64]{0,1:T(8,128)(2,1)S(1)}, bf16[4096,64]{0,1:T(8,128)(2,1)}, u32[]{:S(2)}) copy-start(bf16[4096,64]{0,1:T(8,128)(2,1)} %param.19) | copy-start | bytes 1572868
  28.9 0.7 copy-start.1
  45.3 3.1 %collective-permute-start = (bf16[2048,256]{1,0:T(8,128)(2,1)}, bf16[2048,256]{1,0:T(8,128)(2,1)S(1)}, u32[]{:S(2)}, u32[]{:S(2)}) collective-permute-start(bf16[2048,256]{1,0:T(8,128)(2,1)} %get-tuple-element.5), channel_id=1, source_target_pairs={{0,1},{1,0},{2,3},{3,2},{4,5},{5,4},{6,7},{7,6},{8,9},{9,8},{10,11... | collective-permute-start | bytes 3145736 | tf_op jit(solution)/shard_map/ppermute | solution.py:202
  49.9 23.0 %copy-start.3 = (bf16[512,256]{1,0:T(8,128)(2,1)S(1)}, bf16[512,256]{1,0:T(8,128)(2,1)}, u32[]{:S(2)}) copy-start(bf16[512,256]{1,0:T(8,128)(2,1)} %param.16) | copy-start | bytes 786436
  49.9 23.0 %copy-start.6 = (bf16[13,512]{1,0:T(8,128)(2,1)S(1)}, bf16[13,512]{1,0:T(8,128)(2,1)}, u32[]{:S(2)}) copy-start(bf16[13,512]{1,0:T(8,128)(2,1)} %param.15) | copy-start | bytes 39940
  49.9 23.0 %copy-start.7 = (bf16[16,13]{1,0:T(8,128)(2,1)S(1)}, bf16[16,13]{1,0:T(8,128)(2,1)}, u32[]{:S(2)}) copy-start(bf16[16,13]{1,0:T(8,128)(2,1)} %param.14) | copy-start | bytes 1252
  49.9 23.2 %copy-start.4 = (bf16[256,128]{1,0:T(8,128)(2,1)S(1)}, bf16[256,128]{1,0:T(8,128)(2,1)}, u32[]{:S(2)}) copy-start(bf16[256,128]{1,0:T(8,128)(2,1)} %param.17) | copy-start | bytes 196612
  49.9 23.4 %copy-start.8 = (bf16[1024]{0:T(1024)(128)(2,1)S(1)}, bf16[1024]{0:T(1024)(128)(2,1)}, u32[]{:S(2)}) copy-start(bf16[1024]{0:T(1024)(128)(2,1)} %param.27) | copy-start | bytes 6148
  50.0 15.5 %collective-permute-start.1 = (bf16[512,256]{1,0:T(8,128)(2,1)S(1)}, bf16[512,256]{1,0:T(8,128)(2,1)S(1)}, u32[]{:S(2)}, u32[]{:S(2)}) collective-permute-start(bf16[512,256]{1,0:T(8,128)(2,1)S(1)} %get-tuple-element.6), channel_id=1, source_target_pairs={{0,2},{2,4},{4,6},{6,0},{1,3},{3,5},{5,7},{7,1},{8,10},{10,12},{12... | collective-permute-start | bytes 786440 | tf_op jit(solution)/shard_map/ppermute | solution.py:202
  50.5 15.0 %collective-permute-start.2 = (bf16[512,256]{1,0:T(8,128)(2,1)S(1)}, bf16[512,256]{1,0:T(8,128)(2,1)S(1)}, u32[]{:S(2)}, u32[]{:S(2)}) collective-permute-start(bf16[512,256]{1,0:T(8,128)(2,1)S(1)} %get-tuple-element.8), channel_id=1, source_target_pairs={{0,4},{2,6},{4,0},{6,2},{1,5},{3,7},{5,1},{7,3},{8,12},{10,14},{12... | collective-permute-start | bytes 786440 | tf_op jit(solution)/shard_map/ppermute | solution.py:202
  53.2 12.9 %collective-permute-start.3 = (bf16[512,256]{1,0:T(8,128)(2,1)S(1)}, bf16[512,256]{1,0:T(8,128)(2,1)S(1)}, u32[]{:S(2)}, u32[]{:S(2)}) collective-permute-start(bf16[512,256]{1,0:T(8,128)(2,1)S(1)} %get-tuple-element.7), channel_id=1, source_target_pairs={{0,6},{2,0},{4,2},{6,4},{1,7},{3,1},{5,3},{7,5},{8,14},{10,8},{12,... | collective-permute-start | bytes 786440 | tf_op jit(solution)/shard_map/ppermute | solution.py:202
  66.9 17.7 %all-to-all-start.1 = ((bf16[32,16,256]{2,1,0:T(8,128)(2,1)}), bf16[32,16,256]{2,1,0:T(8,128)(2,1)S(1)}, u32[]{:S(2)}, u32[]{:S(2)}) async-start(bf16[32,16,256]{2,1,0:T(8,128)(2,1)} %bitcast.11), calls=%async_computation.1 | async-start | bytes 524288 | tf_op jit(solution)/shard_map/all_to_all | solution.py:246
  93.1 0.6 copy-start.5

commit v3 on v2

--- a/solution.py
+++ b/solution.py
@@ -11,6 +11,10 @@
 LANES = 128
 ROWS = 4096
 SOURCES = 256
+FEATURES = 65
+PITCH = 72
+INTER = 2208
+VMEM = pl.BlockSpec(memory_space=pltpu.VMEM)
 
 
 def drawn_left(packed, field, unit, bits):
@@ -188,6 +192,55 @@
     )(place, words, wide, narrow)
 
 
+def top_kernel(bottom_ref, home_ref, first_ref, last_ref, hidden_ref, logits_ref, stack, grams, joined):
+    bottom = bottom_ref[...].astype(jnp.float32)
+    stack[:, 0:1, :] = bottom[:, None, :]
+    for table in range(32):
+        both = home_ref[table].astype(jnp.float32)
+        stack[:, 1 + table : 2 + table, :] = both[:, None, :LANES]
+        stack[:, 33 + table : 34 + table, :] = both[:, None, LANES:]
+    stack[:, FEATURES:, :] = jnp.zeros((BAGS, PITCH - FEATURES, LANES), jnp.float32)
+    for bag in range(BAGS):
+        features = stack[bag].astype(jnp.bfloat16)
+        grams[bag * PITCH : (bag + 1) * PITCH, 0:PITCH] = lax.dot_general(
+            features, features, (((1,), (1,)), ((), ())), preferred_element_type=jnp.float32
+        )
+    joined[:, 0:LANES] = bottom
+    at = LANES
+    for f in range(FEATURES - 1):
+        count = FEATURES - 1 - f
+        line = grams[pl.ds(f, BAGS, stride=PITCH), :]
+        joined[:, at : at + count] = line[:, f + 1 : FEATURES]
+        at += count
+    hidden = jnp.dot(
+        joined[...].astype(jnp.bfloat16), first_ref[...], preferred_element_type=jnp.float32
+    )
+    hidden = jnp.maximum(hidden, 0.0).astype(jnp.bfloat16)
+    hidden_ref[...] = hidden
+    logits_ref[...] = jnp.sum(
+        hidden.astype(jnp.float32) * last_ref[...].astype(jnp.float32), axis=1, keepdims=True
+    )
+
+
+def top(bottom, home, top_first, top_last):
+    return pl.pallas_call(
+        top_kernel,
+        out_shape=(
+            jax.ShapeDtypeStruct((BAGS, 1024), jnp.bfloat16),
+            jax.ShapeDtypeStruct((BAGS, 1), jnp.float32),
+        ),
+        in_specs=[VMEM] * 4,
+        out_specs=(VMEM, VMEM),
+        scratch_shapes=[
+            pltpu.VMEM((BAGS, PITCH, LANES), jnp.float32),
+            pltpu.VMEM((BAGS * PITCH, LANES), jnp.float32),
+            pltpu.VMEM((BAGS, INTER), jnp.float32),
+        ],
+        compiler_params=pltpu.CompilerParams(vmem_limit_bytes=16 * 1024 * 1024),
+        name="top",
+    )(bottom, home, top_first, top_last.reshape(1, 1024))
+
+
 HOME = ("y", "z", "x", "row")
 TABLES = ("y", "z")
 
@@ -250,13 +303,8 @@
     bottom = dense_layer(
         dense_layer(dense_layer(dense_input, bottom_first), bottom_second), bottom_third
     )
-    features = jnp.concatenate([bottom[None], home[:, :, :LANES], home[:, :, LANES:]], 0)
-    products = jnp.einsum("fbe,gbe->bfg", features, features, preferred_element_type=jnp.float32)
-    pairs = jnp.concatenate([products[:, f, f + 1 :] for f in range(64)], 1)
-    joined = jnp.concatenate([bottom.astype(jnp.float32), pairs], 1).astype(jnp.bfloat16)
-    hidden = dense_layer(joined, top_first)
-    logits = jnp.dot(hidden, top_last, preferred_element_type=jnp.float32)
-    return (hidden, logits)
+    hidden, logits = top(bottom, home, top_first, top_last)
+    return (hidden, logits.reshape(BAGS))
 
 
 def solution(mesh):

time: 95 us -> 91.5 us (0.963)
  matrix products: 9.81 us -> 5.88 us
  Pallas kernels: 15.7 us -> 18.8 us
  local copies, waits for them, and re-layouts: 6.65 us -> 3.78 us
    squeeze x64 -> x0, local copies, waits for them, and re-layouts: 4.78 us -> none  [body(): pairs = jnp.concatenate([products[:, f, f + 1:] for f in range(64)], 1)]
    dot_general x3 -> x2, matrix products: 3.35 us -> 0.37 us  [dense_layer(): jnp.dot(values, weight, preferred_element_type=jnp.float32)]
    unnamed x21 -> x18, local copies, waits for them, and re-layouts: 0.78 us -> 2.97 us
    pallas_call x0 -> x1, Pallas kernels: none -> 2.11 us  [top(): pl.pallas_call(top_kernel, out_shape=(jax.ShapeDtypeStruct((BAGS, 1024),...]
    dot_general x2 -> x0, matrix products: 0.96 us -> none  [the longest x1 0.64 us: body(): logits = jnp.dot(hidden, top_last, preferred_element_type=jnp.float32)]
    pallas_call x1, Pallas kernels: 15.7 us -> 16.6 us  [pool(): pl.pallas_call(pool_kernel, out_shape=(half, half), in_specs=[pl.BlockSpe...]
  transfers between devices with their start and end apart: 6 -> 6, of which waited for: 5 -> 6; matrix products, arithmetic and copies ran while one was open for 7% -> 7% of each run, Pallas kernels for 0% -> 0%
where the time goes in v3:
time: 91.5 us; the launch traced here: 90.6 us
  waiting for transfers between devices  31 us (34%)
  starting transfers between devices  25.7 us (28%)
  Pallas kernels  18.8 us (21%)
  matrix products  5.88 us (6%)
  other arithmetic  4.69 us (5%)
  local copies, waits for them, and re-layouts  3.78 us (4%)
    pallas_call x1, Pallas kernels, pool(): pl.pallas_call(pool_kernel, out_shape=(half, half), in_specs=[pl.BlockSpe...  16.6 us
    all_to_all x1, starting transfers between devices, body(): words = lax.all_to_all(words, HOME, 0, 0, tiled=True)  14.4 us
    ppermute x4, waiting for transfers between devices, turned(): lax.ppermute(block, axis, [(i, (i + shift) % count) for i in range(count)])  13.9 us
    all_to_all x1, waiting for transfers between devices, body(): lax.all_to_all(total.astype(jnp.bfloat16).reshape(32, BAGS, 256), TABLES,...  11.3 us
    all_to_all x1, starting transfers between devices, body(): lax.all_to_all(total.astype(jnp.bfloat16).reshape(32, BAGS, 256), TABLES,...  6.2 us
    all_to_all x1, waiting for transfers between devices, body(): words = lax.all_to_all(words, HOME, 0, 0, tiled=True)  5.85 us
    ppermute x4, starting transfers between devices, turned(): lax.ppermute(block, axis, [(i, (i + shift) % count) for i in range(count)])  5.13 us
    unnamed x18, local copies, waits for them, and re-layouts  2.97 us
  transfers between devices with their start and end apart: 6, of which 6 were waited for; matrix products, arithmetic and copies ran while one was open for 7% of the time, Pallas kernels for 0%

profile of v3, /device:TPU:32, one launch (start us, length us, event | category | flops | bytes accessed | tf_op | source)
XLA Modules:
  0.0 90.6 jit_solution(14945298680188699098)
XLA Ops:
  0.6 0.0 copy-start
  0.6 1.0 %or_bitcast_fusion = s32[32,8,16]{0,1,2:T(8,128)S(1)} fusion(s32[16,32,8]{1,2,0:T(8,128)} %param.22, s32[16,32,8]{1,2,0:T(8,128)} %param.20, s32[16,32]{1,0:T(8,128)} %param.23, s32[16,32]{1,0:T(8,128)} %param.21), kind=kLoop, calls=%fused_computation.13 | loop fusion | flops 24576 | bytes 53248 | tf_op jit(solution)/shard_map/transpose | solution.py:283
  1.7 0.1 copy.23
  1.8 0.7 broadcast_in_dim.16
  2.5 14.4 %all-to-all-start = ((s32[256,1,128]{2,1,0:T(1,128)}), s32[256,1,128]{2,1,0:T(1,128)S(1)}, u32[]{:S(2)}, u32[]{:S(2)}) async-start(s32[256,1,128]{2,1,0:T(1,128)} %bitcast.4), calls=%async_computation | async-start | bytes 262144 | tf_op jit(solution)/shard_map/all_to_all | solution.py:285
  16.9 0.6 pad_add_fusion.place_ref
  17.5 0.0 copy-done
  17.5 0.0 copy-start.3
  17.5 2.9 %convolution_bitcast_fusion.wide_ref = f32[4096,128]{1,0:T(8,128)} fusion(bf16[4096,256]{1,0:T(8,128)(2,1)S(1)} %copy-done, bf16[32,256,128]{2,1,0:T(8,128)(2,1)} %param.24, s32[]{:T(128)S(6)} %select_n.15), kind=kOutput, calls=%fused_computation | convolution fusion | flops 268435456 | bytes 4259844 | tf_op jit(solution)/shard_map/dot_general | solution.py:289
  20.4 0.0 copy-done.3
  20.4 2.6 %convolution_bitcast_fusion.1.narrow_ref = f32[4096,128]{1,0:T(8,128)} fusion(bf16[4096,64]{0,1:T(8,128)(2,1)S(1)} %copy-done.3, bf16[32,64,128]{2,1,0:T(8,128)(2,1)} %param.25, s32[]{:T(128)S(6)} %select_n.15), kind=kOutput, calls=%fused_computation.1 | convolution fusion | flops 67108864 | bytes 2637828 | tf_op jit(solution)/shard_map/dot_general | solution.py:290
  23.0 5.8 %all-to-all-done = s32[256,1,128]{2,1,0:T(1,128)S(1)} async-done(((s32[256,1,128]{2,1,0:T(1,128)}), s32[256,1,128]{2,1,0:T(1,128)S(1)}, u32[]{:S(2)}, u32[]{:S(2)}) %all-to-all-start) | async-done | bytes 131104 | tf_op jit(solution)/shard_map/all_to_all | solution.py:285
  28.9 0.0 copy-start.2
  28.9 0.6 copy-done.2
  29.5 16.6 %shard_map.149 = (bf16[2048,256]{1,0:T(8,128)(2,1)}, bf16[2048,256]{1,0:T(8,128)(2,1)}) custom-call(s32[2]{0:T(128)} %pad_add_fusion.place_ref, s32[256,128]{1,0:T(8,128)} %bitcast.25, f32[4096,128]{1,0:T(8,128)} %convolution_bitcast_fusion.wide_ref, f32[4096,128]{1,0:T(8,128)} %convolution_bitcast_fusion.1.narrow_ref), custom_call_target="tpu_custom_call" | custom-call | tf_op jit(solution)/shard_map/pallas_call | solution.py:173
  46.2 0.5 collective-permute-start
  46.6 2.5 %collective-permute-done = bf16[2048,256]{1,0:T(8,128)(2,1)S(1)} collective-permute-done((bf16[2048,256]{1,0:T(8,128)(2,1)}, bf16[2048,256]{1,0:T(8,128)(2,1)S(1)}, u32[]{:S(2)}, u32[]{:S(2)}) %collective-permute-start) | collective-permute-done | bytes 1048608 | tf_op jit(solution)/shard_map/ppermute | solution.py:255
  49.1 1.5 %add_convert_fusion = bf16[2048,256]{1,0:T(8,128)(2,1)S(1)} fusion(bf16[2048,256]{1,0:T(8,128)(2,1)S(1)} %collective-permute-done, bf16[2048,256]{1,0:T(8,128)(2,1)} %get-tuple-element.6), kind=kLoop, calls=%fused_computation.2 | loop fusion | flops 2097152 | bytes 3145728 | tf_op jit(solution)/shard_map/convert_element_type | solution.py:294
  50.7 0.0 copy-start.8
  50.7 0.0 copy-start.4
  50.7 0.0 copy-start.6
  50.7 0.0 copy-start.7
  50.7 0.0 copy-start.5
  50.7 0.1 fusion.13
  50.8 0.8 collective-permute-start.1
  51.6 2.6 %collective-permute-start.2 = (bf16[512,256]{1,0:T(8,128)(2,1)S(1)}, bf16[512,256]{1,0:T(8,128)(2,1)S(1)}, u32[]{:S(2)}, u32[]{:S(2)}) collective-permute-start(bf16[512,256]{1,0:T(8,128)(2,1)S(1)} %get-tuple-element.12), channel_id=1, source_target_pairs={{0,4},{2,6},{4,0},{6,2},{1,5},{3,7},{5,1},{7,3},{8,12},{10,14},{12... | collective-permute-start | bytes 786440 | tf_op jit(solution)/shard_map/ppermute | solution.py:255
  54.2 1.2 %collective-permute-start.3 = (bf16[512,256]{1,0:T(8,128)(2,1)S(1)}, bf16[512,256]{1,0:T(8,128)(2,1)S(1)}, u32[]{:S(2)}, u32[]{:S(2)}) collective-permute-start(bf16[512,256]{1,0:T(8,128)(2,1)S(1)} %get-tuple-element.11), channel_id=1, source_target_pairs={{0,6},{2,0},{4,2},{6,4},{1,7},{3,1},{5,3},{7,5},{8,14},{10,8},{12,... | collective-permute-start | bytes 786440 | tf_op jit(solution)/shard_map/ppermute | solution.py:255
  55.5 6.0 %collective-permute-done.1 = bf16[512,256]{1,0:T(8,128)(2,1)S(1)} collective-permute-done((bf16[512,256]{1,0:T(8,128)(2,1)S(1)}, bf16[512,256]{1,0:T(8,128)(2,1)S(1)}, u32[]{:S(2)}, u32[]{:S(2)}) %collective-permute-start.1) | collective-permute-done | bytes 262176 | tf_op jit(solution)/shard_map/ppermute | solution.py:255
  61.5 4.8 %collective-permute-done.2 = bf16[512,256]{1,0:T(8,128)(2,1)S(1)} collective-permute-done((bf16[512,256]{1,0:T(8,128)(2,1)S(1)}, bf16[512,256]{1,0:T(8,128)(2,1)S(1)}, u32[]{:S(2)}, u32[]{:S(2)}) %collective-permute-start.2) | collective-permute-done | bytes 262176 | tf_op jit(solution)/shard_map/ppermute | solution.py:255
  66.3 0.6 collective-permute-done.3
  66.9 0.8 add_convert_fusion.1
  67.7 6.2 %all-to-all-start.1 = ((bf16[32,16,256]{2,1,0:T(8,128)(2,1)}), bf16[32,16,256]{2,1,0:T(8,128)(2,1)S(1)}, u32[]{:S(2)}, u32[]{:S(2)}) async-start(bf16[32,16,256]{2,1,0:T(8,128)(2,1)} %bitcast.10), calls=%async_computation.1 | async-start | bytes 524288 | tf_op jit(solution)/shard_map/all_to_all | solution.py:299
  73.9 0.0 copy-done.8
  74.0 0.0 copy-done.4
  74.0 0.0 copy-done.6
  74.0 0.0 copy-done.7
  74.0 0.2 fusion.3
  74.2 0.0 copy-done.5
  74.2 0.1 fusion.4.bottom_ref
  74.4 11.3 %all-to-all-done.1.home_ref = bf16[32,16,256]{2,1,0:T(8,128)(2,1)S(1)} async-done(((bf16[32,16,256]{2,1,0:T(8,128)(2,1)}), bf16[32,16,256]{2,1,0:T(8,128)(2,1)S(1)}, u32[]{:S(2)}, u32[]{:S(2)}) %all-to-all-start.1) | async-done | bytes 262176 | tf_op jit(solution)/shard_map/all_to_all | solution.py:299
  85.6 0.0 copy-start.1
  85.6 2.3 %copy-done.1 = bf16[2208,1024]{1,0:T(8,128)(2,1)S(1)} copy-done((bf16[2208,1024]{1,0:T(8,128)(2,1)S(1)}, bf16[2208,1024]{1,0:T(8,128)(2,1)}, u32[]{:S(2)}) %copy-start.1) | copy-done | bytes 4522008
  87.9 2.1 %top.1 = (bf16[16,1024]{1,0:T(8,128)(2,1)}, f32[16,1]{1,0:T(8,128)S(1)}) custom-call(bf16[16,128]{1,0:T(8,128)(2,1)S(1)} %fusion.4.bottom_ref, bf16[32,16,256]{2,1,0:T(8,128)(2,1)S(1)} %all-to-all-done.1.home_ref, bf16[2208,1024]{1,0:T(8,128)(2,1)S(1)} %copy-done.1, bf16[1,1024]{1,0:T(2,128)(2,1)S(1)} %reshape.31.last_ref), custom_call_target="tpu_custom_call" | custom-call | tf_op jit(solution)/shard_map/top/pallas_call | solution.py:226
  90.0 0.6 reduce
  (2 shorter events, 0.0 us)
Async XLA Ops:
  0.6 16.9 %copy-start = (bf16[4096,256]{1,0:T(8,128)(2,1)S(1)}, bf16[4096,256]{1,0:T(8,128)(2,1)}, u32[]{:S(2)}) copy-start(bf16[4096,256]{1,0:T(8,128)(2,1)} %param.18) | copy-start | bytes 6291460
  2.5 26.4 %all-to-all-start = ((s32[256,1,128]{2,1,0:T(1,128)}), s32[256,1,128]{2,1,0:T(1,128)S(1)}, u32[]{:S(2)}, u32[]{:S(2)}) async-start(s32[256,1,128]{2,1,0:T(1,128)} %bitcast.4), calls=%async_computation | async-start | bytes 262144 | tf_op jit(solution)/shard_map/all_to_all | solution.py:285
  17.5 3.0 %copy-start.3 = (bf16[4096,64]{0,1:T(8,128)(2,1)S(1)}, bf16[4096,64]{0,1:T(8,128)(2,1)}, u32[]{:S(2)}) copy-start(bf16[4096,64]{0,1:T(8,128)(2,1)} %param.19) | copy-start | bytes 1572868
  28.9 0.6 copy-start.2
  46.2 3.0 %collective-permute-start = (bf16[2048,256]{1,0:T(8,128)(2,1)}, bf16[2048,256]{1,0:T(8,128)(2,1)S(1)}, u32[]{:S(2)}, u32[]{:S(2)}) collective-permute-start(bf16[2048,256]{1,0:T(8,128)(2,1)} %get-tuple-element.7), channel_id=1, source_target_pairs={{0,1},{1,0},{2,3},{3,2},{4,5},{5,4},{6,7},{7,6},{8,9},{9,8},{10,11... | collective-permute-start | bytes 3145736 | tf_op jit(solution)/shard_map/ppermute | solution.py:255
  50.7 23.3 %copy-start.8 = (bf16[1024]{0:T(1024)(128)(2,1)S(1)}, bf16[1024]{0:T(1024)(128)(2,1)}, u32[]{:S(2)}) copy-start(bf16[1024]{0:T(1024)(128)(2,1)} %param.27) | copy-start | bytes 6148
  50.7 23.3 %copy-start.4 = (bf16[512,256]{1,0:T(8,128)(2,1)S(1)}, bf16[512,256]{1,0:T(8,128)(2,1)}, u32[]{:S(2)}) copy-start(bf16[512,256]{1,0:T(8,128)(2,1)} %param.16) | copy-start | bytes 786436
  50.7 23.3 %copy-start.6 = (bf16[13,512]{1,0:T(8,128)(2,1)S(1)}, bf16[13,512]{1,0:T(8,128)(2,1)}, u32[]{:S(2)}) copy-start(bf16[13,512]{1,0:T(8,128)(2,1)} %param.15) | copy-start | bytes 39940
  50.7 23.3 %copy-start.7 = (bf16[16,13]{1,0:T(8,128)(2,1)S(1)}, bf16[16,13]{1,0:T(8,128)(2,1)}, u32[]{:S(2)}) copy-start(bf16[16,13]{1,0:T(8,128)(2,1)} %param.14) | copy-start | bytes 1252
  50.7 23.5 %copy-start.5 = (bf16[256,128]{1,0:T(8,128)(2,1)S(1)}, bf16[256,128]{1,0:T(8,128)(2,1)}, u32[]{:S(2)}) copy-start(bf16[256,128]{1,0:T(8,128)(2,1)} %param.17) | copy-start | bytes 196612
  50.8 10.7 %collective-permute-start.1 = (bf16[512,256]{1,0:T(8,128)(2,1)S(1)}, bf16[512,256]{1,0:T(8,128)(2,1)S(1)}, u32[]{:S(2)}, u32[]{:S(2)}) collective-permute-start(bf16[512,256]{1,0:T(8,128)(2,1)S(1)} %get-tuple-element.10), channel_id=1, source_target_pairs={{0,2},{2,4},{4,6},{6,0},{1,3},{3,5},{5,7},{7,1},{8,10},{10,12},{12... | collective-permute-start | bytes 786440 | tf_op jit(solution)/shard_map/ppermute | solution.py:255
  51.6 14.7 %collective-permute-start.2 = (bf16[512,256]{1,0:T(8,128)(2,1)S(1)}, bf16[512,256]{1,0:T(8,128)(2,1)S(1)}, u32[]{:S(2)}, u32[]{:S(2)}) collective-permute-start(bf16[512,256]{1,0:T(8,128)(2,1)S(1)} %get-tuple-element.12), channel_id=1, source_target_pairs={{0,4},{2,6},{4,0},{6,2},{1,5},{3,7},{5,1},{7,3},{8,12},{10,14},{12... | collective-permute-start | bytes 786440 | tf_op jit(solution)/shard_map/ppermute | solution.py:255
  54.2 12.7 %collective-permute-start.3 = (bf16[512,256]{1,0:T(8,128)(2,1)S(1)}, bf16[512,256]{1,0:T(8,128)(2,1)S(1)}, u32[]{:S(2)}, u32[]{:S(2)}) collective-permute-start(bf16[512,256]{1,0:T(8,128)(2,1)S(1)} %get-tuple-element.11), channel_id=1, source_target_pairs={{0,6},{2,0},{4,2},{6,4},{1,7},{3,1},{5,3},{7,5},{8,14},{10,8},{12,... | collective-permute-start | bytes 786440 | tf_op jit(solution)/shard_map/ppermute | solution.py:255
  67.7 17.9 %all-to-all-start.1 = ((bf16[32,16,256]{2,1,0:T(8,128)(2,1)}), bf16[32,16,256]{2,1,0:T(8,128)(2,1)S(1)}, u32[]{:S(2)}, u32[]{:S(2)}) async-start(bf16[32,16,256]{2,1,0:T(8,128)(2,1)} %bitcast.10), calls=%async_computation.1 | async-start | bytes 524288 | tf_op jit(solution)/shard_map/all_to_all | solution.py:299
  85.6 2.3 %copy-start.1 = (bf16[2208,1024]{1,0:T(8,128)(2,1)S(1)}, bf16[2208,1024]{1,0:T(8,128)(2,1)}, u32[]{:S(2)}) copy-start(bf16[2208,1024]{1,0:T(8,128)(2,1)} %first_ref.1) | copy-start | bytes 13565956

commit v4 on v3

v4 whole, which is shorter than its diff:
```python
import jax
import jax.numpy as jnp
from jax import lax
from jax.experimental import pallas as pl
from jax.experimental.pallas import tpu as pltpu
from jax.sharding import Mesh
from jax.sharding import PartitionSpec as P

BAGS = 16
LANES = 128
ROWS = 4096
SOURCES = 256
LINES = 32
BLOCKS = 16
SHIFTS = (1, 3, 2, 0)
FEATURES = 65
PITCH = 72
INTER = 2208
TOP = 1024
LIMIT = pltpu.CompilerParams(vmem_limit_bytes=60 * 1024 * 1024)
VMEM = pl.BlockSpec(memory_space=pltpu.VMEM)
SMEM = pl.BlockSpec(memory_space=pltpu.SMEM)
ANY = pl.BlockSpec(memory_space=pl.ANY)


def drawn_left(packed, field, unit, bits):
    for bit in range(bits):
        moved = jnp.where((packed & (1 << (field + bit))) != 0, packed, 0)
        packed = packed - moved + pltpu.roll(moved, LANES - (unit << bit), 1)
    return packed


def as_matrix(flags):
    return jnp.where(flags, 1.0, 0.0).astype(jnp.bfloat16)


def counted(flags, before):
    return jnp.dot(as_matrix(flags), before, preferred_element_type=jnp.float32).astype(jnp.int32)


def prepared(place_ref, words_ref, firsts_ref, more_v, lists_ref):
    my_x = place_ref[0]
    my_row = place_ref[1]
    shard = my_x * 2 + my_row
    at = lax.broadcasted_iota(jnp.int32, (LANES, LANES), 0)
    to = lax.broadcasted_iota(jnp.int32, (LANES, LANES), 1)
    same_bag = as_matrix(((at & 15) == (to & 15)) & (at < to))
    any_bag = as_matrix(at < to)
    lane = lax.broadcasted_iota(jnp.int32, (SOURCES, LANES), 1)
    target = lax.broadcasted_iota(jnp.int32, (SOURCES, LANES), 0) * BAGS + (lane & 15)
    parts = []
    for shift in SHIFTS:
        for row in (0, 1):
            start = ((my_x + shift) & 3) * 2 + (my_row ^ row)
            parts.append(words_ref[pl.ds(start, 32, stride=8), :])
    words = jnp.concatenate(parts, 0)
    most = jnp.int32(0)
    picks = []
    for kind, value in enumerate((words & 65535, (words >> 16) & 65535)):
        local = (value >> 12) == shard
        gap = (lane >> 4) - counted(local, same_bag)
        packed = jnp.where(local, (value & 4095) | (gap << 12) | (1 << 15), 0)
        packed = drawn_left(packed, 12, BAGS, 3)
        picks.append(jnp.where(packed != 0, packed & 4095, ROWS))
        more = (packed != 0) & (lane >= BAGS)
        before = counted(more, any_bag)
        most = jnp.maximum(most, jnp.max(before + more.astype(jnp.int32)))
        extra = (packed & 4095) | (target << 12) | ((lane - before) << 24) | jnp.int32(-(2**31))
        extra = drawn_left(jnp.where(more, extra, 0), 24, 1, 7)
        more_v[kind] = jnp.transpose(extra)
    pair = jnp.where(lane < BAGS, picks[0] | (picks[1] << 16), 0)
    for part in range(4):
        line = pair[part * 64 : part * 64 + 8]
        for j in range(1, 8):
            low = part * 64 + j * 8
            line = line + pltpu.roll(pair[low : low + 8], j * BAGS, 1)
        firsts_ref[part * 8 : (part + 1) * 8] = line
    lane = lax.broadcasted_iota(jnp.int32, (LINES, LANES), 1)

    def one_block(block, _):
        rows = pl.ds(pl.multiple_of(block * 8, 8), 8)
        held = jnp.concatenate(
            [
                more_v[kind, rows, half * LANES : (half + 1) * LANES]
                for kind in (0, 1)
                for half in (0, 1)
            ],
            0,
        )
        used = held < 0
        before = counted(used, any_bag)
        ones = used.astype(jnp.int32)
        total = jnp.sum(ones, axis=1, keepdims=True)
        part = jnp.sum(jnp.where(lane < 64, ones, 0), axis=1, keepdims=True)
        packed = jnp.where(used, (held & 0xFFFFFF) | ((lane - before) << 24), 0)
        packed = drawn_left(packed, 24, 1, 7) & 0xFFFFFF
        counts = jnp.where(lane == 0, total, 0) + jnp.where(lane == 1, part, 0)
        lists_ref[pl.ds(pl.multiple_of(block * LINES, LINES), LINES), :] = packed | (counts << 24)
        return 0

    blocks = jnp.maximum((most + 7) >> 3, 1)
    lax.fori_loop(0, blocks, one_block, 0)
    return blocks


def pooled(first_part, parts, blocks, first_line, firsts, lists_ref, lists, wide_rows, narrow_rows,
           wide_sum, narrow_sum, keep_ref, send_ref, sem):
    low_row = first_part * 1024
    spans = ((0, 0), (1, 1)) if parts == 3 else ((1, 2),)

    def block_copy(block):
        rows = pl.ds(pl.multiple_of(block * LINES, LINES), LINES)
        return pltpu.make_async_copy(lists_ref.at[rows], lists, sem)

    block_copy(0).start()

    def one_group(group, _):
        for part in range(parts):
            for j in range(8):
                base = pl.multiple_of(part * 1024 + j * 128 + group * BAGS, BAGS)
                for low in range(0, BAGS, 8):
                    bags = range(low, low + 8)
                    both = [firsts[first_line + part * 8 + group, j * BAGS + bag] for bag in bags]
                    wide = [wide_rows[pl.ds(pair & 65535, 1), :] for pair in both]
                    narrow = [narrow_rows[pl.ds(pair >> 16, 1), :] for pair in both]
                    for bag, row in zip(bags, wide):
                        wide_sum[pl.ds(base + bag, 1), :] = row
                    for bag, row in zip(bags, narrow):
                        narrow_sum[pl.ds(base + bag, 1), :] = row
        return 0

    lax.fori_loop(0, 8, one_group, 0)

    def one_block(block, _):
        @pl.when(block > 0)
        def _():
            block_copy(block).start()

        block_copy(block).wait()

        for kind, rows, sums in ((0, wide_rows, wide_sum), (1, narrow_rows, narrow_sum)):

            def some(k, low, count):
                entries = [lists[k, low + i] for i in range(count)]
                places = [pl.ds(((entry >> 12) & 4095) - low_row, 1) for entry in entries]
                values = [
                    sums[place, :] + rows[pl.ds(entry & 4095, 1), :]
                    for entry, place in zip(entries, places)
                ]
                for place, value in zip(places, values):
                    sums[place, :] = value

            for half, span in spans:

                def one_list(k, _, span=span):
                    low, high = 0, lax.shift_right_logical(lists[k, 0], 24)
                    if span:
                        middle = lax.shift_right_logical(lists[k, 1], 24)
                        low, high = (low, middle) if span == 1 else (middle, high)

                    def four(i, _):
                        some(k, low + i * 4, 4)
                        return 0

                    def one(i, _):
                        some(k, i, 1)
                        return 0

                    fours = (high - low) >> 2
                    lax.fori_loop(0, fours, four, 0)
                    lax.fori_loop(low + fours * 4, high, one, 0)
                    return 0

                start = kind * 16 + half * 8
                lax.fori_loop(start, start + 8, one_list, 0)
        return 0

    lax.fori_loop(0, blocks, one_block, 0)

    for part in range(parts):
        for row, ref in enumerate((keep_ref, send_ref)):

            def one(i, _):
                to = pl.ds(pl.multiple_of(part * 512 + i * 128, 128), 128)
                source = pl.ds(pl.multiple_of(part * 1024 + row * 512 + i * 128, 128), 128)
                ref[to, 0:LANES] = wide_sum[source, :].astype(jnp.bfloat16)
                ref[to, LANES:] = narrow_sum[source, :].astype(jnp.bfloat16)
                return 0

            lax.fori_loop(0, 4, one, 0)


def table_copies(wide_ref, narrow_ref, wide_rows, narrow_rows, sems):
    pairs = ((wide_ref, wide_rows), (narrow_ref, narrow_rows))
    copies = []
    for at, (ref, rows) in enumerate(pairs):
        copies.append(pltpu.make_async_copy(ref, rows.at[pl.ds(0, ROWS)], sems.at[at]))
        copies[-1].start()
        rows[pl.ds(ROWS, 8), :] = jnp.zeros((8, LANES), jnp.float32)
    return copies


def first_kernel(place_ref, words_ref, wide_ref, narrow_ref, keep_ref, send_ref, firsts_ref,
                 lists_ref, blocks_ref, more_v, wide_rows, narrow_rows, wide_sum, narrow_sum,
                 firsts, lists, sems):
    copies = table_copies(wide_ref, narrow_ref, wide_rows, narrow_rows, sems)
    blocks = prepared(place_ref, words_ref, firsts_ref, more_v, lists_ref)
    blocks_ref[0] = blocks
    copies.append(pltpu.make_async_copy(firsts_ref, firsts, sems.at[2]))
    copies[-1].start()
    for copy in copies:
        copy.wait()
    pooled(0, 3, blocks, 0, firsts, lists_ref, lists, wide_rows, narrow_rows, wide_sum, narrow_sum,
           keep_ref, send_ref, sems.at[3])


def last_kernel(blocks_ref, firsts_ref, lists_ref, wide_ref, narrow_ref, keep_ref, send_ref,
                wide_rows, narrow_rows, wide_sum, narrow_sum, lists, sems):
    copies = table_copies(wide_ref, narrow_ref, wide_rows, narrow_rows, sems)
    for copy in copies:
        copy.wait()
    pooled(3, 1, blocks_ref[0], 24, firsts_ref, lists_ref, lists, wide_rows, narrow_rows, wide_sum,
           narrow_sum, keep_ref, send_ref, sems.at[2])


def shapes(parts):
    half = jax.ShapeDtypeStruct((parts * 512, 2 * LANES), jnp.bfloat16)
    rows = pltpu.VMEM((ROWS + 8, LANES), jnp.float32)
    sums = pltpu.VMEM((parts * 1024, LANES), jnp.float32)
    cost = pl.CostEstimate(flops=10**6, bytes_accessed=10**7, transcendentals=0)
    return half, [rows, rows, sums, sums], cost


def pool_first(place, words, wide, narrow):
    half, buffers, cost = shapes(3)
    return pl.pallas_call(
        first_kernel,
        out_shape=(
            half,
            half,
            jax.ShapeDtypeStruct((32, LANES), jnp.int32),
            jax.ShapeDtypeStruct((BLOCKS * LINES, LANES), jnp.int32),
            jax.ShapeDtypeStruct((1,), jnp.int32),
        ),
        in_specs=[SMEM, VMEM, ANY, ANY],
        out_specs=(VMEM, VMEM, VMEM, VMEM, SMEM),
        scratch_shapes=[pltpu.VMEM((2, LANES, SOURCES), jnp.int32)]
        + buffers
        + [
            pltpu.SMEM((LINES, LANES), jnp.int32),
            pltpu.SMEM((LINES, LANES), jnp.int32),
            pltpu.SemaphoreType.DMA((4,)),
        ],
        compiler_params=LIMIT,
        cost_estimate=cost,
        name="pool_first",
    )(place, words, wide, narrow)


def pool_last(blocks, firsts, lists, wide, narrow):
    half, buffers, cost = shapes(1)
    return pl.pallas_call(
        last_kernel,
        out_shape=(half, half),
        in_specs=[SMEM, SMEM, ANY, ANY, ANY],
        out_specs=(VMEM, VMEM),
        scratch_shapes=buffers
        + [pltpu.SMEM((LINES, LANES), jnp.int32), pltpu.SemaphoreType.DMA((3,))],
        compiler_params=LIMIT,
        cost_estimate=cost,
        name="pool_last",
    )(blocks, firsts, lists, wide, narrow)


def top_kernel(bottom_ref, home_ref, first_ref, last_ref, hidden_ref, logits_ref, stack, grams, joined):
    bottom = bottom_ref[...].astype(jnp.float32)
    stack[:, 0:1, :] = bottom[:, None, :]
    for table in range(32):
        both = home_ref[table].astype(jnp.float32)
        stack[:, 1 + table : 2 + table, :] = both[:, None, :LANES]
        stack[:, 33 + table : 34 + table, :] = both[:, None, LANES:]
    stack[:, FEATURES:, :] = jnp.zeros((BAGS, PITCH - FEATURES, LANES), jnp.float32)
    for bag in range(BAGS):
        features = stack[bag].astype(jnp.bfloat16)
        grams[bag * PITCH : (bag + 1) * PITCH, 0:PITCH] = lax.dot_general(
            features, features, (((1,), (1,)), ((), ())), preferred_element_type=jnp.float32
        )
    joined[:, 0:LANES] = bottom
    at = LANES
    for f in range(FEATURES - 1):
        count = FEATURES - 1 - f
        line = grams[pl.ds(f, BAGS, stride=PITCH), :]
        joined[:, at : at + count] = line[:, f + 1 : FEATURES]
        at += count
    hidden = jnp.dot(
        joined[...].astype(jnp.bfloat16), first_ref[...], preferred_element_type=jnp.float32
    )
    hidden = jnp.maximum(hidden, 0.0).astype(jnp.bfloat16)
    hidden_ref[...] = hidden
    logits_ref[...] = lax.dot_general(
        last_ref[...], hidden, (((1,), (1,)), ((), ())), preferred_element_type=jnp.float32
    )


def top(bottom, home, top_first, top_last):
    return pl.pallas_call(
        top_kernel,
        out_shape=(
            jax.ShapeDtypeStruct((BAGS, TOP), jnp.bfloat16),
            jax.ShapeDtypeStruct((1, BAGS), jnp.float32),
        ),
        in_specs=[VMEM] * 4,
        out_specs=(VMEM, VMEM),
        scratch_shapes=[
            pltpu.VMEM((BAGS, PITCH, LANES), jnp.float32),
            pltpu.VMEM((BAGS * PITCH, LANES), jnp.float32),
            pltpu.VMEM((BAGS, INTER), jnp.float32),
        ],
        compiler_params=pltpu.CompilerParams(vmem_limit_bytes=16 * 1024 * 1024),
        name="top",
    )(bottom, home, top_first, top_last.reshape(1, TOP))


HOME = ("y", "z", "x", "row")
TABLES = ("y", "z")


def dense_layer(values, weight):
    return jnp.maximum(jnp.dot(values, weight, preferred_element_type=jnp.float32), 0.0).astype(
        jnp.bfloat16
    )


def turned(block, axis, count, shift):
    return lax.ppermute(block, axis, [(i, (i + shift) % count) for i in range(count)])


def added(one, other):
    return (one.astype(jnp.float32) + other.astype(jnp.float32)).astype(jnp.bfloat16)


def coded(indices, lengths):
    slots = lax.broadcasted_iota(jnp.int32, indices.shape, 2)
    return jnp.where(slots < lengths[:, :, None], indices, 32768)


def body(
    dense_input,
    bottom_first,
    bottom_second,
    bottom_third,
    wide_tables,
    narrow_tables,
    wide_indices,
    wide_lengths,
    narrow_indices,
    narrow_lengths,
    wide_projection,
    narrow_projection,
    top_first,
    top_last,
):
    own_table = lax.axis_index(TABLES)
    place = jnp.stack([lax.axis_index("x"), lax.axis_index("row")]).astype(jnp.int32)

    words = coded(wide_indices, wide_lengths) | (coded(narrow_indices, narrow_lengths) << 16)
    words = jnp.transpose(words, (1, 2, 0)).reshape(32, 1, LANES)
    words = jnp.broadcast_to(words, (32, 8, LANES)).reshape(256, LANES)
    words = lax.all_to_all(words, HOME, 0, 0, tiled=True)

    wide_weight = lax.dynamic_index_in_dim(wide_projection, own_table, 0, keepdims=False)
    narrow_weight = lax.dynamic_index_in_dim(narrow_projection, own_table, 0, keepdims=False)
    wide_rows = jnp.dot(wide_tables, wide_weight, preferred_element_type=jnp.float32)
    narrow_rows = jnp.dot(narrow_tables, narrow_weight, preferred_element_type=jnp.float32)

    keep, send, firsts, lists, blocks = pool_first(place, words, wide_rows, narrow_rows)
    both = added(keep, turned(send, "row", 2, 1))
    both, lists = lax.optimization_barrier((both, lists))
    moved = [
        turned(both[at * 512 : (at + 1) * 512], "x", 4, shift)
        for at, shift in enumerate(SHIFTS[:3])
    ]
    keep, send = pool_last(blocks, firsts, lists, wide_rows, narrow_rows)
    total = keep.astype(jnp.float32)
    for part in moved + [turned(send, "row", 2, 1)]:
        total = total + part.astype(jnp.float32)
    home = lax.all_to_all(
        total.astype(jnp.bfloat16).reshape(32, BAGS, 256), TABLES, 0, 0, tiled=True
    )

    bottom = dense_layer(
        dense_layer(dense_layer(dense_input, bottom_first), bottom_second), bottom_third
    )
    hidden, logits = top(bottom, home, top_first, top_last)
    return (hidden, logits.reshape(BAGS))


def solution(mesh):
    fine = Mesh(mesh.devices.reshape(4, 8, 4, 2), HOME)
    split = P(HOME)
    in_specs = (split, P(), P(), P()) + (split,) * 6 + (P(),) * 4
    return jax.shard_map(
        body, mesh=fine, in_specs=in_specs, out_specs=(split, split), check_vma=False
    )
```

time: 91.5 us -> 85.1 us (0.930)
  waiting for transfers between devices: 31 us -> 23.5 us
  Pallas kernels: 18.8 us -> 21 us
  starting transfers between devices: 25.7 us -> 24.6 us
    ppermute x4 -> x5, waiting for transfers between devices: 13.9 us -> 6.3 us  [turned(): lax.ppermute(block, axis, [(i, (i + shift) % count) for i in range(count)])]
    pallas_call x2 -> x3, Pallas kernels: 18.8 us -> 21 us  [the longest x1 11.7 us: pool_first(): pl.pallas_call(first_kernel, out_shape=(half, half, jax.ShapeDtypeStruct(...]
    convert_element_type x1, other arithmetic: 0.83 us -> 1.82 us  [body(): total.astype(jnp.bfloat16).reshape(32, BAGS, 256)]
    ppermute x4 -> x5, starting transfers between devices: 5.13 us -> 4.39 us  [turned(): lax.ppermute(block, axis, [(i, (i + shift) % count) for i in range(count)])]
  transfers between devices with their start and end apart: 6 -> 7, of which waited for: 6 -> 5; matrix products, arithmetic and copies ran while one was open for 7% -> 8% of each run, Pallas kernels for 0% -> 8%
where the time goes in v4:
time: 85.1 us; the launch traced here: 84.5 us
  starting transfers between devices  24.6 us (29%)
  waiting for transfers between devices  23.5 us (28%)
  Pallas kernels  21 us (25%)
  matrix products  5.86 us (7%)
  other arithmetic  4.86 us (6%)
  local copies, waits for them, and re-layouts  3.78 us (4%)
    all_to_all x1, starting transfers between devices, body(): words = lax.all_to_all(words, HOME, 0, 0, tiled=True)  14.4 us
    pallas_call x1, Pallas kernels, pool_first(): pl.pallas_call(first_kernel, out_shape=(half, half, jax.ShapeDtypeStruct(...  11.7 us
    all_to_all x1, waiting for transfers between devices, body(): lax.all_to_all(total.astype(jnp.bfloat16).reshape(32, BAGS, 256), TABLES,...  11.4 us
    pallas_call x1, Pallas kernels, pool_last(): pl.pallas_call(last_kernel, out_shape=(half, half), in_specs=[SMEM, SMEM,...  7.17 us
    ppermute x5, waiting for transfers between devices, turned(): lax.ppermute(block, axis, [(i, (i + shift) % count) for i in range(count)])  6.3 us
    all_to_all x1, waiting for transfers between devices, body(): words = lax.all_to_all(words, HOME, 0, 0, tiled=True)  5.85 us
    all_to_all x1, starting transfers between devices, body(): lax.all_to_all(total.astype(jnp.bfloat16).reshape(32, BAGS, 256), TABLES,...  5.84 us
    ppermute x5, starting transfers between devices, turned(): lax.ppermute(block, axis, [(i, (i + shift) % count) for i in range(count)])  4.39 us
  transfers between devices with their start and end apart: 7, of which 5 were waited for; matrix products, arithmetic and copies ran while one was open for 8% of the time, Pallas kernels for 8%

profile of v4, /device:TPU:32, one launch (start us, length us, event | category | flops | bytes accessed | tf_op | source)
XLA Modules:
  0.0 84.5 jit_solution(8746631300783345060)
XLA Ops:
  0.6 0.0 copy-start
  0.6 1.0 %or_bitcast_fusion = s32[32,8,16]{0,1,2:T(8,128)S(1)} fusion(s32[16,32,8]{1,2,0:T(8,128)} %param.22, s32[16,32,8]{1,2,0:T(8,128)} %param.20, s32[16,32]{1,0:T(8,128)} %param.23, s32[16,32]{1,0:T(8,128)} %param.21), kind=kLoop, calls=%fused_computation.13 | loop fusion | flops 24576 | bytes 53248 | tf_op jit(solution)/shard_map/transpose | solution.py:367
  1.7 0.1 copy.23
  1.8 0.7 broadcast_in_dim.16
  2.5 14.4 %all-to-all-start = ((s32[256,1,128]{2,1,0:T(1,128)}), s32[256,1,128]{2,1,0:T(1,128)S(1)}, u32[]{:S(2)}, u32[]{:S(2)}) async-start(s32[256,1,128]{2,1,0:T(1,128)} %bitcast.4), calls=%async_computation | async-start | bytes 262144 | tf_op jit(solution)/shard_map/all_to_all | solution.py:369
  16.9 0.7 pad_add_fusion.place_ref
  17.5 0.0 copy-done
  17.5 0.0 copy-start.3
  17.5 2.9 %convolution_bitcast_fusion.wide_ref = f32[4096,128]{1,0:T(8,128)} fusion(bf16[4096,256]{1,0:T(8,128)(2,1)S(1)} %copy-done, bf16[32,256,128]{2,1,0:T(8,128)(2,1)} %param.24, s32[]{:T(128)S(6)} %select_n.15), kind=kOutput, calls=%fused_computation | convolution fusion | flops 268435456 | bytes 4259844 | tf_op jit(solution)/shard_map/dot_general | solution.py:373
  20.5 0.0 copy-done.3
  20.5 2.6 %convolution_bitcast_fusion.1.narrow_ref = f32[4096,128]{1,0:T(8,128)} fusion(bf16[4096,64]{0,1:T(8,128)(2,1)S(1)} %copy-done.3, bf16[32,64,128]{2,1,0:T(8,128)(2,1)} %param.25, s32[]{:T(128)S(6)} %select_n.15), kind=kOutput, calls=%fused_computation.1 | convolution fusion | flops 67108864 | bytes 2637828 | tf_op jit(solution)/shard_map/dot_general | solution.py:374
  23.0 5.8 %all-to-all-done = s32[256,1,128]{2,1,0:T(1,128)S(1)} async-done(((s32[256,1,128]{2,1,0:T(1,128)}), s32[256,1,128]{2,1,0:T(1,128)S(1)}, u32[]{:S(2)}, u32[]{:S(2)}) %all-to-all-start) | async-done | bytes 131104 | tf_op jit(solution)/shard_map/all_to_all | solution.py:369
  28.9 0.0 copy-start.2
  28.9 0.6 copy-done.2
  29.5 11.7 %pool_first.1 = (bf16[1536,256]{1,0:T(8,128)(2,1)}, bf16[1536,256]{1,0:T(8,128)(2,1)}, s32[32,128]{1,0:T(8,128)}, s32[512,128]{1,0:T(8,128)}, s32[1]{0:T(128)}) custom-call(s32[2]{0:T(128)} %pad_add_fusion.place_ref, s32[256,128]{1,0:T(8,128)} %bitcast.26, f32[4096,128]{1,0:T(8,128)} %convolution_bitcast_fusion.wide_ref, ...), custom_call_target="tpu_custom_call" | custom-call | flops 1000000 | bytes 10000000 | tf_op jit(solution)/shard_map/pool_first/pallas_call | solution.py:236
  41.2 0.3 collective-permute-start
  41.6 2.2 %collective-permute-done = bf16[1536,256]{1,0:T(8,128)(2,1)S(1)} collective-permute-done((bf16[1536,256]{1,0:T(8,128)(2,1)}, bf16[1536,256]{1,0:T(8,128)(2,1)S(1)}, u32[]{:S(2)}, u32[]{:S(2)}) %collective-permute-start) | collective-permute-done | bytes 786464 | tf_op jit(solution)/shard_map/ppermute | solution.py:335
  43.8 1.3 %add_convert_fusion = bf16[1536,256]{1,0:T(8,128)(2,1)S(1)} fusion(bf16[1536,256]{1,0:T(8,128)(2,1)S(1)} %collective-permute-done, bf16[1536,256]{1,0:T(8,128)(2,1)} %get-tuple-element.15), kind=kLoop, calls=%fused_computation.2 | loop fusion | flops 1572864 | bytes 2359296 | tf_op jit(solution)/shard_map/convert_element_type | solution.py:339
  45.2 0.1 fusion.13
  45.2 0.7 collective-permute-start.1
  45.9 2.6 %collective-permute-start.2 = (bf16[512,256]{1,0:T(8,128)(2,1)S(1)}, bf16[512,256]{1,0:T(8,128)(2,1)S(1)}, u32[]{:S(2)}, u32[]{:S(2)}) collective-permute-start(bf16[512,256]{1,0:T(8,128)(2,1)S(1)} %get-tuple-element.26), channel_id=1, source_target_pairs={{0,6},{2,0},{4,2},{6,4},{1,7},{3,1},{5,3},{7,5},{8,14},{10,8},{12,... | collective-permute-start | bytes 786440 | tf_op jit(solution)/shard_map/ppermute | solution.py:335
  48.5 0.7 collective-permute-start.3
  49.2 7.2 %pool_last.1 = (bf16[512,256]{1,0:T(8,128)(2,1)}, bf16[512,256]{1,0:T(8,128)(2,1)}) custom-call(s32[1]{0:T(128)} %get-tuple-element.13.blocks_ref, s32[32,128]{1,0:T(8,128)} %get-tuple-element.14.firsts_ref, s32[512,128]{1,0:T(8,128)} %get-tuple-element.18.lists_ref, f32[4096,128]{1,0:T(8,128)} %convolution_bitcast_fusion.wide_ref, ...), custom_call_target="tpu_custom_call" | custom-call | flops 1000000 | bytes 10000000 | tf_op jit(solution)/shard_map/pool_last/pallas_call | solution.py:262
  56.4 0.0 copy-start.8
  56.4 0.0 copy-start.4
  56.4 0.0 copy-start.6
  56.4 0.0 copy-start.7
  56.4 0.0 copy-start.5
  56.4 0.1 collective-permute-start.4
  56.5 0.0 collective-permute-done.1
  56.5 3.3 %collective-permute-done.2 = bf16[512,256]{1,0:T(8,128)(2,1)S(1)} collective-permute-done((bf16[512,256]{1,0:T(8,128)(2,1)S(1)}, bf16[512,256]{1,0:T(8,128)(2,1)S(1)}, u32[]{:S(2)}, u32[]{:S(2)}) %collective-permute-start.2) | collective-permute-done | bytes 262176 | tf_op jit(solution)/shard_map/ppermute | solution.py:335
  59.9 0.7 collective-permute-done.3
  60.6 0.0 collective-permute-done.4
  60.6 1.8 %add_convert_fusion.1 = bf16[512,256]{1,0:T(8,128)(2,1)} fusion(bf16[512,256]{1,0:T(8,128)(2,1)S(1)} %collective-permute-done.4, bf16[512,256]{1,0:T(8,128)(2,1)S(1)} %collective-permute-done.3, bf16[512,256]{1,0:T(8,128)(2,1)S(1)} %collective-permute-done.2, bf16[512,256]{1,0:T(8,128)(2,1)S(1)} %collective-permute-done.1, bf16[512,256]{1,0:T(8,128)(2,1)} %get-tuple-element.19), kind=kLoop, calls=%fused_computation.10 | loop fusion | flops 1310720 | bytes 1572864 | tf_op jit(solution)/shard_map/convert_element_type | solution.py:388
  62.4 5.8 %all-to-all-start.1 = ((bf16[32,16,256]{2,1,0:T(8,128)(2,1)}), bf16[32,16,256]{2,1,0:T(8,128)(2,1)S(1)}, u32[]{:S(2)}, u32[]{:S(2)}) async-start(bf16[32,16,256]{2,1,0:T(8,128)(2,1)} %bitcast.10), calls=%async_computation.1 | async-start | bytes 524288 | tf_op jit(solution)/shard_map/all_to_all | solution.py:387
  68.3 0.0 copy-done.8
  68.3 0.0 copy-done.4
  68.3 0.0 copy-done.6
  68.3 0.0 copy-done.7
  68.3 0.2 fusion.3
  68.5 0.0 copy-done.5
  68.5 0.1 fusion.4.bottom_ref
  68.7 11.4 %all-to-all-done.1.home_ref = bf16[32,16,256]{2,1,0:T(8,128)(2,1)S(1)} async-done(((bf16[32,16,256]{2,1,0:T(8,128)(2,1)}), bf16[32,16,256]{2,1,0:T(8,128)(2,1)S(1)}, u32[]{:S(2)}, u32[]{:S(2)}) %all-to-all-start.1) | async-done | bytes 262176 | tf_op jit(solution)/shard_map/all_to_all | solution.py:387
  80.0 0.0 copy-start.1
  80.0 2.3 %copy-done.1 = bf16[2208,1024]{1,0:T(8,128)(2,1)S(1)} copy-done((bf16[2208,1024]{1,0:T(8,128)(2,1)S(1)}, bf16[2208,1024]{1,0:T(8,128)(2,1)}, u32[]{:S(2)}) %copy-start.1) | copy-done | bytes 4522008
  82.3 2.1 %top.1 = (bf16[16,1024]{1,0:T(8,128)(2,1)}, f32[1,16]{1,0:T(1,128)}) custom-call(bf16[16,128]{1,0:T(8,128)(2,1)S(1)} %fusion.4.bottom_ref, bf16[32,16,256]{2,1,0:T(8,128)(2,1)S(1)} %all-to-all-done.1.home_ref, bf16[2208,1024]{1,0:T(8,128)(2,1)S(1)} %copy-done.1, bf16[1,1024]{1,0:T(2,128)(2,1)S(1)} %reshape.22.last_ref), custom_call_target="tpu_custom_call" | custom-call | tf_op jit(solution)/shard_map/top/pallas_call | solution.py:306
  (2 shorter events, 0.0 us)
Async XLA Ops:
  0.6 16.9 %copy-start = (bf16[4096,256]{1,0:T(8,128)(2,1)S(1)}, bf16[4096,256]{1,0:T(8,128)(2,1)}, u32[]{:S(2)}) copy-start(bf16[4096,256]{1,0:T(8,128)(2,1)} %param.18) | copy-start | bytes 6291460
  2.5 26.4 %all-to-all-start = ((s32[256,1,128]{2,1,0:T(1,128)}), s32[256,1,128]{2,1,0:T(1,128)S(1)}, u32[]{:S(2)}, u32[]{:S(2)}) async-start(s32[256,1,128]{2,1,0:T(1,128)} %bitcast.4), calls=%async_computation | async-start | bytes 262144 | tf_op jit(solution)/shard_map/all_to_all | solution.py:369
  17.5 2.9 %copy-start.3 = (bf16[4096,64]{0,1:T(8,128)(2,1)S(1)}, bf16[4096,64]{0,1:T(8,128)(2,1)}, u32[]{:S(2)}) copy-start(bf16[4096,64]{0,1:T(8,128)(2,1)} %param.19) | copy-start | bytes 1572868
  28.9 0.6 copy-start.2
  41.2 2.6 %collective-permute-start = (bf16[1536,256]{1,0:T(8,128)(2,1)}, bf16[1536,256]{1,0:T(8,128)(2,1)S(1)}, u32[]{:S(2)}, u32[]{:S(2)}) collective-permute-start(bf16[1536,256]{1,0:T(8,128)(2,1)} %get-tuple-element.16), channel_id=1, source_target_pairs={{0,1},{1,0},{2,3},{3,2},{4,5},{5,4},{6,7},{7,6},{8,9},{9,8},{10,11... | collective-permute-start | bytes 2359304 | tf_op jit(solution)/shard_map/ppermute | solution.py:335
  45.2 11.3 %collective-permute-start.1 = (bf16[512,256]{1,0:T(8,128)(2,1)S(1)}, bf16[512,256]{1,0:T(8,128)(2,1)S(1)}, u32[]{:S(2)}, u32[]{:S(2)}) collective-permute-start(bf16[512,256]{1,0:T(8,128)(2,1)S(1)} %get-tuple-element.24), channel_id=1, source_target_pairs={{0,2},{2,4},{4,6},{6,0},{1,3},{3,5},{5,7},{7,1},{8,10},{10,12},{12... | collective-permute-start | bytes 786440 | tf_op jit(solution)/shard_map/ppermute | solution.py:335
  45.9 13.9 %collective-permute-start.2 = (bf16[512,256]{1,0:T(8,128)(2,1)S(1)}, bf16[512,256]{1,0:T(8,128)(2,1)S(1)}, u32[]{:S(2)}, u32[]{:S(2)}) collective-permute-start(bf16[512,256]{1,0:T(8,128)(2,1)S(1)} %get-tuple-element.26), channel_id=1, source_target_pairs={{0,6},{2,0},{4,2},{6,4},{1,7},{3,1},{5,3},{7,5},{8,14},{10,8},{12,... | collective-permute-start | bytes 786440 | tf_op jit(solution)/shard_map/ppermute | solution.py:335
  48.5 12.0 %collective-permute-start.3 = (bf16[512,256]{1,0:T(8,128)(2,1)S(1)}, bf16[512,256]{1,0:T(8,128)(2,1)S(1)}, u32[]{:S(2)}, u32[]{:S(2)}) collective-permute-start(bf16[512,256]{1,0:T(8,128)(2,1)S(1)} %get-tuple-element.25), channel_id=1, source_target_pairs={{0,4},{2,6},{4,0},{6,2},{1,5},{3,7},{5,1},{7,3},{8,12},{10,14},{12... | collective-permute-start | bytes 786440 | tf_op jit(solution)/shard_map/ppermute | solution.py:335
  56.4 11.9 %copy-start.8 = (bf16[1024]{0:T(1024)(128)(2,1)S(1)}, bf16[1024]{0:T(1024)(128)(2,1)}, u32[]{:S(2)}) copy-start(bf16[1024]{0:T(1024)(128)(2,1)} %param.27) | copy-start | bytes 6148
  56.4 11.9 %copy-start.4 = (bf16[512,256]{1,0:T(8,128)(2,1)S(1)}, bf16[512,256]{1,0:T(8,128)(2,1)}, u32[]{:S(2)}) copy-start(bf16[512,256]{1,0:T(8,128)(2,1)} %param.16) | copy-start | bytes 786436
  56.4 11.9 %copy-start.6 = (bf16[13,512]{1,0:T(8,128)(2,1)S(1)}, bf16[13,512]{1,0:T(8,128)(2,1)}, u32[]{:S(2)}) copy-start(bf16[13,512]{1,0:T(8,128)(2,1)} %param.15) | copy-start | bytes 39940
  56.4 11.9 %copy-start.7 = (bf16[16,13]{1,0:T(8,128)(2,1)S(1)}, bf16[16,13]{1,0:T(8,128)(2,1)}, u32[]{:S(2)}) copy-start(bf16[16,13]{1,0:T(8,128)(2,1)} %param.14) | copy-start | bytes 1252
  56.4 12.1 %copy-start.5 = (bf16[256,128]{1,0:T(8,128)(2,1)S(1)}, bf16[256,128]{1,0:T(8,128)(2,1)}, u32[]{:S(2)}) copy-start(bf16[256,128]{1,0:T(8,128)(2,1)} %param.17) | copy-start | bytes 196612
  56.4 4.2 %collective-permute-start.4 = (bf16[512,256]{1,0:T(8,128)(2,1)}, bf16[512,256]{1,0:T(8,128)(2,1)S(1)}, u32[]{:S(2)}, u32[]{:S(2)}) collective-permute-start(bf16[512,256]{1,0:T(8,128)(2,1)} %get-tuple-element.21), channel_id=1, source_target_pairs={{0,1},{1,0},{2,3},{3,2},{4,5},{5,4},{6,7},{7,6},{8,9},{9,8},{10,11... | collective-permute-start | bytes 786440 | tf_op jit(solution)/shard_map/ppermute | solution.py:335
  62.4 17.6 %all-to-all-start.1 = ((bf16[32,16,256]{2,1,0:T(8,128)(2,1)}), bf16[32,16,256]{2,1,0:T(8,128)(2,1)S(1)}, u32[]{:S(2)}, u32[]{:S(2)}) async-start(bf16[32,16,256]{2,1,0:T(8,128)(2,1)} %bitcast.10), calls=%async_computation.1 | async-start | bytes 524288 | tf_op jit(solution)/shard_map/all_to_all | solution.py:387
  80.0 2.3 %copy-start.1 = (bf16[2208,1024]{1,0:T(8,128)(2,1)S(1)}, bf16[2208,1024]{1,0:T(8,128)(2,1)}, u32[]{:S(2)}) copy-start(bf16[2208,1024]{1,0:T(8,128)(2,1)} %first_ref.1) | copy-start | bytes 13565956

commit v5 on v4

--- a/solution.py
+++ b/solution.py
@@ -17,10 +17,11 @@
 PITCH = 72
 INTER = 2208
 TOP = 1024
-LIMIT = pltpu.CompilerParams(vmem_limit_bytes=60 * 1024 * 1024)
+LIMIT = pltpu.CompilerParams(vmem_limit_bytes=24 * 1024 * 1024)
 VMEM = pl.BlockSpec(memory_space=pltpu.VMEM)
 SMEM = pl.BlockSpec(memory_space=pltpu.SMEM)
 ANY = pl.BlockSpec(memory_space=pl.ANY)
+HBM = pl.BlockSpec(memory_space=pltpu.HBM)
 
 
 def drawn_left(packed, field, unit, bits):
@@ -242,7 +243,7 @@
             jax.ShapeDtypeStruct((BLOCKS * LINES, LANES), jnp.int32),
             jax.ShapeDtypeStruct((1,), jnp.int32),
         ),
-        in_specs=[SMEM, VMEM, ANY, ANY],
+        in_specs=[SMEM, VMEM, HBM, HBM],
         out_specs=(VMEM, VMEM, VMEM, VMEM, SMEM),
         scratch_shapes=[pltpu.VMEM((2, LANES, SOURCES), jnp.int32)]
         + buffers
@@ -262,7 +263,7 @@
     return pl.pallas_call(
         last_kernel,
         out_shape=(half, half),
-        in_specs=[SMEM, SMEM, ANY, ANY, ANY],
+        in_specs=[SMEM, SMEM, ANY, HBM, HBM],
         out_specs=(VMEM, VMEM),
         scratch_shapes=buffers
         + [pltpu.SMEM((LINES, LANES), jnp.int32), pltpu.SemaphoreType.DMA((3,))],
@@ -373,6 +374,8 @@
     wide_rows = jnp.dot(wide_tables, wide_weight, preferred_element_type=jnp.float32)
     narrow_rows = jnp.dot(narrow_tables, narrow_weight, preferred_element_type=jnp.float32)
 
+    wide_rows = pltpu.with_memory_space_constraint(wide_rows, pltpu.HBM)
+    narrow_rows = pltpu.with_memory_space_constraint(narrow_rows, pltpu.HBM)
     keep, send, firsts, lists, blocks = pool_first(place, words, wide_rows, narrow_rows)
     both = added(keep, turned(send, "row", 2, 1))
     both, lists = lax.optimization_barrier((both, lists))

time: 85.1 us -> 80.7 us (0.948)
  other arithmetic: 4.86 us -> 2.18 us
  Pallas kernels: 21 us -> 19.2 us
  waiting for transfers between devices: 23.5 us -> 24.9 us
  starting transfers between devices: 24.6 us -> 23.7 us
    convert_element_type x1, other arithmetic: 1.33 us -> 0.2 us  [added(): (one.astype(jnp.float32) + other.astype(jnp.float32)).astype(jnp.bfloat16)]
    pallas_call x1, Pallas kernels: 11.7 us -> 10.7 us  [pool_first(): pl.pallas_call(first_kernel, out_shape=(half, half, jax.ShapeDtypeStruct(...]
    convert_element_type x1, other arithmetic: 1.82 us -> 0.87 us  [body(): total.astype(jnp.bfloat16).reshape(32, BAGS, 256)]
    pallas_call x1, Pallas kernels: 7.17 us -> 6.29 us  [pool_last(): pl.pallas_call(last_kernel, out_shape=(half, half), in_specs=[SMEM, SMEM,...]
    all_to_all x1, starting transfers between devices: 5.84 us -> 4.98 us  [body(): lax.all_to_all(total.astype(jnp.bfloat16).reshape(32, BAGS, 256), TABLES,...]
    unnamed x18 -> x16, local copies, waits for them, and re-layouts: 2.97 us -> 2.33 us
  transfers between devices with their start and end apart: 7 -> 7, of which waited for: 5 -> 4; matrix products, arithmetic and copies ran while one was open for 8% -> 7% of each run, Pallas kernels for 8% -> 8%
where the time goes in v5:
time: 80.7 us; the launch traced here: 79.7 us
  waiting for transfers between devices  24.9 us (31%)
  starting transfers between devices  23.7 us (29%)
  Pallas kernels  19.2 us (24%)
  matrix products  5.87 us (7%)
  local copies, waits for them, and re-layouts  3.14 us (4%)
  other arithmetic  2.18 us (3%)
  between operations  0.81 us (1%)
    all_to_all x1, starting transfers between devices, body(): words = lax.all_to_all(words, HOME, 0, 0, tiled=True)  14.4 us
    all_to_all x1, waiting for transfers between devices, body(): lax.all_to_all(total.astype(jnp.bfloat16).reshape(32, BAGS, 256), TABLES,...  11.3 us
    pallas_call x1, Pallas kernels, pool_first(): pl.pallas_call(first_kernel, out_shape=(half, half, jax.ShapeDtypeStruct(...  10.7 us
    ppermute x5, waiting for transfers between devices, turned(): lax.ppermute(block, axis, [(i, (i + shift) % count) for i in range(count)])  7.12 us
    all_to_all x1, waiting for transfers between devices, body(): words = lax.all_to_all(words, HOME, 0, 0, tiled=True)  6.44 us
    pallas_call x1, Pallas kernels, pool_last(): pl.pallas_call(last_kernel, out_shape=(half, half), in_specs=[SMEM, SMEM,...  6.29 us
    all_to_all x1, starting transfers between devices, body(): lax.all_to_all(total.astype(jnp.bfloat16).reshape(32, BAGS, 256), TABLES,...  4.98 us
    ppermute x5, starting transfers between devices, turned(): lax.ppermute(block, axis, [(i, (i + shift) % count) for i in range(count)])  4.3 us
  transfers between devices with their start and end apart: 7, of which 4 were waited for; matrix products, arithmetic and copies ran while one was open for 7% of the time, Pallas kernels for 8%

profile of v5, /device:TPU:32, one launch (start us, length us, event | category | flops | bytes accessed | tf_op | source)
XLA Modules:
  0.0 79.7 jit_solution(13142409623284280590)
XLA Ops:
  0.6 0.0 copy-start
  0.6 1.0 %or_bitcast_fusion = s32[32,8,16]{0,1,2:T(8,128)S(1)} fusion(s32[16,32,8]{1,2,0:T(8,128)} %param.22, s32[16,32,8]{1,2,0:T(8,128)} %param.20, s32[16,32]{1,0:T(8,128)} %param.23, s32[16,32]{1,0:T(8,128)} %param.21), kind=kLoop, calls=%fused_computation.13 | loop fusion | flops 24576 | bytes 53248 | tf_op jit(solution)/shard_map/transpose | solution.py:368
  1.7 0.1 copy.23
  1.8 0.7 broadcast_in_dim.16
  2.5 14.4 %all-to-all-start = ((s32[256,1,128]{2,1,0:T(1,128)}), s32[256,1,128]{2,1,0:T(1,128)S(1)}, u32[]{:S(2)}, u32[]{:S(2)}) async-start(s32[256,1,128]{2,1,0:T(1,128)} %bitcast.4), calls=%async_computation | async-start | bytes 262144 | tf_op jit(solution)/shard_map/all_to_all | solution.py:370
  16.9 0.1 pad_add_fusion.place_ref
  16.9 0.0 copy-done
  16.9 0.0 copy-start.2
  16.9 2.9 %convolution_bitcast_fusion.wide_ref = f32[4096,128]{1,0:T(8,128)} fusion(bf16[4096,256]{1,0:T(8,128)(2,1)S(1)} %copy-done, bf16[32,256,128]{2,1,0:T(8,128)(2,1)} %param.24, s32[]{:T(128)S(6)} %select_n.15), kind=kOutput, calls=%fused_computation | convolution fusion | flops 268435456 | bytes 4259844 | tf_op jit(solution)/shard_map/dot_general | solution.py:374
  19.9 0.0 copy-done.2
  19.9 2.6 %convolution_bitcast_fusion.1.narrow_ref = f32[4096,128]{1,0:T(8,128)} fusion(bf16[4096,64]{0,1:T(8,128)(2,1)S(1)} %copy-done.2, bf16[32,64,128]{2,1,0:T(8,128)(2,1)} %param.25, s32[]{:T(128)S(6)} %select_n.15), kind=kOutput, calls=%fused_computation.1 | convolution fusion | flops 67108864 | bytes 2637828 | tf_op jit(solution)/shard_map/dot_general | solution.py:375
  22.4 6.4 %all-to-all-done = s32[256,1,128]{2,1,0:T(1,128)S(1)} async-done(((s32[256,1,128]{2,1,0:T(1,128)}), s32[256,1,128]{2,1,0:T(1,128)S(1)}, u32[]{:S(2)}, u32[]{:S(2)}) %all-to-all-start) | async-done | bytes 131104 | tf_op jit(solution)/shard_map/all_to_all | solution.py:370
  28.9 10.7 %pool_first.1 = (bf16[1536,256]{1,0:T(8,128)(2,1)S(1)}, bf16[1536,256]{1,0:T(8,128)(2,1)S(1)}, s32[32,128]{1,0:T(8,128)S(1)}, s32[512,128]{1,0:T(8,128)S(1)}, s32[1]{0:T(128)}) custom-call(s32[2]{0:T(128)S(1)} %pad_add_fusion.place_ref, s32[256,128]{1,0:T(8,128)S(1)} %bitcast.26, f32[4096,128]{1,0:T(8,128)} %convolution_bitcast_fusion.wide_ref, ...), custom_call_target="tpu_custom_call" | custom-call | flops 1000000 | bytes 10000000 | tf_op jit(solution)/shard_map/pool_first/pallas_call | solution.py:237
  39.6 0.4 collective-permute-start
  40.0 2.0 %collective-permute-done = bf16[1536,256]{1,0:T(8,128)(2,1)S(1)} collective-permute-done((bf16[1536,256]{1,0:T(8,128)(2,1)S(1)}, bf16[1536,256]{1,0:T(8,128)(2,1)S(1)}, u32[]{:S(2)}, u32[]{:S(2)}) %collective-permute-start) | collective-permute-done | bytes 786464 | tf_op jit(solution)/shard_map/ppermute | solution.py:336
  42.0 0.2 add_convert_fusion
  42.2 0.1 fusion.13
  42.3 0.6 collective-permute-start.1
  42.9 2.7 %collective-permute-start.2 = (bf16[512,256]{1,0:T(8,128)(2,1)S(1)}, bf16[512,256]{1,0:T(8,128)(2,1)S(1)}, u32[]{:S(2)}, u32[]{:S(2)}) collective-permute-start(bf16[512,256]{1,0:T(8,128)(2,1)S(1)} %get-tuple-element.26), channel_id=1, source_target_pairs={{0,6},{2,0},{4,2},{6,4},{1,7},{3,1},{5,3},{7,5},{8,14},{10,8},{12,... | collective-permute-start | bytes 786440 | tf_op jit(solution)/shard_map/ppermute | solution.py:336
  45.6 0.5 collective-permute-start.3
  46.1 6.3 %pool_last.1 = (bf16[512,256]{1,0:T(8,128)(2,1)S(1)}, bf16[512,256]{1,0:T(8,128)(2,1)S(1)}) custom-call(s32[1]{0:T(128)} %get-tuple-element.13.blocks_ref, s32[32,128]{1,0:T(8,128)S(1)} %get-tuple-element.14.firsts_ref, s32[512,128]{1,0:T(8,128)S(1)} %get-tuple-element.18.lists_ref, f32[4096,128]{1,0:T(8,128)} %convolution_bitcast_fusion.wide_ref, ...), custom_call_target="tpu_custom_call" | custom-call | flops 1000000 | bytes 10000000 | tf_op jit(solution)/shard_map/pool_last/pallas_call | solution.py:263
  52.4 0.0 copy-start.7
  52.4 0.0 copy-start.3
  52.4 0.0 copy-start.5
  52.4 0.0 copy-start.6
  52.4 0.0 copy-start.4
  52.4 0.1 collective-permute-start.4
  52.5 5.1 %collective-permute-done.1 = bf16[512,256]{1,0:T(8,128)(2,1)S(1)} collective-permute-done((bf16[512,256]{1,0:T(8,128)(2,1)S(1)}, bf16[512,256]{1,0:T(8,128)(2,1)S(1)}, u32[]{:S(2)}, u32[]{:S(2)}) %collective-permute-start.1) | collective-permute-done | bytes 262176 | tf_op jit(solution)/shard_map/ppermute | solution.py:336
  57.7 0.0 collective-permute-done.2
  57.7 0.0 collective-permute-done.3
  57.7 0.0 collective-permute-done.4
  57.7 0.9 %add_convert_fusion.1 = bf16[512,256]{1,0:T(8,128)(2,1)} fusion(bf16[512,256]{1,0:T(8,128)(2,1)S(1)} %collective-permute-done.4, bf16[512,256]{1,0:T(8,128)(2,1)S(1)} %collective-permute-done.3, bf16[512,256]{1,0:T(8,128)(2,1)S(1)} %collective-permute-done.2, bf16[512,256]{1,0:T(8,128)(2,1)S(1)} %collective-permute-done.1, ...), kind=kLoop, calls=%fused_computation.10 | loop fusion | flops 1310720 | bytes 1572864 | tf_op jit(solution)/shard_map/convert_element_type | solution.py:391
  58.5 5.0 %all-to-all-start.1 = ((bf16[32,16,256]{2,1,0:T(8,128)(2,1)}), bf16[32,16,256]{2,1,0:T(8,128)(2,1)S(1)}, u32[]{:S(2)}, u32[]{:S(2)}) async-start(bf16[32,16,256]{2,1,0:T(8,128)(2,1)} %bitcast.10), calls=%async_computation.1 | async-start | bytes 524288 | tf_op jit(solution)/shard_map/all_to_all | solution.py:390
  63.5 0.0 copy-done.7
  63.6 0.0 copy-done.3
  63.6 0.0 copy-done.5
  63.6 0.0 copy-done.6
  63.6 0.2 fusion.3
  63.8 0.0 copy-done.4
  63.8 0.1 fusion.4.bottom_ref
  64.0 11.3 %all-to-all-done.1.home_ref = bf16[32,16,256]{2,1,0:T(8,128)(2,1)S(1)} async-done(((bf16[32,16,256]{2,1,0:T(8,128)(2,1)}), bf16[32,16,256]{2,1,0:T(8,128)(2,1)S(1)}, u32[]{:S(2)}, u32[]{:S(2)}) %all-to-all-start.1) | async-done | bytes 262176 | tf_op jit(solution)/shard_map/all_to_all | solution.py:390
  75.3 0.0 copy-start.1
  75.3 2.3 %copy-done.1 = bf16[2208,1024]{1,0:T(8,128)(2,1)S(1)} copy-done((bf16[2208,1024]{1,0:T(8,128)(2,1)S(1)}, bf16[2208,1024]{1,0:T(8,128)(2,1)}, u32[]{:S(2)}) %copy-start.1) | copy-done | bytes 4522008
  77.6 2.1 %top.1 = (bf16[16,1024]{1,0:T(8,128)(2,1)}, f32[1,16]{1,0:T(1,128)}) custom-call(bf16[16,128]{1,0:T(8,128)(2,1)S(1)} %fusion.4.bottom_ref, bf16[32,16,256]{2,1,0:T(8,128)(2,1)S(1)} %all-to-all-done.1.home_ref, bf16[2208,1024]{1,0:T(8,128)(2,1)S(1)} %copy-done.1, bf16[1,1024]{1,0:T(2,128)(2,1)S(1)} %reshape.22.last_ref), custom_call_target="tpu_custom_call" | custom-call | tf_op jit(solution)/shard_map/top/pallas_call | solution.py:307
  (2 shorter events, 0.0 us)
Async XLA Ops:
  0.6 16.3 %copy-start = (bf16[4096,256]{1,0:T(8,128)(2,1)S(1)}, bf16[4096,256]{1,0:T(8,128)(2,1)}, u32[]{:S(2)}) copy-start(bf16[4096,256]{1,0:T(8,128)(2,1)} %param.18) | copy-start | bytes 6291460
  2.5 26.4 %all-to-all-start = ((s32[256,1,128]{2,1,0:T(1,128)}), s32[256,1,128]{2,1,0:T(1,128)S(1)}, u32[]{:S(2)}, u32[]{:S(2)}) async-start(s32[256,1,128]{2,1,0:T(1,128)} %bitcast.4), calls=%async_computation | async-start | bytes 262144 | tf_op jit(solution)/shard_map/all_to_all | solution.py:370
  16.9 2.9 %copy-start.2 = (bf16[4096,64]{0,1:T(8,128)(2,1)S(1)}, bf16[4096,64]{0,1:T(8,128)(2,1)}, u32[]{:S(2)}) copy-start(bf16[4096,64]{0,1:T(8,128)(2,1)} %param.19) | copy-start | bytes 1572868
  39.6 2.4 %collective-permute-start = (bf16[1536,256]{1,0:T(8,128)(2,1)S(1)}, bf16[1536,256]{1,0:T(8,128)(2,1)S(1)}, u32[]{:S(2)}, u32[]{:S(2)}) collective-permute-start(bf16[1536,256]{1,0:T(8,128)(2,1)S(1)} %get-tuple-element.16), channel_id=1, source_target_pairs={{0,1},{1,0},{2,3},{3,2},{4,5},{5,4},{6,7},{7,6},{8,9},{9,8},{10,11... | collective-permute-start | bytes 2359304 | tf_op jit(solution)/shard_map/ppermute | solution.py:336
  42.3 15.4 %collective-permute-start.1 = (bf16[512,256]{1,0:T(8,128)(2,1)S(1)}, bf16[512,256]{1,0:T(8,128)(2,1)S(1)}, u32[]{:S(2)}, u32[]{:S(2)}) collective-permute-start(bf16[512,256]{1,0:T(8,128)(2,1)S(1)} %get-tuple-element.24), channel_id=1, source_target_pairs={{0,2},{2,4},{4,6},{6,0},{1,3},{3,5},{5,7},{7,1},{8,10},{10,12},{12... | collective-permute-start | bytes 786440 | tf_op jit(solution)/shard_map/ppermute | solution.py:336
  42.9 14.8 %collective-permute-start.2 = (bf16[512,256]{1,0:T(8,128)(2,1)S(1)}, bf16[512,256]{1,0:T(8,128)(2,1)S(1)}, u32[]{:S(2)}, u32[]{:S(2)}) collective-permute-start(bf16[512,256]{1,0:T(8,128)(2,1)S(1)} %get-tuple-element.26), channel_id=1, source_target_pairs={{0,6},{2,0},{4,2},{6,4},{1,7},{3,1},{5,3},{7,5},{8,14},{10,8},{12,... | collective-permute-start | bytes 786440 | tf_op jit(solution)/shard_map/ppermute | solution.py:336
  45.6 12.1 %collective-permute-start.3 = (bf16[512,256]{1,0:T(8,128)(2,1)S(1)}, bf16[512,256]{1,0:T(8,128)(2,1)S(1)}, u32[]{:S(2)}, u32[]{:S(2)}) collective-permute-start(bf16[512,256]{1,0:T(8,128)(2,1)S(1)} %get-tuple-element.25), channel_id=1, source_target_pairs={{0,4},{2,6},{4,0},{6,2},{1,5},{3,7},{5,1},{7,3},{8,12},{10,14},{12... | collective-permute-start | bytes 786440 | tf_op jit(solution)/shard_map/ppermute | solution.py:336
  52.4 11.2 %copy-start.7 = (bf16[1024]{0:T(1024)(128)(2,1)S(1)}, bf16[1024]{0:T(1024)(128)(2,1)}, u32[]{:S(2)}) copy-start(bf16[1024]{0:T(1024)(128)(2,1)} %param.27) | copy-start | bytes 6148
  52.4 11.2 %copy-start.3 = (bf16[512,256]{1,0:T(8,128)(2,1)S(1)}, bf16[512,256]{1,0:T(8,128)(2,1)}, u32[]{:S(2)}) copy-start(bf16[512,256]{1,0:T(8,128)(2,1)} %param.16) | copy-start | bytes 786436
  52.4 11.2 %copy-start.5 = (bf16[13,512]{1,0:T(8,128)(2,1)S(1)}, bf16[13,512]{1,0:T(8,128)(2,1)}, u32[]{:S(2)}) copy-start(bf16[13,512]{1,0:T(8,128)(2,1)} %param.15) | copy-start | bytes 39940
  52.4 11.2 %copy-start.6 = (bf16[16,13]{1,0:T(8,128)(2,1)S(1)}, bf16[16,13]{1,0:T(8,128)(2,1)}, u32[]{:S(2)}) copy-start(bf16[16,13]{1,0:T(8,128)(2,1)} %param.14) | copy-start | bytes 1252
  52.4 11.4 %copy-start.4 = (bf16[256,128]{1,0:T(8,128)(2,1)S(1)}, bf16[256,128]{1,0:T(8,128)(2,1)}, u32[]{:S(2)}) copy-start(bf16[256,128]{1,0:T(8,128)(2,1)} %param.17) | copy-start | bytes 196612
  52.4 5.2 %collective-permute-start.4 = (bf16[512,256]{1,0:T(8,128)(2,1)S(1)}, bf16[512,256]{1,0:T(8,128)(2,1)S(1)}, u32[]{:S(2)}, u32[]{:S(2)}) collective-permute-start(bf16[512,256]{1,0:T(8,128)(2,1)S(1)} %get-tuple-element.21), channel_id=1, source_target_pairs={{0,1},{1,0},{2,3},{3,2},{4,5},{5,4},{6,7},{7,6},{8,9},{9,8},{10,11... | collective-permute-start | bytes 786440 | tf_op jit(solution)/shard_map/ppermute | solution.py:336
  58.5 16.8 %all-to-all-start.1 = ((bf16[32,16,256]{2,1,0:T(8,128)(2,1)}), bf16[32,16,256]{2,1,0:T(8,128)(2,1)S(1)}, u32[]{:S(2)}, u32[]{:S(2)}) async-start(bf16[32,16,256]{2,1,0:T(8,128)(2,1)} %bitcast.10), calls=%async_computation.1 | async-start | bytes 524288 | tf_op jit(solution)/shard_map/all_to_all | solution.py:390
  75.3 2.3 %copy-start.1 = (bf16[2208,1024]{1,0:T(8,128)(2,1)S(1)}, bf16[2208,1024]{1,0:T(8,128)(2,1)}, u32[]{:S(2)}) copy-start(bf16[2208,1024]{1,0:T(8,128)(2,1)} %first_ref.1) | copy-start | bytes 13565956

commit v6 on v5

--- a/solution.py
+++ b/solution.py
@@ -17,6 +17,7 @@
 PITCH = 72
 INTER = 2208
 TOP = 1024
+SLABS = [pl.ds(0, 768), pl.ds(768, 768), pl.ds(1536, 672)]
 LIMIT = pltpu.CompilerParams(vmem_limit_bytes=24 * 1024 * 1024)
 VMEM = pl.BlockSpec(memory_space=pltpu.VMEM)
 SMEM = pl.BlockSpec(memory_space=pltpu.SMEM)
@@ -273,7 +274,12 @@
     )(blocks, firsts, lists, wide, narrow)
 
 
-def top_kernel(bottom_ref, home_ref, first_ref, last_ref, hidden_ref, logits_ref, stack, grams, joined):
+def top_kernel(bottom_ref, home_ref, first_ref, last_ref, hidden_ref, logits_ref, stack, grams, joined,
+               first, sems):
+    copies = []
+    for at, rows in enumerate(SLABS):
+        copies.append(pltpu.make_async_copy(first_ref.at[rows], first.at[rows], sems.at[at]))
+        copies[-1].start()
     bottom = bottom_ref[...].astype(jnp.float32)
     stack[:, 0:1, :] = bottom[:, None, :]
     for table in range(32):
@@ -293,9 +299,12 @@
         line = grams[pl.ds(f, BAGS, stride=PITCH), :]
         joined[:, at : at + count] = line[:, f + 1 : FEATURES]
         at += count
-    hidden = jnp.dot(
-        joined[...].astype(jnp.bfloat16), first_ref[...], preferred_element_type=jnp.float32
-    )
+    hidden = jnp.zeros((BAGS, TOP), jnp.float32)
+    for copy, rows in zip(copies, SLABS):
+        copy.wait()
+        hidden = hidden + jnp.dot(
+            joined[:, rows].astype(jnp.bfloat16), first[rows, :], preferred_element_type=jnp.float32
+        )
     hidden = jnp.maximum(hidden, 0.0).astype(jnp.bfloat16)
     hidden_ref[...] = hidden
     logits_ref[...] = lax.dot_general(
@@ -310,12 +319,14 @@
             jax.ShapeDtypeStruct((BAGS, TOP), jnp.bfloat16),
             jax.ShapeDtypeStruct((1, BAGS), jnp.float32),
         ),
-        in_specs=[VMEM] * 4,
+        in_specs=[VMEM, VMEM, HBM, VMEM],
         out_specs=(VMEM, VMEM),
         scratch_shapes=[
             pltpu.VMEM((BAGS, PITCH, LANES), jnp.float32),
             pltpu.VMEM((BAGS * PITCH, LANES), jnp.float32),
             pltpu.VMEM((BAGS, INTER), jnp.float32),
+            pltpu.VMEM((INTER, TOP), jnp.bfloat16),
+            pltpu.SemaphoreType.DMA((3,)),
         ],
         compiler_params=pltpu.CompilerParams(vmem_limit_bytes=16 * 1024 * 1024),
         name="top",
@@ -394,6 +405,7 @@
     bottom = dense_layer(
         dense_layer(dense_layer(dense_input, bottom_first), bottom_second), bottom_third
     )
+    top_first = pltpu.with_memory_space_constraint(top_first, pltpu.HBM)
     hidden, logits = top(bottom, home, top_first, top_last)
     return (hidden, logits.reshape(BAGS))
 

time: 80.7 us -> 80.8 us (level)
  local copies, waits for them, and re-layouts: 3.14 us -> 0.86 us
  Pallas kernels: 19.2 us -> 21.1 us
    unnamed x16 -> x14, local copies, waits for them, and re-layouts: 2.33 us -> 0.04 us
    pallas_call x1, Pallas kernels: 2.13 us -> 4.05 us  [top(): pl.pallas_call(top_kernel, out_shape=(jax.ShapeDtypeStruct((BAGS, TOP), j...]
  transfers between devices with their start and end apart: 7 -> 7, of which waited for: 4 -> 4; matrix products, arithmetic and copies ran while one was open for 7% -> 8% of each run, Pallas kernels for 8% -> 8%
where the time goes in v6:
time: 80.8 us; the launch traced here: 79.4 us
  waiting for transfers between devices  24.7 us (31%)
  starting transfers between devices  23.8 us (29%)
  Pallas kernels  21.1 us (26%)
  matrix products  5.88 us (7%)
  other arithmetic  2.17 us (3%)
  local copies, waits for them, and re-layouts  0.86 us (1%)
    all_to_all x1, starting transfers between devices, body(): words = lax.all_to_all(words, HOME, 0, 0, tiled=True)  14.4 us
    all_to_all x1, waiting for transfers between devices, body(): lax.all_to_all(total.astype(jnp.bfloat16).reshape(32, BAGS, 256), TABLES,...  11.4 us
    pallas_call x1, Pallas kernels, pool_first(): pl.pallas_call(first_kernel, out_shape=(half, half, jax.ShapeDtypeStruct(...  10.8 us
    ppermute x5, waiting for transfers between devices, turned(): lax.ppermute(block, axis, [(i, (i + shift) % count) for i in range(count)])  6.93 us
    all_to_all x1, waiting for transfers between devices, body(): words = lax.all_to_all(words, HOME, 0, 0, tiled=True)  6.46 us
    pallas_call x1, Pallas kernels, pool_last(): pl.pallas_call(last_kernel, out_shape=(half, half), in_specs=[SMEM, SMEM,...  6.28 us
    all_to_all x1, starting transfers between devices, body(): lax.all_to_all(total.astype(jnp.bfloat16).reshape(32, BAGS, 256), TABLES,...  4.99 us
    ppermute x5, starting transfers between devices, turned(): lax.ppermute(block, axis, [(i, (i + shift) % count) for i in range(count)])  4.44 us
  transfers between devices with their start and end apart: 7, of which 4 were waited for; matrix products, arithmetic and copies ran while one was open for 8% of the time, Pallas kernels for 8%

profile of v6, /device:TPU:32, one launch (start us, length us, event | category | flops | bytes accessed | tf_op | source)
XLA Modules:
  0.0 79.4 jit_solution(567554632712799411)
XLA Ops:
  0.6 0.0 copy-start
  0.6 1.0 %or_bitcast_fusion = s32[32,8,16]{0,1,2:T(8,128)S(1)} fusion(s32[16,32,8]{1,2,0:T(8,128)} %param.22, s32[16,32,8]{1,2,0:T(8,128)} %param.20, s32[16,32]{1,0:T(8,128)} %param.23, s32[16,32]{1,0:T(8,128)} %param.21), kind=kLoop, calls=%fused_computation.13 | loop fusion | flops 24576 | bytes 53248 | tf_op jit(solution)/shard_map/transpose | solution.py:379
  1.7 0.1 copy.23
  1.8 0.7 broadcast_in_dim.16
  2.5 14.4 %all-to-all-start = ((s32[256,1,128]{2,1,0:T(1,128)}), s32[256,1,128]{2,1,0:T(1,128)S(1)}, u32[]{:S(2)}, u32[]{:S(2)}) async-start(s32[256,1,128]{2,1,0:T(1,128)} %bitcast.4), calls=%async_computation | async-start | bytes 262144 | tf_op jit(solution)/shard_map/all_to_all | solution.py:381
  16.9 0.1 pad_add_fusion.place_ref
  16.9 0.0 copy-done
  16.9 0.0 copy-start.1
  16.9 3.0 %convolution_bitcast_fusion.wide_ref = f32[4096,128]{1,0:T(8,128)} fusion(bf16[4096,256]{1,0:T(8,128)(2,1)S(1)} %copy-done, bf16[32,256,128]{2,1,0:T(8,128)(2,1)} %param.24, s32[]{:T(128)S(6)} %select_n.15), kind=kOutput, calls=%fused_computation | convolution fusion | flops 268435456 | bytes 4259844 | tf_op jit(solution)/shard_map/dot_general | solution.py:385
  19.9 0.0 copy-done.1
  19.9 2.6 %convolution_bitcast_fusion.1.narrow_ref = f32[4096,128]{1,0:T(8,128)} fusion(bf16[4096,64]{0,1:T(8,128)(2,1)S(1)} %copy-done.1, bf16[32,64,128]{2,1,0:T(8,128)(2,1)} %param.25, s32[]{:T(128)S(6)} %select_n.15), kind=kOutput, calls=%fused_computation.1 | convolution fusion | flops 67108864 | bytes 2637828 | tf_op jit(solution)/shard_map/dot_general | solution.py:386
  22.4 6.5 %all-to-all-done = s32[256,1,128]{2,1,0:T(1,128)S(1)} async-done(((s32[256,1,128]{2,1,0:T(1,128)}), s32[256,1,128]{2,1,0:T(1,128)S(1)}, u32[]{:S(2)}, u32[]{:S(2)}) %all-to-all-start) | async-done | bytes 131104 | tf_op jit(solution)/shard_map/all_to_all | solution.py:381
  28.9 10.8 %pool_first.1 = (bf16[1536,256]{1,0:T(8,128)(2,1)S(1)}, bf16[1536,256]{1,0:T(8,128)(2,1)S(1)}, s32[32,128]{1,0:T(8,128)S(1)}, s32[512,128]{1,0:T(8,128)S(1)}, s32[1]{0:T(128)}) custom-call(s32[2]{0:T(128)S(1)} %pad_add_fusion.place_ref, s32[256,128]{1,0:T(8,128)S(1)} %bitcast.26, f32[4096,128]{1,0:T(8,128)} %convolution_bitcast_fusion.wide_ref, ...), custom_call_target="tpu_custom_call" | custom-call | flops 1000000 | bytes 10000000 | tf_op jit(solution)/shard_map/pool_first/pallas_call | solution.py:238
  39.7 0.3 collective-permute-start
  40.0 2.1 %collective-permute-done = bf16[1536,256]{1,0:T(8,128)(2,1)S(1)} collective-permute-done((bf16[1536,256]{1,0:T(8,128)(2,1)S(1)}, bf16[1536,256]{1,0:T(8,128)(2,1)S(1)}, u32[]{:S(2)}, u32[]{:S(2)}) %collective-permute-start) | collective-permute-done | bytes 786464 | tf_op jit(solution)/shard_map/ppermute | solution.py:347
  42.1 0.2 add_convert_fusion
  42.3 0.1 fusion.13
  42.4 0.5 collective-permute-start.1
  42.9 2.8 %collective-permute-start.2 = (bf16[512,256]{1,0:T(8,128)(2,1)S(1)}, bf16[512,256]{1,0:T(8,128)(2,1)S(1)}, u32[]{:S(2)}, u32[]{:S(2)}) collective-permute-start(bf16[512,256]{1,0:T(8,128)(2,1)S(1)} %get-tuple-element.26), channel_id=1, source_target_pairs={{0,6},{2,0},{4,2},{6,4},{1,7},{3,1},{5,3},{7,5},{8,14},{10,8},{12,... | collective-permute-start | bytes 786440 | tf_op jit(solution)/shard_map/ppermute | solution.py:347
  45.7 0.7 collective-permute-start.3
  46.4 6.3 %pool_last.1 = (bf16[512,256]{1,0:T(8,128)(2,1)S(1)}, bf16[512,256]{1,0:T(8,128)(2,1)S(1)}) custom-call(s32[1]{0:T(128)} %get-tuple-element.13.blocks_ref, s32[32,128]{1,0:T(8,128)S(1)} %get-tuple-element.14.firsts_ref, s32[512,128]{1,0:T(8,128)S(1)} %get-tuple-element.18.lists_ref, f32[4096,128]{1,0:T(8,128)} %convolution_bitcast_fusion.wide_ref, ...), custom_call_target="tpu_custom_call" | custom-call | flops 1000000 | bytes 10000000 | tf_op jit(solution)/shard_map/pool_last/pallas_call | solution.py:264
  52.7 0.0 copy-start.6
  52.7 0.0 copy-start.2
  52.7 0.0 copy-start.4
  52.7 0.0 copy-start.5
  52.7 0.0 copy-start.3
  52.7 0.1 collective-permute-start.4
  52.8 4.9 %collective-permute-done.1 = bf16[512,256]{1,0:T(8,128)(2,1)S(1)} collective-permute-done((bf16[512,256]{1,0:T(8,128)(2,1)S(1)}, bf16[512,256]{1,0:T(8,128)(2,1)S(1)}, u32[]{:S(2)}, u32[]{:S(2)}) %collective-permute-start.1) | collective-permute-done | bytes 262176 | tf_op jit(solution)/shard_map/ppermute | solution.py:347
  57.7 0.0 collective-permute-done.2
  57.7 0.0 collective-permute-done.3
  57.7 0.0 collective-permute-done.4
  57.7 0.9 %add_convert_fusion.1 = bf16[512,256]{1,0:T(8,128)(2,1)} fusion(bf16[512,256]{1,0:T(8,128)(2,1)S(1)} %collective-permute-done.4, bf16[512,256]{1,0:T(8,128)(2,1)S(1)} %collective-permute-done.3, bf16[512,256]{1,0:T(8,128)(2,1)S(1)} %collective-permute-done.2, bf16[512,256]{1,0:T(8,128)(2,1)S(1)} %collective-permute-done.1, ...), kind=kLoop, calls=%fused_computation.10 | loop fusion | flops 1310720 | bytes 1572864 | tf_op jit(solution)/shard_map/convert_element_type | solution.py:402
  58.6 5.0 %all-to-all-start.1 = ((bf16[32,16,256]{2,1,0:T(8,128)(2,1)}), bf16[32,16,256]{2,1,0:T(8,128)(2,1)S(1)}, u32[]{:S(2)}, u32[]{:S(2)}) async-start(bf16[32,16,256]{2,1,0:T(8,128)(2,1)} %bitcast.10), calls=%async_computation.1 | async-start | bytes 524288 | tf_op jit(solution)/shard_map/all_to_all | solution.py:401
  63.6 0.0 copy-done.6
  63.6 0.0 copy-done.2
  63.6 0.0 copy-done.4
  63.6 0.0 copy-done.5
  63.6 0.2 fusion.3
  63.9 0.0 copy-done.3
  63.9 0.1 fusion.4.bottom_ref
  64.0 11.4 %all-to-all-done.1.home_ref = bf16[32,16,256]{2,1,0:T(8,128)(2,1)S(1)} async-done(((bf16[32,16,256]{2,1,0:T(8,128)(2,1)}), bf16[32,16,256]{2,1,0:T(8,128)(2,1)S(1)}, u32[]{:S(2)}, u32[]{:S(2)}) %all-to-all-start.1) | async-done | bytes 262176 | tf_op jit(solution)/shard_map/all_to_all | solution.py:401
  75.4 4.0 %top.1 = (bf16[16,1024]{1,0:T(8,128)(2,1)}, f32[1,16]{1,0:T(1,128)}) custom-call(bf16[16,128]{1,0:T(8,128)(2,1)S(1)} %fusion.4.bottom_ref, bf16[32,16,256]{2,1,0:T(8,128)(2,1)S(1)} %all-to-all-done.1.home_ref, bf16[2208,1024]{1,0:T(8,128)(2,1)} %first_ref.1, bf16[1,1024]{1,0:T(2,128)(2,1)S(1)} %reshape.22.last_ref), custom_call_target="tpu_custom_call" | custom-call | tf_op jit(solution)/shard_map/top/pallas_call | solution.py:316
  (2 shorter events, 0.0 us)
Async XLA Ops:
  0.6 16.3 %copy-start = (bf16[4096,256]{1,0:T(8,128)(2,1)S(1)}, bf16[4096,256]{1,0:T(8,128)(2,1)}, u32[]{:S(2)}) copy-start(bf16[4096,256]{1,0:T(8,128)(2,1)} %param.18) | copy-start | bytes 6291460
  2.5 26.4 %all-to-all-start = ((s32[256,1,128]{2,1,0:T(1,128)}), s32[256,1,128]{2,1,0:T(1,128)S(1)}, u32[]{:S(2)}, u32[]{:S(2)}) async-start(s32[256,1,128]{2,1,0:T(1,128)} %bitcast.4), calls=%async_computation | async-start | bytes 262144 | tf_op jit(solution)/shard_map/all_to_all | solution.py:381
  16.9 3.0 %copy-start.1 = (bf16[4096,64]{0,1:T(8,128)(2,1)S(1)}, bf16[4096,64]{0,1:T(8,128)(2,1)}, u32[]{:S(2)}) copy-start(bf16[4096,64]{0,1:T(8,128)(2,1)} %param.19) | copy-start | bytes 1572868
  39.7 2.4 %collective-permute-start = (bf16[1536,256]{1,0:T(8,128)(2,1)S(1)}, bf16[1536,256]{1,0:T(8,128)(2,1)S(1)}, u32[]{:S(2)}, u32[]{:S(2)}) collective-permute-start(bf16[1536,256]{1,0:T(8,128)(2,1)S(1)} %get-tuple-element.16), channel_id=1, source_target_pairs={{0,1},{1,0},{2,3},{3,2},{4,5},{5,4},{6,7},{7,6},{8,9},{9,8},{10,11... | collective-permute-start | bytes 2359304 | tf_op jit(solution)/shard_map/ppermute | solution.py:347
  42.4 15.3 %collective-permute-start.1 = (bf16[512,256]{1,0:T(8,128)(2,1)S(1)}, bf16[512,256]{1,0:T(8,128)(2,1)S(1)}, u32[]{:S(2)}, u32[]{:S(2)}) collective-permute-start(bf16[512,256]{1,0:T(8,128)(2,1)S(1)} %get-tuple-element.24), channel_id=1, source_target_pairs={{0,2},{2,4},{4,6},{6,0},{1,3},{3,5},{5,7},{7,1},{8,10},{10,12},{12... | collective-permute-start | bytes 786440 | tf_op jit(solution)/shard_map/ppermute | solution.py:347
  42.9 14.9 %collective-permute-start.2 = (bf16[512,256]{1,0:T(8,128)(2,1)S(1)}, bf16[512,256]{1,0:T(8,128)(2,1)S(1)}, u32[]{:S(2)}, u32[]{:S(2)}) collective-permute-start(bf16[512,256]{1,0:T(8,128)(2,1)S(1)} %get-tuple-element.26), channel_id=1, source_target_pairs={{0,6},{2,0},{4,2},{6,4},{1,7},{3,1},{5,3},{7,5},{8,14},{10,8},{12,... | collective-permute-start | bytes 786440 | tf_op jit(solution)/shard_map/ppermute | solution.py:347
  45.7 12.0 %collective-permute-start.3 = (bf16[512,256]{1,0:T(8,128)(2,1)S(1)}, bf16[512,256]{1,0:T(8,128)(2,1)S(1)}, u32[]{:S(2)}, u32[]{:S(2)}) collective-permute-start(bf16[512,256]{1,0:T(8,128)(2,1)S(1)} %get-tuple-element.25), channel_id=1, source_target_pairs={{0,4},{2,6},{4,0},{6,2},{1,5},{3,7},{5,1},{7,3},{8,12},{10,14},{12... | collective-permute-start | bytes 786440 | tf_op jit(solution)/shard_map/ppermute | solution.py:347
  52.7 10.9 %copy-start.6 = (bf16[1024]{0:T(1024)(128)(2,1)S(1)}, bf16[1024]{0:T(1024)(128)(2,1)}, u32[]{:S(2)}) copy-start(bf16[1024]{0:T(1024)(128)(2,1)} %param.27) | copy-start | bytes 6148
  52.7 10.9 %copy-start.2 = (bf16[512,256]{1,0:T(8,128)(2,1)S(1)}, bf16[512,256]{1,0:T(8,128)(2,1)}, u32[]{:S(2)}) copy-start(bf16[512,256]{1,0:T(8,128)(2,1)} %param.16) | copy-start | bytes 786436
  52.7 10.9 %copy-start.4 = (bf16[13,512]{1,0:T(8,128)(2,1)S(1)}, bf16[13,512]{1,0:T(8,128)(2,1)}, u32[]{:S(2)}) copy-start(bf16[13,512]{1,0:T(8,128)(2,1)} %param.15) | copy-start | bytes 39940
  52.7 10.9 %copy-start.5 = (bf16[16,13]{1,0:T(8,128)(2,1)S(1)}, bf16[16,13]{1,0:T(8,128)(2,1)}, u32[]{:S(2)}) copy-start(bf16[16,13]{1,0:T(8,128)(2,1)} %param.14) | copy-start | bytes 1252
  52.7 11.1 %copy-start.3 = (bf16[256,128]{1,0:T(8,128)(2,1)S(1)}, bf16[256,128]{1,0:T(8,128)(2,1)}, u32[]{:S(2)}) copy-start(bf16[256,128]{1,0:T(8,128)(2,1)} %param.17) | copy-start | bytes 196612
  52.7 5.0 %collective-permute-start.4 = (bf16[512,256]{1,0:T(8,128)(2,1)S(1)}, bf16[512,256]{1,0:T(8,128)(2,1)S(1)}, u32[]{:S(2)}, u32[]{:S(2)}) collective-permute-start(bf16[512,256]{1,0:T(8,128)(2,1)S(1)} %get-tuple-element.21), channel_id=1, source_target_pairs={{0,1},{1,0},{2,3},{3,2},{4,5},{5,4},{6,7},{7,6},{8,9},{9,8},{10,11... | collective-permute-start | bytes 786440 | tf_op jit(solution)/shard_map/ppermute | solution.py:347
  58.6 16.8 %all-to-all-start.1 = ((bf16[32,16,256]{2,1,0:T(8,128)(2,1)}), bf16[32,16,256]{2,1,0:T(8,128)(2,1)S(1)}, u32[]{:S(2)}, u32[]{:S(2)}) async-start(bf16[32,16,256]{2,1,0:T(8,128)(2,1)} %bitcast.10), calls=%async_computation.1 | async-start | bytes 524288 | tf_op jit(solution)/shard_map/all_to_all | solution.py:401

commit v7 on v6

--- a/solution.py
+++ b/solution.py
@@ -17,7 +17,7 @@
 PITCH = 72
 INTER = 2208
 TOP = 1024
-SLABS = [pl.ds(0, 768), pl.ds(768, 768), pl.ds(1536, 672)]
+SLABS = [pl.ds(at, min(256, INTER - at)) for at in range(0, INTER, 256)]
 LIMIT = pltpu.CompilerParams(vmem_limit_bytes=24 * 1024 * 1024)
 VMEM = pl.BlockSpec(memory_space=pltpu.VMEM)
 SMEM = pl.BlockSpec(memory_space=pltpu.SMEM)
@@ -326,7 +326,7 @@
             pltpu.VMEM((BAGS * PITCH, LANES), jnp.float32),
             pltpu.VMEM((BAGS, INTER), jnp.float32),
             pltpu.VMEM((INTER, TOP), jnp.bfloat16),
-            pltpu.SemaphoreType.DMA((3,)),
+            pltpu.SemaphoreType.DMA((len(SLABS),)),
         ],
         compiler_params=pltpu.CompilerParams(vmem_limit_bytes=16 * 1024 * 1024),
         name="top",

time: 80.8 us -> 80.3 us (level); the launches traced: 79.4 us -> 80 us
  transfers between devices with their start and end apart: 7 -> 7, of which waited for: 4 -> 4; matrix products, arithmetic and copies ran while one was open for 8% -> 7% of each run, Pallas kernels for 8% -> 8%
where the time goes in v7:
time: 80.3 us; the launch traced here: 80 us
  waiting for transfers between devices  25.1 us (31%)
  starting transfers between devices  24.3 us (30%)
  Pallas kernels  20.8 us (26%)
  matrix products  5.88 us (7%)
  other arithmetic  2.17 us (3%)
  local copies, waits for them, and re-layouts  0.86 us (1%)
    all_to_all x1, starting transfers between devices, body(): words = lax.all_to_all(words, HOME, 0, 0, tiled=True)  14.4 us
    all_to_all x1, waiting for transfers between devices, body(): lax.all_to_all(total.astype(jnp.bfloat16).reshape(32, BAGS, 256), TABLES,...  11.6 us
    pallas_call x1, Pallas kernels, pool_first(): pl.pallas_call(first_kernel, out_shape=(half, half, jax.ShapeDtypeStruct(...  10.7 us
    ppermute x5, waiting for transfers between devices, turned(): lax.ppermute(block, axis, [(i, (i + shift) % count) for i in range(count)])  7.06 us
    all_to_all x1, waiting for transfers between devices, body(): words = lax.all_to_all(words, HOME, 0, 0, tiled=True)  6.46 us
    pallas_call x1, Pallas kernels, pool_last(): pl.pallas_call(last_kernel, out_shape=(half, half), in_specs=[SMEM, SMEM,...  6.27 us
    all_to_all x1, starting transfers between devices, body(): lax.all_to_all(total.astype(jnp.bfloat16).reshape(32, BAGS, 256), TABLES,...  5.31 us
    ppermute x5, starting transfers between devices, turned(): lax.ppermute(block, axis, [(i, (i + shift) % count) for i in range(count)])  4.64 us
  transfers between devices with their start and end apart: 7, of which 4 were waited for; matrix products, arithmetic and copies ran while one was open for 7% of the time, Pallas kernels for 8%

profile of v7, /device:TPU:32, one launch (start us, length us, event | category | flops | bytes accessed | tf_op | source)
XLA Modules:
  0.0 80.0 jit_solution(12023657663022002362)
XLA Ops:
  0.6 0.0 copy-start
  0.6 1.0 %or_bitcast_fusion = s32[32,8,16]{0,1,2:T(8,128)S(1)} fusion(s32[16,32,8]{1,2,0:T(8,128)} %param.22, s32[16,32,8]{1,2,0:T(8,128)} %param.20, s32[16,32]{1,0:T(8,128)} %param.23, s32[16,32]{1,0:T(8,128)} %param.21), kind=kLoop, calls=%fused_computation.13 | loop fusion | flops 24576 | bytes 53248 | tf_op jit(solution)/shard_map/transpose | solution.py:379
  1.7 0.1 copy.23
  1.8 0.7 broadcast_in_dim.16
  2.5 14.4 %all-to-all-start = ((s32[256,1,128]{2,1,0:T(1,128)}), s32[256,1,128]{2,1,0:T(1,128)S(1)}, u32[]{:S(2)}, u32[]{:S(2)}) async-start(s32[256,1,128]{2,1,0:T(1,128)} %bitcast.4), calls=%async_computation | async-start | bytes 262144 | tf_op jit(solution)/shard_map/all_to_all | solution.py:381
  16.9 0.1 pad_add_fusion.place_ref
  16.9 0.0 copy-done
  16.9 0.0 copy-start.1
  16.9 3.0 %convolution_bitcast_fusion.wide_ref = f32[4096,128]{1,0:T(8,128)} fusion(bf16[4096,256]{1,0:T(8,128)(2,1)S(1)} %copy-done, bf16[32,256,128]{2,1,0:T(8,128)(2,1)} %param.24, s32[]{:T(128)S(6)} %select_n.15), kind=kOutput, calls=%fused_computation | convolution fusion | flops 268435456 | bytes 4259844 | tf_op jit(solution)/shard_map/dot_general | solution.py:385
  19.9 0.0 copy-done.1
  19.9 2.6 %convolution_bitcast_fusion.1.narrow_ref = f32[4096,128]{1,0:T(8,128)} fusion(bf16[4096,64]{0,1:T(8,128)(2,1)S(1)} %copy-done.1, bf16[32,64,128]{2,1,0:T(8,128)(2,1)} %param.25, s32[]{:T(128)S(6)} %select_n.15), kind=kOutput, calls=%fused_computation.1 | convolution fusion | flops 67108864 | bytes 2637828 | tf_op jit(solution)/shard_map/dot_general | solution.py:386
  22.4 6.5 %all-to-all-done = s32[256,1,128]{2,1,0:T(1,128)S(1)} async-done(((s32[256,1,128]{2,1,0:T(1,128)}), s32[256,1,128]{2,1,0:T(1,128)S(1)}, u32[]{:S(2)}, u32[]{:S(2)}) %all-to-all-start) | async-done | bytes 131104 | tf_op jit(solution)/shard_map/all_to_all | solution.py:381
  28.9 10.7 %pool_first.1 = (bf16[1536,256]{1,0:T(8,128)(2,1)S(1)}, bf16[1536,256]{1,0:T(8,128)(2,1)S(1)}, s32[32,128]{1,0:T(8,128)S(1)}, s32[512,128]{1,0:T(8,128)S(1)}, s32[1]{0:T(128)}) custom-call(s32[2]{0:T(128)S(1)} %pad_add_fusion.place_ref, s32[256,128]{1,0:T(8,128)S(1)} %bitcast.26, f32[4096,128]{1,0:T(8,128)} %convolution_bitcast_fusion.wide_ref, ...), custom_call_target="tpu_custom_call" | custom-call | flops 1000000 | bytes 10000000 | tf_op jit(solution)/shard_map/pool_first/pallas_call | solution.py:238
  39.6 0.6 collective-permute-start
  40.2 1.9 %collective-permute-done = bf16[1536,256]{1,0:T(8,128)(2,1)S(1)} collective-permute-done((bf16[1536,256]{1,0:T(8,128)(2,1)S(1)}, bf16[1536,256]{1,0:T(8,128)(2,1)S(1)}, u32[]{:S(2)}, u32[]{:S(2)}) %collective-permute-start) | collective-permute-done | bytes 786464 | tf_op jit(solution)/shard_map/ppermute | solution.py:347
  42.1 0.2 add_convert_fusion
  42.3 0.1 fusion.13
  42.4 0.5 collective-permute-start.1
  42.9 2.8 %collective-permute-start.2 = (bf16[512,256]{1,0:T(8,128)(2,1)S(1)}, bf16[512,256]{1,0:T(8,128)(2,1)S(1)}, u32[]{:S(2)}, u32[]{:S(2)}) collective-permute-start(bf16[512,256]{1,0:T(8,128)(2,1)S(1)} %get-tuple-element.26), channel_id=1, source_target_pairs={{0,6},{2,0},{4,2},{6,4},{1,7},{3,1},{5,3},{7,5},{8,14},{10,8},{12,... | collective-permute-start | bytes 786440 | tf_op jit(solution)/shard_map/ppermute | solution.py:347
  45.7 0.6 collective-permute-start.3
  46.3 6.3 %pool_last.1 = (bf16[512,256]{1,0:T(8,128)(2,1)S(1)}, bf16[512,256]{1,0:T(8,128)(2,1)S(1)}) custom-call(s32[1]{0:T(128)} %get-tuple-element.13.blocks_ref, s32[32,128]{1,0:T(8,128)S(1)} %get-tuple-element.14.firsts_ref, s32[512,128]{1,0:T(8,128)S(1)} %get-tuple-element.18.lists_ref, f32[4096,128]{1,0:T(8,128)} %convolution_bitcast_fusion.wide_ref, ...), custom_call_target="tpu_custom_call" | custom-call | flops 1000000 | bytes 10000000 | tf_op jit(solution)/shard_map/pool_last/pallas_call | solution.py:264
  52.6 0.0 copy-start.6
  52.6 0.0 copy-start.2
  52.6 0.0 copy-start.4
  52.6 0.0 copy-start.5
  52.6 0.0 copy-start.3
  52.6 0.1 collective-permute-start.4
  52.7 5.1 %collective-permute-done.1 = bf16[512,256]{1,0:T(8,128)(2,1)S(1)} collective-permute-done((bf16[512,256]{1,0:T(8,128)(2,1)S(1)}, bf16[512,256]{1,0:T(8,128)(2,1)S(1)}, u32[]{:S(2)}, u32[]{:S(2)}) %collective-permute-start.1) | collective-permute-done | bytes 262176 | tf_op jit(solution)/shard_map/ppermute | solution.py:347
  57.9 0.0 collective-permute-done.2
  57.9 0.0 collective-permute-done.3
  57.9 0.0 collective-permute-done.4
  57.9 0.9 %add_convert_fusion.1 = bf16[512,256]{1,0:T(8,128)(2,1)} fusion(bf16[512,256]{1,0:T(8,128)(2,1)S(1)} %collective-permute-done.4, bf16[512,256]{1,0:T(8,128)(2,1)S(1)} %collective-permute-done.3, bf16[512,256]{1,0:T(8,128)(2,1)S(1)} %collective-permute-done.2, bf16[512,256]{1,0:T(8,128)(2,1)S(1)} %collective-permute-done.1, ...), kind=kLoop, calls=%fused_computation.10 | loop fusion | flops 1310720 | bytes 1572864 | tf_op jit(solution)/shard_map/convert_element_type | solution.py:402
  58.7 5.3 %all-to-all-start.1 = ((bf16[32,16,256]{2,1,0:T(8,128)(2,1)}), bf16[32,16,256]{2,1,0:T(8,128)(2,1)S(1)}, u32[]{:S(2)}, u32[]{:S(2)}) async-start(bf16[32,16,256]{2,1,0:T(8,128)(2,1)} %bitcast.10), calls=%async_computation.1 | async-start | bytes 524288 | tf_op jit(solution)/shard_map/all_to_all | solution.py:401
  64.1 0.0 copy-done.6
  64.1 0.0 copy-done.2
  64.1 0.0 copy-done.4
  64.1 0.0 copy-done.5
  64.1 0.2 fusion.3
  64.3 0.0 copy-done.3
  64.3 0.1 fusion.4.bottom_ref
  64.5 11.6 %all-to-all-done.1.home_ref = bf16[32,16,256]{2,1,0:T(8,128)(2,1)S(1)} async-done(((bf16[32,16,256]{2,1,0:T(8,128)(2,1)}), bf16[32,16,256]{2,1,0:T(8,128)(2,1)S(1)}, u32[]{:S(2)}, u32[]{:S(2)}) %all-to-all-start.1) | async-done | bytes 262176 | tf_op jit(solution)/shard_map/all_to_all | solution.py:401
  76.1 3.9 %top.1 = (bf16[16,1024]{1,0:T(8,128)(2,1)}, f32[1,16]{1,0:T(1,128)}) custom-call(bf16[16,128]{1,0:T(8,128)(2,1)S(1)} %fusion.4.bottom_ref, bf16[32,16,256]{2,1,0:T(8,128)(2,1)S(1)} %all-to-all-done.1.home_ref, bf16[2208,1024]{1,0:T(8,128)(2,1)} %first_ref.1, bf16[1,1024]{1,0:T(2,128)(2,1)S(1)} %reshape.22.last_ref), custom_call_target="tpu_custom_call" | custom-call | tf_op jit(solution)/shard_map/top/pallas_call | solution.py:316
  (2 shorter events, 0.0 us)
Async XLA Ops:
  0.6 16.3 %copy-start = (bf16[4096,256]{1,0:T(8,128)(2,1)S(1)}, bf16[4096,256]{1,0:T(8,128)(2,1)}, u32[]{:S(2)}) copy-start(bf16[4096,256]{1,0:T(8,128)(2,1)} %param.18) | copy-start | bytes 6291460
  2.5 26.4 %all-to-all-start = ((s32[256,1,128]{2,1,0:T(1,128)}), s32[256,1,128]{2,1,0:T(1,128)S(1)}, u32[]{:S(2)}, u32[]{:S(2)}) async-start(s32[256,1,128]{2,1,0:T(1,128)} %bitcast.4), calls=%async_computation | async-start | bytes 262144 | tf_op jit(solution)/shard_map/all_to_all | solution.py:381
  16.9 3.0 %copy-start.1 = (bf16[4096,64]{0,1:T(8,128)(2,1)S(1)}, bf16[4096,64]{0,1:T(8,128)(2,1)}, u32[]{:S(2)}) copy-start(bf16[4096,64]{0,1:T(8,128)(2,1)} %param.19) | copy-start | bytes 1572868
  39.6 2.5 %collective-permute-start = (bf16[1536,256]{1,0:T(8,128)(2,1)S(1)}, bf16[1536,256]{1,0:T(8,128)(2,1)S(1)}, u32[]{:S(2)}, u32[]{:S(2)}) collective-permute-start(bf16[1536,256]{1,0:T(8,128)(2,1)S(1)} %get-tuple-element.16), channel_id=1, source_target_pairs={{0,1},{1,0},{2,3},{3,2},{4,5},{5,4},{6,7},{7,6},{8,9},{9,8},{10,11... | collective-permute-start | bytes 2359304 | tf_op jit(solution)/shard_map/ppermute | solution.py:347
  42.4 15.5 %collective-permute-start.1 = (bf16[512,256]{1,0:T(8,128)(2,1)S(1)}, bf16[512,256]{1,0:T(8,128)(2,1)S(1)}, u32[]{:S(2)}, u32[]{:S(2)}) collective-permute-start(bf16[512,256]{1,0:T(8,128)(2,1)S(1)} %get-tuple-element.24), channel_id=1, source_target_pairs={{0,2},{2,4},{4,6},{6,0},{1,3},{3,5},{5,7},{7,1},{8,10},{10,12},{12... | collective-permute-start | bytes 786440 | tf_op jit(solution)/shard_map/ppermute | solution.py:347
  42.9 15.0 %collective-permute-start.2 = (bf16[512,256]{1,0:T(8,128)(2,1)S(1)}, bf16[512,256]{1,0:T(8,128)(2,1)S(1)}, u32[]{:S(2)}, u32[]{:S(2)}) collective-permute-start(bf16[512,256]{1,0:T(8,128)(2,1)S(1)} %get-tuple-element.26), channel_id=1, source_target_pairs={{0,6},{2,0},{4,2},{6,4},{1,7},{3,1},{5,3},{7,5},{8,14},{10,8},{12,... | collective-permute-start | bytes 786440 | tf_op jit(solution)/shard_map/ppermute | solution.py:347
  45.7 12.2 %collective-permute-start.3 = (bf16[512,256]{1,0:T(8,128)(2,1)S(1)}, bf16[512,256]{1,0:T(8,128)(2,1)S(1)}, u32[]{:S(2)}, u32[]{:S(2)}) collective-permute-start(bf16[512,256]{1,0:T(8,128)(2,1)S(1)} %get-tuple-element.25), channel_id=1, source_target_pairs={{0,4},{2,6},{4,0},{6,2},{1,5},{3,7},{5,1},{7,3},{8,12},{10,14},{12... | collective-permute-start | bytes 786440 | tf_op jit(solution)/shard_map/ppermute | solution.py:347
  52.6 11.5 %copy-start.6 = (bf16[1024]{0:T(1024)(128)(2,1)S(1)}, bf16[1024]{0:T(1024)(128)(2,1)}, u32[]{:S(2)}) copy-start(bf16[1024]{0:T(1024)(128)(2,1)} %param.27) | copy-start | bytes 6148
  52.6 11.5 %copy-start.2 = (bf16[512,256]{1,0:T(8,128)(2,1)S(1)}, bf16[512,256]{1,0:T(8,128)(2,1)}, u32[]{:S(2)}) copy-start(bf16[512,256]{1,0:T(8,128)(2,1)} %param.16) | copy-start | bytes 786436
  52.6 11.5 %copy-start.4 = (bf16[13,512]{1,0:T(8,128)(2,1)S(1)}, bf16[13,512]{1,0:T(8,128)(2,1)}, u32[]{:S(2)}) copy-start(bf16[13,512]{1,0:T(8,128)(2,1)} %param.15) | copy-start | bytes 39940
  52.6 11.5 %copy-start.5 = (bf16[16,13]{1,0:T(8,128)(2,1)S(1)}, bf16[16,13]{1,0:T(8,128)(2,1)}, u32[]{:S(2)}) copy-start(bf16[16,13]{1,0:T(8,128)(2,1)} %param.14) | copy-start | bytes 1252
  52.6 11.7 %copy-start.3 = (bf16[256,128]{1,0:T(8,128)(2,1)S(1)}, bf16[256,128]{1,0:T(8,128)(2,1)}, u32[]{:S(2)}) copy-start(bf16[256,128]{1,0:T(8,128)(2,1)} %param.17) | copy-start | bytes 196612
  52.6 5.2 %collective-permute-start.4 = (bf16[512,256]{1,0:T(8,128)(2,1)S(1)}, bf16[512,256]{1,0:T(8,128)(2,1)S(1)}, u32[]{:S(2)}, u32[]{:S(2)}) collective-permute-start(bf16[512,256]{1,0:T(8,128)(2,1)S(1)} %get-tuple-element.21), channel_id=1, source_target_pairs={{0,1},{1,0},{2,3},{3,2},{4,5},{5,4},{6,7},{7,6},{8,9},{9,8},{10,11... | collective-permute-start | bytes 786440 | tf_op jit(solution)/shard_map/ppermute | solution.py:347
  58.7 17.3 %all-to-all-start.1 = ((bf16[32,16,256]{2,1,0:T(8,128)(2,1)}), bf16[32,16,256]{2,1,0:T(8,128)(2,1)S(1)}, u32[]{:S(2)}, u32[]{:S(2)}) async-start(bf16[32,16,256]{2,1,0:T(8,128)(2,1)} %bitcast.10), calls=%async_computation.1 | async-start | bytes 524288 | tf_op jit(solution)/shard_map/all_to_all | solution.py:401
